TPU v7x, 32 devices: a whole 2x2x4 slice. The times are simulated.
32 devices in a mesh: seq: 8 (over z, x), head: 4 (over y, core).
Axes of the slice: x: 2, y: 2, z: 4, core: 2. Of those that a mesh axis runs over, the one named last changes fastest.
Arguments:
- inputs: bfloat16 [8192, 2048], P('seq', 'head'), may hold values from -6 to 6
- w_qkv: bfloat16 [3, 2048, 2048], P(None, None, 'head'), may hold values from -0.125 to 0.125
- level_weight: float32 [16, 4], P('head'), may hold values from 0.5 to 2
- grad_out: bfloat16 [8192, 2048], P('seq', 'head'), may hold values from -6 to 6
Outputs:
- attn_out: bfloat16 [8192, 2048], P('seq', 'head')
- grad_query: bfloat16 [8192, 2048], P('seq', 'head')
- grad_key: bfloat16 [8192, 2048], P('seq', 'head')
- grad_value: bfloat16 [8192, 2048], P('seq', 'head')
All inputs are finite; a program needn't handle non-finite values.
Results may differ from a plain program's by a relative error of at most 0.012.
Values may be sent and summed in bfloat16 or wider, within the bound.
No kernel may reach another device: no remote copies, remote signals or barrier semaphores. Data moves between devices by JAX's collectives and lax.ppermute only.
A program may use at most 128 MiB of HBM per device.

v0:
```python
import functools
import math

import jax
import jax.numpy as jnp
from jax import lax
from jax.experimental import pallas as pl
from jax.experimental.pallas import tpu as pltpu
from jax.sharding import PartitionSpec as P

SHARES = (10, 12, 13, 14, 15)
CHUNKS = len(SHARES)
GROUP = 4
FIRST = (3, 2, 1)
MIB = 2**20
VMEM = pl.BlockSpec(memory_space=pltpu.VMEM)
SMEM = pl.BlockSpec(memory_space=pltpu.SMEM)
ANY = pl.BlockSpec(memory_space=pl.ANY)
HBM = pl.BlockSpec(memory_space=pltpu.HBM)
NN = (((1,), (0,)), ((), ()))
NT = (((1,), (1,)), ((), ()))
TN = (((0,), (0,)), ((), ()))
BF16 = jnp.bfloat16
F32 = jnp.float32


def dot(a, b, dims=NN):
    return lax.dot_general(a, b, dims, preferred_element_type=F32)


def swap(value, axis, mask):
    pairs = [(source, source ^ mask) for source in range(lax.axis_size(axis))]
    return lax.ppermute(value, axis, pairs)


def bit_of(position, bit):
    return lax.rem(position // 2**bit, 2) == 1


def call(kernel, outs, operands, specs, flops, scratch=(), out_specs=None, limit=4, moved=0, aliases=()):
    return pl.pallas_call(
        kernel,
        out_shape=outs,
        in_specs=specs,
        out_specs=[VMEM] * len(outs) if out_specs is None else out_specs,
        scratch_shapes=scratch,
        input_output_aliases=dict(aliases),
        compiler_params=pltpu.CompilerParams(vmem_limit_bytes=limit * MIB),
        cost_estimate=pl.CostEstimate(flops=flops, bytes_accessed=moved, transcendentals=0),
    )(*operands)


def load_kernel(spans, x_ref, *refs):
    outs, sems = refs[-len(spans) - 1 : -1], refs[-1]
    copies = []
    for i, (first, last) in enumerate(spans):
        rows = x_ref.at[pl.ds(first, last - first)]
        copies.append(pltpu.make_async_copy(rows, outs[i], sems.at[i]))
    for copy in copies:
        copy.start()
    for copy in copies:
        copy.wait()


def load(source, spans, after=()):
    return call(
        functools.partial(load_kernel, spans),
        [pltpu.VMEM((last - first, *source.shape[1:]), BF16) for first, last in spans],
        [pltpu.with_memory_space_constraint(source, pltpu.HBM), *after],
        [HBM] + [ANY] * len(after),
        0,
        [pltpu.SemaphoreType.DMA((len(spans),))],
        limit=2,
        moved=4 * source.size,
    )


def load_weights_kernel(parts, g_ref, w_ref, after_ref, g_out, w_out, sems):
    me = lax.axis_index("head")
    depth = w_ref.shape[1] // parts
    width = w_ref.shape[2]
    copies = [pltpu.make_async_copy(g_ref, g_out, sems.at[3 * parts])]
    for k in range(parts):
        rows = pl.ds(pl.multiple_of((me ^ k) * depth, depth), depth)
        for j in range(3):
            copies.append(
                pltpu.make_async_copy(
                    w_ref.at[j, rows],
                    w_out.at[pl.ds(k * depth, depth), pl.ds(j * width, width)],
                    sems.at[3 * k + j],
                )
            )
    for copy in copies:
        copy.start()
    for copy in copies:
        copy.wait()


def tie_kernel(value_ref, *refs):
    del value_ref, refs


def tie(value, *after, flops=0):
    return pl.pallas_call(
        tie_kernel,
        out_shape=pltpu.VMEM(value.shape, value.dtype),
        in_specs=[VMEM] + [ANY] * len(after),
        out_specs=VMEM,
        input_output_aliases={0: 0},
        compiler_params=pltpu.CompilerParams(vmem_limit_bytes=MIB),
        cost_estimate=pl.CostEstimate(flops=flops, bytes_accessed=0, transcendentals=0),
    )(value, *after)


def beside(refs, span):
    count = span[1] - span[0]
    found = [ref[...] if ref.shape[0] == count else ref[span[0] : span[1], :] for ref in refs]
    return found[0] if len(found) == 1 else jnp.concatenate(found, axis=1)


def write_states(span, heads, q_ref, k_ref, v_ref, g_ref, state_ref):
    size = q_ref.shape[1] // heads
    for h in range(heads):
        cols = slice(h * size, (h + 1) * size)
        state_ref[0, h] = dot(k_ref[:, cols], v_ref[:, cols], TN)
        state_ref[1, h] = dot(q_ref[:, cols], g_ref[span[0] : span[1], cols], TN)


def early_kernel(span, count, w_ref, *refs):
    segments, states = refs[:count], refs[count:-2]
    total_ref, sum_ref = refs[-2:]
    rows = beside(segments, span)
    total_ref[...] = dot(rows, w_ref[: rows.shape[1], :])
    sums = states[0][...]
    for state in states[1:]:
        sums = sums + state[...]
    sum_ref[...] = sums


def project_kernel(span, count, heads, w_ref, g_ref, *refs):
    outs, state_ref = refs[-4:-1], refs[-1]
    width = outs[0].shape[1]
    total = dot(beside(refs[:count], span), w_ref[...])
    for j, out_ref in enumerate(outs):
        out_ref[...] = total[:, j * width : (j + 1) * width].astype(BF16)
    write_states(span, heads, *outs, g_ref, state_ref)


def last_kernel(span, heads, w_ref, g_ref, part_ref, sum_ref, late_ref, *refs):
    outs, state_ref, total_ref, sends = refs[:3], refs[3], refs[4], refs[5:]
    width = outs[0].shape[1]
    start = w_ref.shape[0] - late_ref.shape[1]
    total = part_ref[...] + dot(late_ref[...], w_ref[start:, :])
    for j, out_ref in enumerate(outs):
        out_ref[...] = total[:, j * width : (j + 1) * width].astype(BF16)
    write_states(span, heads, *outs, g_ref, state_ref)
    share = heads // GROUP
    place = lax.rem(lax.axis_index("seq"), GROUP)
    total_ref[...] = sum_ref[...] + state_ref[...]
    for m, send in enumerate(sends, 1):
        for s in range(2):
            for e in range(share):
                send[s, e] = total_ref[s, (place ^ m) * share + e].astype(BF16)


def local_kernel(span, heads, weight_ref, q_ref, k_ref, v_ref, g_ref, after_ref, out_ref):
    rows = q_ref.shape[0]
    size = q_ref.shape[1] // heads
    norm = 1.0 / math.sqrt(size * g_ref.shape[0])
    at = lax.broadcasted_iota(jnp.int32, (rows, rows), 0)
    of = lax.broadcasted_iota(jnp.int32, (rows, rows), 1)
    columns = [slice(h * size, (h + 1) * size) for h in range(heads)]
    masked = []
    for h, cols in enumerate(columns):
        q, k, v = q_ref[:, cols], k_ref[:, cols], v_ref[:, cols]
        g = g_ref[span[0] : span[1], cols]
        scale = weight_ref[h, 0] * norm
        found = []
        for left, right, causal in (
            (q, k, at >= of),
            (g, v, at >= of),
            (v, g, of >= at),
            (k, q, of >= at),
        ):
            found.append(jnp.where(causal, dot(left, right, NT) * scale, 0.0).astype(BF16))
        masked.append(found)
    for h, cols in enumerate(columns):
        q, k, v = q_ref[:, cols], k_ref[:, cols], v_ref[:, cols]
        g = g_ref[span[0] : span[1], cols]
        for j, value in enumerate((v, k, q, g)):
            out_ref[j, :, cols] = dot(masked[h][j], value)


def owner_kernel(final, total_ref, *refs):
    got, refs = dict(zip(FIRST, refs)), refs[GROUP - 1 :]
    near_ref, far_ref, *nexts = refs[-3 if final else -4 :]
    position = lax.axis_index("seq")
    place = lax.rem(position, GROUP)
    heads = total_ref.shape[1]
    share = heads // GROUP
    odd, high = bit_of(position, 0), bit_of(position, 1)
    for e in range(share):
        mine, other = [], []
        for s in range(2):
            mine.append(total_ref[s, place * share + e] + got[1][s, e].astype(F32))
            other.append(got[2][s, e].astype(F32) + got[3][s, e].astype(F32))
        sums = [mine[s] + other[s] for s in range(2)]
        write_next(sums, e, 2, final, *nexts)
        near_ref[e] = jnp.where(high, other[0], other[1]).astype(BF16)
        far_ref[e] = jnp.where(high, mine[1], mine[0]).astype(BF16)
    for h in range(heads):
        near_ref[share + h] = jnp.where(odd, total_ref[1, h], total_ref[0, h]).astype(BF16)


def write_next(sums, e, bit, final, next_ref, sum_ref=None):
    if final:
        value = jnp.where(bit_of(lax.axis_index("seq"), bit), sums[1], sums[0])
        next_ref[e] = value.astype(BF16)
        return
    for s in range(2):
        sum_ref[s, e] = sums[s]
        next_ref[s, e] = sums[s].astype(BF16)


def climb_kernel(bit, next_final, got_ref, old_ref, level_ref, *nexts):
    on = bit_of(lax.axis_index("seq"), bit)
    for e in range(got_ref.shape[1]):
        both = [got_ref[s, e].astype(F32) for s in range(2)]
        level_ref[e] = jnp.where(on, both[0], both[1]).astype(BF16)
        sums = [old_ref[s, e] + both[s] for s in range(2)]
        write_next(sums, e, bit + 1, next_final, *nexts)


def pair_block(first, second):
    zero = jnp.zeros(first.shape, BF16)
    top = jnp.concatenate([first.astype(BF16), zero], axis=1)
    bottom = jnp.concatenate([zero, second.astype(BF16)], axis=1)
    return jnp.concatenate([top, bottom], axis=0)


def gather_mixes(levels, first, side, weight_ref, block, mix_ref):
    position = lax.axis_index("seq")
    place = lax.rem(position, GROUP)
    heads, size = mix_ref.shape[:2]
    share = heads // GROUP
    for m in range(GROUP):
        for e in range(share):
            h = (place ^ m) * share + e
            total = None
            for b in range(len(levels) // GROUP):
                level = first + b
                coef = weight_ref[h, level + 1] * (1.0 / math.sqrt(size * block * 2**level))
                taken = bit_of(position, level)
                if side == 1:
                    taken = jnp.logical_not(taken)
                term = jnp.where(taken, coef, 0.0) * levels[b * GROUP + m][e].astype(F32)
                total = term if total is None else total + term
            mix_ref[h] = total


def write_side(spans, side, ascending, weight_of, rows_of, part_refs, outs, held, sems):
    chunks = len(spans)
    size = held.shape[-1]
    copies = []
    for c in range(chunks) if ascending else reversed(range(chunks)):
        span = slice(*spans[c])
        weights = weight_of(c)
        for j in range(2):
            ref = rows_of[2 * side + j][c]
            rows = span if ref.shape[0] != spans[c][1] - spans[c][0] else slice(None)
            for p, weight in enumerate(weights):
                cols = slice(p * weight.shape[0], (p + 1) * weight.shape[0])
                term = dot(ref[rows, cols], weight, NT if 2 * side + j in (1, 2) else NN)
                held[j, span, cols] = (term + part_refs[c][2 * side + j, :, cols]).astype(BF16)
            copy = pltpu.make_async_copy(
                held.at[j, span], outs[2 * side + j].at[span], sems.at[j, c]
            )
            copy.start()
            copies.append(copy)
    for copy in copies:
        copy.wait()


def early_side_kernel(spans, heads, top, weight_ref, g_ref, *refs):
    chunks = len(spans)
    levels, refs = refs[: (top - 1) * GROUP], refs[(top - 1) * GROUP :]
    q_refs, refs = refs[:chunks], refs[chunks:]
    k_refs, refs = refs[:chunks], refs[chunks:]
    v_refs, refs = refs[:chunks], refs[chunks:]
    state_refs, refs = refs[:chunks], refs[chunks:]
    part_refs, refs = refs[:chunks], refs[chunks:]
    outs, (base_ref, held, mix_ref, sems) = refs[:4], refs[4:]
    position = lax.axis_index("seq")
    block = g_ref.shape[0]
    size = mix_ref.shape[-1]
    norm = 1.0 / math.sqrt(size * block)

    def sums_of(side):
        gather_mixes(levels, 1, side, weight_ref, block, mix_ref)
        taken = bit_of(position, 0)
        if side == 1:
            taken = jnp.logical_not(taken)
        found = []
        for h in range(heads):
            coef = jnp.where(taken, weight_ref[h, 1] * norm, 0.0)
            found.append(mix_ref[h] + coef * levels[1][heads // GROUP + h].astype(F32))
        return found

    def add(sums, side, c):
        return [
            total + weight_ref[h, 0] * norm * state_refs[c][side, h] for h, total in enumerate(sums)
        ]

    for side in range(2):
        reached = bit_of(position, top)

        @pl.when(reached if side == 1 else jnp.logical_not(reached))
        def _():
            sums = [sums_of(side)]

            def weight_of(c):
                weights = [pair_block(*sums[0][h : h + 2]) for h in range(0, heads, 2)]
                sums[0] = add(sums[0], side, c)
                return weights

            rows_of = (q_refs, [g_ref] * chunks, v_refs, k_refs)
            write_side(spans, side, side == 0, weight_of, rows_of, part_refs, outs, held, sems)
            other = sums_of(1 - side)
            for c in range(chunks) if side == 1 else reversed(range(chunks)):
                for h in range(heads):
                    base_ref[c, h] = other[h]
                other = add(other, 1 - side, c)


def late_side_kernel(spans, heads, top, weight_ref, g_ref, base_ref, *refs):
    chunks = len(spans)
    levels, refs = refs[:GROUP], refs[GROUP:]
    q_refs, refs = refs[:chunks], refs[chunks:]
    k_refs, refs = refs[:chunks], refs[chunks:]
    v_refs, refs = refs[:chunks], refs[chunks:]
    part_refs, refs = refs[:chunks], refs[chunks:]
    outs, (held, mix_ref, sems) = refs[-7:-3], refs[-3:]
    block = g_ref.shape[0]
    reached = bit_of(lax.axis_index("seq"), top)
    for side in range(2):

        @pl.when(reached if side == 0 else jnp.logical_not(reached))
        def _():
            gather_mixes(levels, top, side, weight_ref, block, mix_ref)

            def weight_of(c):
                sums = [base_ref[c, h] + mix_ref[h] for h in range(heads)]
                return [pair_block(*sums[h : h + 2]) for h in range(0, heads, 2)]

            rows_of = (q_refs, [g_ref] * chunks, v_refs, k_refs)
            write_side(spans, side, False, weight_of, rows_of, part_refs, outs, held, sems)


def exchange(totals, sends, local, late):
    depth = lax.axis_size("seq").bit_length() - 1
    heads, square = totals.shape[1], totals.shape[2:]
    share = heads // GROUP
    last = depth - 1

    def nexts(bit):
        if bit == last:
            return [pltpu.VMEM((share, *square), BF16)]
        return [pltpu.VMEM((2, share, *square), BF16), pltpu.VMEM((2, share, *square), F32)]

    def spread(mine, other):
        return [mine, *[swap(mine if m == 1 else other, "seq", m) for m in range(1, GROUP)]]

    one = pltpu.VMEM((share, *square), BF16)
    got = [swap(sends[m - 1], "seq", m) for m in FIRST]
    fillers = [local(c, sends[0]) for c in late]
    mine, other, sent, *sums = call(
        functools.partial(owner_kernel, last == 2),
        [pltpu.VMEM((share + heads, *square), BF16), one, *nexts(2)],
        [totals, *got, *fillers],
        [VMEM] * GROUP + [ANY] * len(fillers),
        10**6,
    )
    levels = spread(mine, other)
    for bit in range(2, last):
        found, sent, *sums = call(
            functools.partial(climb_kernel, bit, bit + 1 == last),
            [one, *nexts(bit + 1)],
            [swap(sent, "seq", 1 << bit), *sums],
            [VMEM] * 2,
            10**6,
        )
        levels += spread(found, found)
    found = tie(swap(sent, "seq", 1 << last), mine, flops=12 * 10**8)
    levels += spread(found, found)
    return levels, fillers


def per_device(inputs, w_qkv, level_weight, grad_out):
    rows, width = grad_out.shape
    heads = level_weight.shape[0]
    size = width // heads
    parts = lax.axis_size("head")
    edges = [rows * sum(SHARES[:c]) // sum(SHARES) for c in range(CHUNKS + 1)]
    spans = list(zip(edges[:-1], edges[1:]))
    depth = inputs.shape[1]
    mine = load(inputs, spans[:1])
    mine = [*mine, *load(inputs, spans[1:], mine)]
    grads, weights = call(
        functools.partial(load_weights_kernel, parts),
        [pltpu.VMEM((rows, width), BF16), pltpu.VMEM((parts * depth, 3 * width), BF16)],
        [
            pltpu.with_memory_space_constraint(grad_out, pltpu.HBM),
            pltpu.with_memory_space_constraint(w_qkv, pltpu.HBM),
            mine[1],
        ],
        [HBM, HBM, ANY],
        0,
        [pltpu.SemaphoreType.DMA((3 * parts + 1,))],
        limit=2,
        moved=4 * (grad_out.size + w_qkv.size),
    )
    top, *lows = [1 << b for b in reversed(range(parts.bit_length() - 1))]
    arrived = [swap(piece, "head", top) for piece in mine]
    arrived[0] = tie(arrived[0], weights)
    whole = {0: inputs}
    for low in lows:
        for k in sorted(whole):
            whole[k | low] = swap(whole[k], "head", low)
    state = pltpu.VMEM((2, heads, size, size), F32)
    qs, ks, vs, states, locals_ = [], [], [], [], []

    def local(c, after):
        chunk = spans[c][1] - spans[c][0]
        return call(
            functools.partial(local_kernel, spans[c], heads),
            [pltpu.VMEM((4, chunk, width), F32)],
            [level_weight, qs[c], ks[c], vs[c], grads, after],
            [SMEM] + [VMEM] * 4 + [ANY],
            100 * chunk * chunk * width if c >= CHUNKS - 2 else 0,
        )[0]

    after = None
    for c in range(CHUNKS):
        pieces = {**whole, 0: mine[c]}
        pieces[top] = arrived[c] if after is None else tie(arrived[c], after)
        for low in lows:
            for k in [k for k in sorted(pieces) if k & top]:
                pieces[k | low] = swap(pieces[k], "head", low)
        segments = [pieces[k] for k in sorted(pieces)]
        span = spans[c]
        chunk = span[1] - span[0]
        flat = pltpu.VMEM((chunk, width), BF16)
        if c < CHUNKS - 1:
            if c > 0:
                locals_.append(local(c - 1, pieces[top]))
            operands = [weights, grads, *segments, *locals_[-1:]]
            got = call(
                functools.partial(project_kernel, span, len(segments), heads),
                [flat, flat, flat, state],
                operands,
                [VMEM] * (2 + len(segments)) + [ANY] * len(locals_[-1:]),
                0,
            )
        else:
            operands = [weights, *segments[:-1], *states]
            begun, before = call(
                functools.partial(early_kernel, span, len(segments) - 1),
                [pltpu.VMEM((chunk, 3 * width), F32), state],
                operands,
                [VMEM] * len(operands),
                0,
            )
            got = call(
                functools.partial(last_kernel, span, heads),
                [
                    flat,
                    flat,
                    flat,
                    state,
                    state,
                    *[pltpu.VMEM((2, heads // GROUP, size, size), BF16)] * (GROUP - 1),
                ],
                [weights, grads, begun, before, segments[-1]],
                [VMEM] * 5,
                0,
            )
        qs.append(got[0])
        ks.append(got[1])
        vs.append(got[2])
        states.append(got[3])
        after = got[3]
    levels, fillers = exchange(got[4], got[5:], local, range(len(locals_), CHUNKS))
    locals_ += fillers
    shapes = [jax.ShapeDtypeStruct((rows, width), BF16)] * 4
    top = len(levels) // GROUP
    flats = [*qs, *ks, *vs]
    scratch = [
        pltpu.VMEM((2, rows, width), BF16),
        pltpu.VMEM((heads, size, size), F32),
        pltpu.SemaphoreType.DMA((2, CHUNKS)),
    ]
    operands = [level_weight, grads, *levels[:-GROUP], *flats, *states, *locals_]
    *written, base = call(
        functools.partial(early_side_kernel, spans, heads, top),
        [*shapes, pltpu.VMEM((CHUNKS, heads, size, size), F32)],
        operands,
        [SMEM] + [VMEM] * (len(operands) - 1),
        0,
        scratch,
        [ANY] * 4 + [VMEM],
        8,
    )
    operands = [level_weight, grads, base, *levels[-GROUP:], *flats, *locals_]
    return call(
        functools.partial(late_side_kernel, spans, heads, top),
        shapes,
        [*operands, *written],
        [SMEM] + [VMEM] * (len(operands) - 1) + [ANY] * 4,
        0,
        scratch,
        [ANY] * 4,
        8,
        aliases={len(operands) + j: j for j in range(4)},
    )


def solution(mesh):
    in_specs = (P("seq", "head"), P(None, None, "head"), P("head", None), P("seq", "head"))
    out_specs = (P("seq", "head"), P("seq", "head"), P("seq", "head"), P("seq", "head"))
    return jax.shard_map(
        per_device, mesh=mesh, in_specs=in_specs, out_specs=out_specs, check_vma=False
    )
```

profile of v0, /device:TPU:0, one launch (start us, length us, event | category | flops | bytes accessed | tf_op | source)
XLA Modules:
  0.0 54.1 jit_solution(9850676677060331317)
XLA Ops:
  0.6 0.5 collective-permute-start
  1.1 0.9 %shard_map.75.refs_0_ = bf16[160,512]{1,0:T(8,128)(2,1)S(1)} custom-call(bf16[1024,512]{1,0:T(8,128)(2,1)} %x_ref.3), custom_call_target="tpu_custom_call" | custom-call | bytes 2097152 | tf_op jit(solution)/shard_map/pallas_call | solution.py:41
  2.1 2.6 %collective-permute-start.5 = (bf16[160,512]{1,0:T(8,128)(2,1)S(1)}, bf16[160,512]{1,0:T(8,128)(2,1)S(1)}, u32[]{:S(2)}, u32[]{:S(2)}) collective-permute-start(bf16[160,512]{1,0:T(8,128)(2,1)S(1)} %shard_map.75.refs_0_), channel_id=1, source_target_pairs={{0,2},{1,3},{2,0},{3,1},{4,6},{5,7},{6,4},{7,5},{8,10},{9,11},{10,... | collective-permute-start | bytes 491528 | tf_op jit(solution)/shard_map/ppermute | solution.py:33
  4.7 1.3 %shard_map.76 = (bf16[192,512]{1,0:T(8,128)(2,1)S(1)}, bf16[208,512]{1,0:T(8,128)(2,1)S(1)}, bf16[224,512]{1,0:T(8,128)(2,1)S(1)}, bf16[240,512]{1,0:T(8,128)(2,1)S(1)}) custom-call(bf16[1024,512]{1,0:T(8,128)(2,1)} %x_ref.3, bf16[160,512]{1,0:T(8,128)(2,1)S(1)} %shard_map.75.refs_0_), custom_call_target="tpu_custom_call" | custom-call | bytes 2097152 | tf_op jit(solution)/shard_map/pallas_call | solution.py:41
  6.0 0.1 collective-permute-start.4
  6.1 3.2 %shard_map.77 = (bf16[1024,512]{1,0:T(8,128)(2,1)S(1)}, bf16[2048,1536]{1,0:T(8,128)(2,1)S(1)}) custom-call(bf16[1024,512]{1,0:T(8,128)(2,1)} %g_ref.1, bf16[3,2048,512]{2,1,0:T(8,128)(2,1)} %w_ref.1, bf16[192,512]{1,0:T(8,128)(2,1)S(1)} %get-tuple-element.44.after_ref.refs_0_), custom_call_target="tpu_custom_call" | custom-call | bytes 14680064 | tf_op jit(solution)/shard_map/pallas_call | solution.py:41
  9.3 0.5 collective-permute-done.5.value_ref
  9.7 0.0 collective-permute-start.6
  9.7 1.9 %collective-permute-start.3 = (bf16[208,512]{1,0:T(8,128)(2,1)S(1)}, bf16[208,512]{1,0:T(8,128)(2,1)S(1)}, u32[]{:S(2)}, u32[]{:S(2)}) collective-permute-start(bf16[208,512]{1,0:T(8,128)(2,1)S(1)} %get-tuple-element.49.refs_0_), channel_id=1, source_target_pairs={{0,2},{1,3},{2,0},{3,1},{4,6},{5,7},{6,4},{7,5},{8,10},{9,11},{10,... | collective-permute-start | bytes 638984 | tf_op jit(solution)/shard_map/ppermute | solution.py:33
  11.7 0.0 collective-permute-done.refs_1_
  11.7 1.5 %shard_map.79 = (bf16[160,512]{1,0:T(8,128)(2,1)S(1)}, bf16[160,512]{1,0:T(8,128)(2,1)S(1)}, bf16[160,512]{1,0:T(8,128)(2,1)S(1)}, f32[2,4,128,128]{3,2,1,0:T(8,128)S(1)}) custom-call(bf16[2048,1536]{1,0:T(8,128)(2,1)S(1)} %get-tuple-element.46.refs_0_.w_ref, bf16[1024,512]{1,0:T(8,128)(2,1)S(1)} %get-tuple-element.45.g_ref, ...), custom_call_target="tpu_custom_call" | custom-call | tf_op jit(solution)/shard_map/pallas_call | solution.py:41
  13.2 0.7 %collective-permute-done.4.value_ref = bf16[192,512]{1,0:T(8,128)(2,1)S(1)} collective-permute-done((bf16[192,512]{1,0:T(8,128)(2,1)S(1)}, bf16[192,512]{1,0:T(8,128)(2,1)S(1)}, u32[]{:S(2)}, u32[]{:S(2)}) %collective-permute-start.4) | collective-permute-done | bytes 196640 | tf_op jit(solution)/shard_map/ppermute | solution.py:33
  13.9 0.0 collective-permute-start.7
  13.9 1.9 %collective-permute-start.2 = (bf16[224,512]{1,0:T(8,128)(2,1)S(1)}, bf16[224,512]{1,0:T(8,128)(2,1)S(1)}, u32[]{:S(2)}, u32[]{:S(2)}) collective-permute-start(bf16[224,512]{1,0:T(8,128)(2,1)S(1)} %get-tuple-element.48.refs_0_), channel_id=1, source_target_pairs={{0,2},{1,3},{2,0},{3,1},{4,6},{5,7},{6,4},{7,5},{8,10},{9,11},{10,... | collective-permute-start | bytes 688136 | tf_op jit(solution)/shard_map/ppermute | solution.py:33
  15.9 1.4 %shard_map.81.refs_4_.refs_24_.refs_19_ = f32[4,160,512]{2,1,0:T(8,128)S(1)} custom-call(f32[4,4]{1,0:T(4,128)S(1)} %copy-done, bf16[160,512]{1,0:T(8,128)(2,1)S(1)} %get-tuple-element.51.q_ref.refs_4_, bf16[160,512]{1,0:T(8,128)(2,1)S(1)} %get-tuple-element.52.k_ref.refs_9_, bf16[160,512]{1,0:T(8,128)(2,1)S(1)} %get-tuple-element.53.v_ref.refs_14_, ...), custom_call_target="tpu_custom_call" | custom-call | tf_op jit(solution)/shard_map/pallas_call | solution.py:41
  17.3 1.7 %shard_map.82 = (bf16[192,512]{1,0:T(8,128)(2,1)S(1)}, bf16[192,512]{1,0:T(8,128)(2,1)S(1)}, bf16[192,512]{1,0:T(8,128)(2,1)S(1)}, f32[2,4,128,128]{3,2,1,0:T(8,128)S(1)}) custom-call(bf16[2048,1536]{1,0:T(8,128)(2,1)S(1)} %get-tuple-element.46.refs_0_.w_ref, bf16[1024,512]{1,0:T(8,128)(2,1)S(1)} %get-tuple-element.45.g_ref, ...), custom_call_target="tpu_custom_call" | custom-call | tf_op jit(solution)/shard_map/pallas_call | solution.py:41
  19.1 0.0 collective-permute-done.3.value_ref
  19.1 0.3 collective-permute-start.8
  19.4 1.1 %collective-permute-start.1 = (bf16[240,512]{1,0:T(8,128)(2,1)S(1)}, bf16[240,512]{1,0:T(8,128)(2,1)S(1)}, u32[]{:S(2)}, u32[]{:S(2)}) collective-permute-start(bf16[240,512]{1,0:T(8,128)(2,1)S(1)} %get-tuple-element.47.refs_0_), channel_id=1, source_target_pairs={{0,2},{1,3},{2,0},{3,1},{4,6},{5,7},{6,4},{7,5},{8,10},{9,11},{10,... | collective-permute-start | bytes 737288 | tf_op jit(solution)/shard_map/ppermute | solution.py:33
  20.5 1.6 %shard_map.84.refs_4_.refs_25_.refs_20_ = f32[4,192,512]{2,1,0:T(8,128)S(1)} custom-call(f32[4,4]{1,0:T(4,128)S(1)} %copy-done, bf16[192,512]{1,0:T(8,128)(2,1)S(1)} %get-tuple-element.55.q_ref.refs_5_, bf16[192,512]{1,0:T(8,128)(2,1)S(1)} %get-tuple-element.56.k_ref.refs_10_, bf16[192,512]{1,0:T(8,128)(2,1)S(1)} %get-tuple-element.57.v_ref.refs_15_, ...), custom_call_target="tpu_custom_call" | custom-call | tf_op jit(solution)/shard_map/pallas_call | solution.py:41
  22.1 1.8 %shard_map.85 = (bf16[208,512]{1,0:T(8,128)(2,1)S(1)}, bf16[208,512]{1,0:T(8,128)(2,1)S(1)}, bf16[208,512]{1,0:T(8,128)(2,1)S(1)}, f32[2,4,128,128]{3,2,1,0:T(8,128)S(1)}) custom-call(bf16[2048,1536]{1,0:T(8,128)(2,1)S(1)} %get-tuple-element.46.refs_0_.w_ref, bf16[1024,512]{1,0:T(8,128)(2,1)S(1)} %get-tuple-element.45.g_ref, ...), custom_call_target="tpu_custom_call" | custom-call | tf_op jit(solution)/shard_map/pallas_call | solution.py:41
  23.9 0.3 collective-permute-start.9
  24.2 1.6 %shard_map.87.refs_4_.refs_26_.refs_21_ = f32[4,208,512]{2,1,0:T(8,128)S(1)} custom-call(f32[4,4]{1,0:T(4,128)S(1)} %copy-done, bf16[208,512]{1,0:T(8,128)(2,1)S(1)} %get-tuple-element.59.q_ref.refs_6_, bf16[208,512]{1,0:T(8,128)(2,1)S(1)} %get-tuple-element.60.k_ref.refs_11_, bf16[208,512]{1,0:T(8,128)(2,1)S(1)} %get-tuple-element.61.v_ref.refs_16_, ...), custom_call_target="tpu_custom_call" | custom-call | tf_op jit(solution)/shard_map/pallas_call | solution.py:41
  25.8 1.9 %shard_map.88 = (bf16[224,512]{1,0:T(8,128)(2,1)S(1)}, bf16[224,512]{1,0:T(8,128)(2,1)S(1)}, bf16[224,512]{1,0:T(8,128)(2,1)S(1)}, f32[2,4,128,128]{3,2,1,0:T(8,128)S(1)}) custom-call(bf16[2048,1536]{1,0:T(8,128)(2,1)S(1)} %get-tuple-element.46.refs_0_.w_ref, bf16[1024,512]{1,0:T(8,128)(2,1)S(1)} %get-tuple-element.45.g_ref, ...), custom_call_target="tpu_custom_call" | custom-call | tf_op jit(solution)/shard_map/pallas_call | solution.py:41
  27.8 0.7 %collective-permute-done.1.value_ref = bf16[240,512]{1,0:T(8,128)(2,1)S(1)} collective-permute-done((bf16[240,512]{1,0:T(8,128)(2,1)S(1)}, bf16[240,512]{1,0:T(8,128)(2,1)S(1)}, u32[]{:S(2)}, u32[]{:S(2)}) %collective-permute-start.1) | collective-permute-done | bytes 245792 | tf_op jit(solution)/shard_map/ppermute | solution.py:33
  28.5 1.4 %shard_map.90 = (f32[240,1536]{1,0:T(8,128)S(1)}, f32[2,4,128,128]{3,2,1,0:T(8,128)S(1)}) custom-call(bf16[2048,1536]{1,0:T(8,128)(2,1)S(1)} %get-tuple-element.46.refs_0_.w_ref, bf16[240,512]{1,0:T(8,128)(2,1)S(1)} %get-tuple-element.47.refs_0_, bf16[1024,512]{1,0:T(8,128)(2,1)S(1)} %collective-permute-done.refs_1_, ...), custom_call_target="tpu_custom_call" | custom-call | tf_op jit(solution)/shard_map/pallas_call | solution.py:41
  30.0 0.1 collective-permute-done.10.late_ref
  30.0 0.9 %shard_map.91 = (bf16[240,512]{1,0:T(8,128)(2,1)S(1)}, bf16[240,512]{1,0:T(8,128)(2,1)S(1)}, bf16[240,512]{1,0:T(8,128)(2,1)S(1)}, f32[2,4,128,128]{3,2,1,0:T(8,...) custom-call(bf16[2048,1536]{1,0:T(8,128)(2,1)S(1)} %get-tuple-elemen, ...), custom_call_target="tpu_custom_call" | custom-call | tf_op jit(solution)/shard_map/pallas_call | solution.py:41
  30.9 2.8 %collective-permute-start.11 = (bf16[2,1,128,128]{3,2,1,0:T(8,128)(2,1)S(1)}, bf16[2,1,128,128]{3,2,1,0:T(8,128)(2,1)S(1)}, u32[]{:S(2)}, u32[]{:S(2)}) collective-permute-start(bf16[2,1,128,128]{3,2,1,0:T(8,128)(2,1)S(1)} %get-tuple-element.66), channel_id=1, source_target_pairs={{0,12},{4,8},{8,4},{12,0},{16,28},{20,24},{24,20},{28,16},{1,13},{... | collective-permute-start | bytes 196616 | tf_op jit(solution)/shard_map/ppermute | solution.py:33
  33.7 0.4 collective-permute-start.12
  34.2 0.3 collective-permute-start.13
  34.5 1.8 %shard_map.93.refs_4_.refs_28_.refs_23_ = f32[4,240,512]{2,1,0:T(8,128)S(1)} custom-call(f32[4,4]{1,0:T(4,128)S(1)} %copy-done, bf16[240,512]{1,0:T(8,128)(2,1)S(1)} %get-tuple-element.72.q_ref.refs_8_, bf16[240,512]{1,0:T(8,128)(2,1)S(1)} %get-tuple-element.73.k_ref.refs_13_, bf16[240,512]{1,0:T(8,128)(2,1)S(1)} %get-tuple-element.74.v_ref.refs_18_, ...), custom_call_target="tpu_custom_call" | custom-call | flops 2949120000 | tf_op jit(solution)/shard_map/pallas_call | solution.py:41
  36.3 1.9 %shard_map.92.refs_3_.refs_27_.refs_22_ = f32[4,224,512]{2,1,0:T(8,128)S(1)} custom-call(f32[4,4]{1,0:T(4,128)S(1)} %copy-done, bf16[224,512]{1,0:T(8,128)(2,1)S(1)} %get-tuple-element.69.q_ref.refs_7_, bf16[224,512]{1,0:T(8,128)(2,1)S(1)} %get-tuple-element.70.k_ref.refs_12_, bf16[224,512]{1,0:T(8,128)(2,1)S(1)} %get-tuple-element.71.v_ref.refs_17_, ...), custom_call_target="tpu_custom_call" | custom-call | flops 2569011200 | tf_op jit(solution)/shard_map/pallas_call | solution.py:41
  38.2 0.2 collective-permute-done.13.refs_2_
  38.4 0.1 shard_map.94
  38.5 2.7 %collective-permute-start.17 = (bf16[1,128,128]{2,1,0:T(8,128)(2,1)S(1)}, bf16[1,128,128]{2,1,0:T(8,128)(2,1)S(1)}, u32[]{:S(2)}, u32[]{:S(2)}) collective-permute-start(bf16[1,128,128]{2,1,0:T(8,128)(2,1)S(1)} %get-tuple-element.79), channel_id=1, source_target_pairs={{0,16},{4,20},{8,24},{12,28},{16,0},{20,4},{24,8},{28,12},{1,17},{... | collective-permute-start | bytes 98312 | tf_op jit(solution)/shard_map/ppermute | solution.py:33
  41.2 1.5 %collective-permute-start.14 = (bf16[5,128,128]{2,1,0:T(8,128)(2,1)S(1)}, bf16[5,128,128]{2,1,0:T(8,128)(2,1)S(1)}, u32[]{:S(2)}, u32[]{:S(2)}) collective-permute-start(bf16[5,128,128]{2,1,0:T(8,128)(2,1)S(1)} %get-tuple-element.75.refs_0_), channel_id=1, source_target_pairs={{0,4},{4,0},{8,12},{12,8},{16,20},{20,16},{24,28},{28,24},{1,5},{5... | collective-permute-start | bytes 491528 | tf_op jit(solution)/shard_map/ppermute | solution.py:33
  42.7 1.6 %collective-permute-start.16 = (bf16[1,128,128]{2,1,0:T(8,128)(2,1)S(1)}, bf16[1,128,128]{2,1,0:T(8,128)(2,1)S(1)}, u32[]{:S(2)}, u32[]{:S(2)}) collective-permute-start(bf16[1,128,128]{2,1,0:T(8,128)(2,1)S(1)} %get-tuple-element.76), channel_id=1, source_target_pairs={{0,12},{4,8},{8,4},{12,0},{16,28},{20,24},{24,20},{28,16},{1,13},{... | collective-permute-start | bytes 98312 | tf_op jit(solution)/shard_map/ppermute | solution.py:33
  44.2 0.4 collective-permute-start.15
  44.7 2.5 %collective-permute-start.20 = (bf16[1,128,128]{2,1,0:T(8,128)(2,1)S(1)}, bf16[1,128,128]{2,1,0:T(8,128)(2,1)S(1)}, u32[]{:S(2)}, u32[]{:S(2)}) collective-permute-start(bf16[1,128,128]{2,1,0:T(8,128)(2,1)S(1)} %shard_map.96.refs_0_), channel_id=1, source_target_pairs={{0,12},{4,8},{8,4},{12,0},{16,28},{20,24},{24,20},{28,16},{1,13},{... | collective-permute-start | bytes 98312 | tf_op jit(solution)/shard_map/ppermute | solution.py:33
  47.2 0.4 collective-permute-start.19
  47.6 0.1 collective-permute-done.16.refs_3_
  47.7 0.5 collective-permute-start.18
  48.1 0.1 collective-permute-done.15.refs_2_
  48.3 2.5 %shard_map.95 = (bf16[1024,512]{1,0:T(8,128)(2,1)}, bf16[1024,512]{1,0:T(8,128)(2,1)}, bf16[1024,512]{1,0:T(8,128)(2,1)}, bf16[1024,512]{1,0:T(8,128)(2,1)}, f32[5,4,128,128]{3,2,1,0:T(8,128)S(1)}) custom-call(f32[4,4]{1,0:T(4,128)S(1)} %copy-done, bf16[1024,512]{1,0:T(8,128)(2,1)S(1)} %get-tuple-element.45.g_ref, ...), custom_call_target="tpu_custom_call" | custom-call | tf_op jit(solution)/shard_map/pallas_call | solution.py:41
  50.8 0.3 collective-permute-done.19.refs_2_
  51.1 0.5 collective-permute-done.18.refs_1_
  51.6 2.3 %shard_map.97 = (bf16[1024,512]{1,0:T(8,128)(2,1)}, bf16[1024,512]{1,0:T(8,128)(2,1)}, bf16[1024,512]{1,0:T(8,128)(2,1)}, bf16[1024,512]{1,0:T(8,128)(2,1)}) custom-call(f32[4,4]{1,0:T(4,128)S(1)} %copy-done, bf16[1024,512]{1,0:T(8,128)(2,1)S(1)} %get-tuple-element.45.g_ref, ...), custom_call_target="tpu_custom_call", output_to_operand_aliasing={{0}: (27, {}), {1}: (28, {}), {2}: (29, {}), {3}: (30, {})} | custom-call | tf_op jit(solution)/shard_map/pallas_call | solution.py:41
  (19 shorter events, 0.0 us)
Async XLA Ops:
  0.6 11.1 %collective-permute-start = (bf16[1024,512]{1,0:T(8,128)(2,1)}, bf16[1024,512]{1,0:T(8,128)(2,1)S(1)}, u32[]{:S(2)}, u32[]{:S(2)}) collective-permute-start(bf16[1024,512]{1,0:T(8,128)(2,1)} %x_ref.3), channel_id=1, source_target_pairs={{0,1},{1,0},{2,3},{3,2},{4,5},{5,4},{6,7},{7,6},{8,9},{9,8},{10,11... | collective-permute-start | bytes 3145736 | tf_op jit(solution)/shard_map/ppermute | solution.py:33
  2.1 7.6 %collective-permute-start.5 = (bf16[160,512]{1,0:T(8,128)(2,1)S(1)}, bf16[160,512]{1,0:T(8,128)(2,1)S(1)}, u32[]{:S(2)}, u32[]{:S(2)}) collective-permute-start(bf16[160,512]{1,0:T(8,128)(2,1)S(1)} %shard_map.75.refs_0_), channel_id=1, source_target_pairs={{0,2},{1,3},{2,0},{3,1},{4,6},{5,7},{6,4},{7,5},{8,10},{9,11},{10,... | collective-permute-start | bytes 491528 | tf_op jit(solution)/shard_map/ppermute | solution.py:33
  6.0 8.0 %collective-permute-start.4 = (bf16[192,512]{1,0:T(8,128)(2,1)S(1)}, bf16[192,512]{1,0:T(8,128)(2,1)S(1)}, u32[]{:S(2)}, u32[]{:S(2)}) collective-permute-start(bf16[192,512]{1,0:T(8,128)(2,1)S(1)} %get-tuple-element.44.after_ref.refs_0_), channel_id=1, source_target_pairs={{0,2},{1,3},{2,0},{3,1},{4,6},{5,7},{6,4},{7,5},{8,10},{9,11},{10,... | collective-permute-start | bytes 589832 | tf_op jit(solution)/shard_map/ppermute | solution.py:33
  9.7 2.0 %collective-permute-start.6 = (bf16[160,512]{1,0:T(8,128)(2,1)S(1)}, bf16[160,512]{1,0:T(8,128)(2,1)S(1)}, u32[]{:S(2)}, u32[]{:S(2)}) collective-permute-start(bf16[160,512]{1,0:T(8,128)(2,1)S(1)} %shard_map.78.refs_2_), channel_id=1, source_target_pairs={{0,1},{1,0},{2,3},{3,2},{4,5},{5,4},{6,7},{7,6},{8,9},{9,8},{10,11... | collective-permute-start | bytes 491528 | tf_op jit(solution)/shard_map/ppermute | solution.py:33
  9.7 9.3 %collective-permute-start.3 = (bf16[208,512]{1,0:T(8,128)(2,1)S(1)}, bf16[208,512]{1,0:T(8,128)(2,1)S(1)}, u32[]{:S(2)}, u32[]{:S(2)}) collective-permute-start(bf16[208,512]{1,0:T(8,128)(2,1)S(1)} %get-tuple-element.49.refs_0_), channel_id=1, source_target_pairs={{0,2},{1,3},{2,0},{3,1},{4,6},{5,7},{6,4},{7,5},{8,10},{9,11},{10,... | collective-permute-start | bytes 638984 | tf_op jit(solution)/shard_map/ppermute | solution.py:33
  11.7 4.2 %copy-start = (f32[4,4]{1,0:T(4,128)S(1)}, f32[4,4]{1,0:T(4,128)}, u32[]{:S(2)}) copy-start(f32[4,4]{1,0:T(4,128)} %weight_ref.13) | copy-start | bytes 196
  13.9 3.4 %collective-permute-start.7 = (bf16[192,512]{1,0:T(8,128)(2,1)S(1)}, bf16[192,512]{1,0:T(8,128)(2,1)S(1)}, u32[]{:S(2)}, u32[]{:S(2)}) collective-permute-start(bf16[192,512]{1,0:T(8,128)(2,1)S(1)} %shard_map.80.after_ref.refs_2_), channel_id=1, source_target_pairs={{0,1},{1,0},{2,3},{3,2},{4,5},{5,4},{6,7},{7,6},{8,9},{9,8},{10,11... | collective-permute-start | bytes 589832 | tf_op jit(solution)/shard_map/ppermute | solution.py:33
  13.9 9.9 %collective-permute-start.2 = (bf16[224,512]{1,0:T(8,128)(2,1)S(1)}, bf16[224,512]{1,0:T(8,128)(2,1)S(1)}, u32[]{:S(2)}, u32[]{:S(2)}) collective-permute-start(bf16[224,512]{1,0:T(8,128)(2,1)S(1)} %get-tuple-element.48.refs_0_), channel_id=1, source_target_pairs={{0,2},{1,3},{2,0},{3,1},{4,6},{5,7},{6,4},{7,5},{8,10},{9,11},{10,... | collective-permute-start | bytes 688136 | tf_op jit(solution)/shard_map/ppermute | solution.py:33
  19.1 2.9 %collective-permute-start.8 = (bf16[208,512]{1,0:T(8,128)(2,1)S(1)}, bf16[208,512]{1,0:T(8,128)(2,1)S(1)}, u32[]{:S(2)}, u32[]{:S(2)}) collective-permute-start(bf16[208,512]{1,0:T(8,128)(2,1)S(1)} %shard_map.83.after_ref.refs_2_), channel_id=1, source_target_pairs={{0,1},{1,0},{2,3},{3,2},{4,5},{5,4},{6,7},{7,6},{8,9},{9,8},{10,11... | collective-permute-start | bytes 638984 | tf_op jit(solution)/shard_map/ppermute | solution.py:33
  19.4 9.1 %collective-permute-start.1 = (bf16[240,512]{1,0:T(8,128)(2,1)S(1)}, bf16[240,512]{1,0:T(8,128)(2,1)S(1)}, u32[]{:S(2)}, u32[]{:S(2)}) collective-permute-start(bf16[240,512]{1,0:T(8,128)(2,1)S(1)} %get-tuple-element.47.refs_0_), channel_id=1, source_target_pairs={{0,2},{1,3},{2,0},{3,1},{4,6},{5,7},{6,4},{7,5},{8,10},{9,11},{10,... | collective-permute-start | bytes 737288 | tf_op jit(solution)/shard_map/ppermute | solution.py:33
  23.9 1.9 %collective-permute-start.9 = (bf16[224,512]{1,0:T(8,128)(2,1)S(1)}, bf16[224,512]{1,0:T(8,128)(2,1)S(1)}, u32[]{:S(2)}, u32[]{:S(2)}) collective-permute-start(bf16[224,512]{1,0:T(8,128)(2,1)S(1)} %shard_map.86.after_ref.refs_2_), channel_id=1, source_target_pairs={{0,1},{1,0},{2,3},{3,2},{4,5},{5,4},{6,7},{7,6},{8,9},{9,8},{10,11... | collective-permute-start | bytes 688136 | tf_op jit(solution)/shard_map/ppermute | solution.py:33
  28.5 1.5 %collective-permute-start.10 = (bf16[240,512]{1,0:T(8,128)(2,1)S(1)}, bf16[240,512]{1,0:T(8,128)(2,1)S(1)}, u32[]{:S(2)}, u32[]{:S(2)}) collective-permute-start(bf16[240,512]{1,0:T(8,128)(2,1)S(1)} %shard_map.89.refs_2_), channel_id=1, source_target_pairs={{0,1},{1,0},{2,3},{3,2},{4,5},{5,4},{6,7},{7,6},{8,9},{9,8},{10,11... | collective-permute-start | bytes 737288 | tf_op jit(solution)/shard_map/ppermute | solution.py:33
  30.9 7.3 %collective-permute-start.11 = (bf16[2,1,128,128]{3,2,1,0:T(8,128)(2,1)S(1)}, bf16[2,1,128,128]{3,2,1,0:T(8,128)(2,1)S(1)}, u32[]{:S(2)}, u32[]{:S(2)}) collective-permute-start(bf16[2,1,128,128]{3,2,1,0:T(8,128)(2,1)S(1)} %get-tuple-element.66), channel_id=1, source_target_pairs={{0,12},{4,8},{8,4},{12,0},{16,28},{20,24},{24,20},{28,16},{1,13},{... | collective-permute-start | bytes 196616 | tf_op jit(solution)/shard_map/ppermute | solution.py:33
  33.7 4.5 %collective-permute-start.12 = (bf16[2,1,128,128]{3,2,1,0:T(8,128)(2,1)S(1)}, bf16[2,1,128,128]{3,2,1,0:T(8,128)(2,1)S(1)}, u32[]{:S(2)}, u32[]{:S(2)}) collective-permute-start(bf16[2,1,128,128]{3,2,1,0:T(8,128)(2,1)S(1)} %get-tuple-element.67), channel_id=1, source_target_pairs={{0,8},{4,12},{8,0},{12,4},{16,24},{20,28},{24,16},{28,20},{1,9},{5... | collective-permute-start | bytes 196616 | tf_op jit(solution)/shard_map/ppermute | solution.py:33
  34.2 4.3 %collective-permute-start.13 = (bf16[2,1,128,128]{3,2,1,0:T(8,128)(2,1)S(1)}, bf16[2,1,128,128]{3,2,1,0:T(8,128)(2,1)S(1)}, u32[]{:S(2)}, u32[]{:S(2)}) collective-permute-start(bf16[2,1,128,128]{3,2,1,0:T(8,128)(2,1)S(1)} %get-tuple-element.68.after_ref), channel_id=1, source_target_pairs={{0,4},{4,0},{8,12},{12,8},{16,20},{20,16},{24,28},{28,24},{1,5},{5... | collective-permute-start | bytes 196616 | tf_op jit(solution)/shard_map/ppermute | solution.py:33
  38.5 6.2 %collective-permute-start.17 = (bf16[1,128,128]{2,1,0:T(8,128)(2,1)S(1)}, bf16[1,128,128]{2,1,0:T(8,128)(2,1)S(1)}, u32[]{:S(2)}, u32[]{:S(2)}) collective-permute-start(bf16[1,128,128]{2,1,0:T(8,128)(2,1)S(1)} %get-tuple-element.79), channel_id=1, source_target_pairs={{0,16},{4,20},{8,24},{12,28},{16,0},{20,4},{24,8},{28,12},{1,17},{... | collective-permute-start | bytes 98312 | tf_op jit(solution)/shard_map/ppermute | solution.py:33
  41.2 7.1 %collective-permute-start.14 = (bf16[5,128,128]{2,1,0:T(8,128)(2,1)S(1)}, bf16[5,128,128]{2,1,0:T(8,128)(2,1)S(1)}, u32[]{:S(2)}, u32[]{:S(2)}) collective-permute-start(bf16[5,128,128]{2,1,0:T(8,128)(2,1)S(1)} %get-tuple-element.75.refs_0_), channel_id=1, source_target_pairs={{0,4},{4,0},{8,12},{12,8},{16,20},{20,16},{24,28},{28,24},{1,5},{5... | collective-permute-start | bytes 491528 | tf_op jit(solution)/shard_map/ppermute | solution.py:33
  42.7 5.0 %collective-permute-start.16 = (bf16[1,128,128]{2,1,0:T(8,128)(2,1)S(1)}, bf16[1,128,128]{2,1,0:T(8,128)(2,1)S(1)}, u32[]{:S(2)}, u32[]{:S(2)}) collective-permute-start(bf16[1,128,128]{2,1,0:T(8,128)(2,1)S(1)} %get-tuple-element.76), channel_id=1, source_target_pairs={{0,12},{4,8},{8,4},{12,0},{16,28},{20,24},{24,20},{28,16},{1,13},{... | collective-permute-start | bytes 98312 | tf_op jit(solution)/shard_map/ppermute | solution.py:33
  44.2 4.1 %collective-permute-start.15 = (bf16[1,128,128]{2,1,0:T(8,128)(2,1)S(1)}, bf16[1,128,128]{2,1,0:T(8,128)(2,1)S(1)}, u32[]{:S(2)}, u32[]{:S(2)}) collective-permute-start(bf16[1,128,128]{2,1,0:T(8,128)(2,1)S(1)} %get-tuple-element.76), channel_id=1, source_target_pairs={{0,8},{4,12},{8,0},{12,4},{16,24},{20,28},{24,16},{28,20},{1,9},{5... | collective-permute-start | bytes 98312 | tf_op jit(solution)/shard_map/ppermute | solution.py:33
  44.7 6.2 %collective-permute-start.20 = (bf16[1,128,128]{2,1,0:T(8,128)(2,1)S(1)}, bf16[1,128,128]{2,1,0:T(8,128)(2,1)S(1)}, u32[]{:S(2)}, u32[]{:S(2)}) collective-permute-start(bf16[1,128,128]{2,1,0:T(8,128)(2,1)S(1)} %shard_map.96.refs_0_), channel_id=1, source_target_pairs={{0,12},{4,8},{8,4},{12,0},{16,28},{20,24},{24,20},{28,16},{1,13},{... | collective-permute-start | bytes 98312 | tf_op jit(solution)/shard_map/ppermute | solution.py:33
  47.2 3.9 %collective-permute-start.19 = (bf16[1,128,128]{2,1,0:T(8,128)(2,1)S(1)}, bf16[1,128,128]{2,1,0:T(8,128)(2,1)S(1)}, u32[]{:S(2)}, u32[]{:S(2)}) collective-permute-start(bf16[1,128,128]{2,1,0:T(8,128)(2,1)S(1)} %shard_map.96.refs_0_), channel_id=1, source_target_pairs={{0,8},{4,12},{8,0},{12,4},{16,24},{20,28},{24,16},{28,20},{1,9},{5... | collective-permute-start | bytes 98312 | tf_op jit(solution)/shard_map/ppermute | solution.py:33
  47.7 3.9 %collective-permute-start.18 = (bf16[1,128,128]{2,1,0:T(8,128)(2,1)S(1)}, bf16[1,128,128]{2,1,0:T(8,128)(2,1)S(1)}, u32[]{:S(2)}, u32[]{:S(2)}) collective-permute-start(bf16[1,128,128]{2,1,0:T(8,128)(2,1)S(1)} %shard_map.96.refs_0_), channel_id=1, source_target_pairs={{0,4},{4,0},{8,12},{12,8},{16,20},{20,16},{24,28},{28,24},{1,5},{5... | collective-permute-start | bytes 98312 | tf_op jit(solution)/shard_map/ppermute | solution.py:33
where the time goes:
time: 54.2 us; the launch traced here: 54.1 us
  Pallas kernels  28 us (52%)
  starting transfers between devices  21.9 us (40%)
  waiting for transfers between devices  3.15 us (6%)
  between operations  1 us (2%)
    pallas_call x17, Pallas kernels, call(): pl.pallas_call(kernel, out_shape=outs, in_specs=specs, out_specs=[VMEM] *...  28 us
    ppermute x21, starting transfers between devices, swap(): return lax.ppermute(value, axis, pairs)  21.9 us
    ppermute x21, waiting for transfers between devices, swap(): return lax.ppermute(value, axis, pairs)  3.15 us
  transfers between devices with their start and end apart: 21, of which 9 were waited for; matrix products, arithmetic and copies ran while one was open for 0% of the time, Pallas kernels for 46%

commit v1 on v0

--- a/solution.py
+++ b/solution.py
@@ -175,20 +175,27 @@
         q, k, v = q_ref[:, cols], k_ref[:, cols], v_ref[:, cols]
         g = g_ref[span[0] : span[1], cols]
         scale = weight_ref[h, 0] * norm
-        found = []
-        for left, right, causal in (
-            (q, k, at >= of),
-            (g, v, at >= of),
-            (v, g, of >= at),
-            (k, q, of >= at),
-        ):
-            found.append(jnp.where(causal, dot(left, right, NT) * scale, 0.0).astype(BF16))
-        masked.append(found)
+        pairs = [(q, k, at >= of), (g, v, at >= of)]
+        if 2 * h >= heads:
+            pairs += [(v, g, of >= at), (k, q, of >= at)]
+        masked.append(
+            [
+                jnp.where(causal, dot(left, right, NT) * scale, 0.0).astype(BF16)
+                for left, right, causal in pairs
+            ]
+        )
     for h, cols in enumerate(columns):
         q, k, v = q_ref[:, cols], k_ref[:, cols], v_ref[:, cols]
         g = g_ref[span[0] : span[1], cols]
-        for j, value in enumerate((v, k, q, g)):
-            out_ref[j, :, cols] = dot(masked[h][j], value)
+        attend, grad = masked[h][:2]
+        out_ref[0, :, cols] = dot(attend, v)
+        out_ref[1, :, cols] = dot(grad, k)
+        if 2 * h >= heads:
+            out_ref[2, :, cols] = dot(masked[h][2], q)
+            out_ref[3, :, cols] = dot(masked[h][3], g)
+        else:
+            out_ref[2, :, cols] = dot(grad, q, TN)
+            out_ref[3, :, cols] = dot(attend, g, TN)
 
 
 def owner_kernel(final, total_ref, *refs):

time: 54.2 us -> 54 us (level)
  transfers between devices with their start and end apart: 21 -> 21, of which waited for: 9 -> 9; matrix products, arithmetic and copies ran while one was open for 0% -> 0% of each run, Pallas kernels for 46% -> 45%
where the time goes in v1:
time: 54 us; the launch traced here: 53.8 us
  Pallas kernels  27.5 us (51%)
  starting transfers between devices  22 us (41%)
  waiting for transfers between devices  3.38 us (6%)
  between operations  0.99 us (2%)
    pallas_call x17, Pallas kernels, call(): pl.pallas_call(kernel, out_shape=outs, in_specs=specs, out_specs=[VMEM] *...  27.5 us
    ppermute x21, starting transfers between devices, swap(): return lax.ppermute(value, axis, pairs)  22 us
    ppermute x21, waiting for transfers between devices, swap(): return lax.ppermute(value, axis, pairs)  3.38 us
  transfers between devices with their start and end apart: 21, of which 9 were waited for; matrix products, arithmetic and copies ran while one was open for 0% of the time, Pallas kernels for 45%

profile of v1, /device:TPU:0, one launch (start us, length us, event | category | flops | bytes accessed | tf_op | source)
XLA Modules:
  0.0 53.8 jit_solution(17436572689022318673)
XLA Ops:
  0.6 0.5 collective-permute-start
  1.1 0.9 %shard_map.75.refs_0_ = bf16[160,512]{1,0:T(8,128)(2,1)S(1)} custom-call(bf16[1024,512]{1,0:T(8,128)(2,1)} %x_ref.3), custom_call_target="tpu_custom_call" | custom-call | bytes 2097152 | tf_op jit(solution)/shard_map/pallas_call | solution.py:41
  2.1 2.6 %collective-permute-start.5 = (bf16[160,512]{1,0:T(8,128)(2,1)S(1)}, bf16[160,512]{1,0:T(8,128)(2,1)S(1)}, u32[]{:S(2)}, u32[]{:S(2)}) collective-permute-start(bf16[160,512]{1,0:T(8,128)(2,1)S(1)} %shard_map.75.refs_0_), channel_id=1, source_target_pairs={{0,2},{1,3},{2,0},{3,1},{4,6},{5,7},{6,4},{7,5},{8,10},{9,11},{10,... | collective-permute-start | bytes 491528 | tf_op jit(solution)/shard_map/ppermute | solution.py:33
  4.7 1.3 %shard_map.76 = (bf16[192,512]{1,0:T(8,128)(2,1)S(1)}, bf16[208,512]{1,0:T(8,128)(2,1)S(1)}, bf16[224,512]{1,0:T(8,128)(2,1)S(1)}, bf16[240,512]{1,0:T(8,128)(2,1)S(1)}) custom-call(bf16[1024,512]{1,0:T(8,128)(2,1)} %x_ref.3, bf16[160,512]{1,0:T(8,128)(2,1)S(1)} %shard_map.75.refs_0_), custom_call_target="tpu_custom_call" | custom-call | bytes 2097152 | tf_op jit(solution)/shard_map/pallas_call | solution.py:41
  6.0 0.1 collective-permute-start.4
  6.1 3.2 %shard_map.77 = (bf16[1024,512]{1,0:T(8,128)(2,1)S(1)}, bf16[2048,1536]{1,0:T(8,128)(2,1)S(1)}) custom-call(bf16[1024,512]{1,0:T(8,128)(2,1)} %g_ref.1, bf16[3,2048,512]{2,1,0:T(8,128)(2,1)} %w_ref.1, bf16[192,512]{1,0:T(8,128)(2,1)S(1)} %get-tuple-element.44.after_ref.refs_0_), custom_call_target="tpu_custom_call" | custom-call | bytes 14680064 | tf_op jit(solution)/shard_map/pallas_call | solution.py:41
  9.3 0.5 collective-permute-done.5.value_ref
  9.7 1.9 %collective-permute-start.3 = (bf16[208,512]{1,0:T(8,128)(2,1)S(1)}, bf16[208,512]{1,0:T(8,128)(2,1)S(1)}, u32[]{:S(2)}, u32[]{:S(2)}) collective-permute-start(bf16[208,512]{1,0:T(8,128)(2,1)S(1)} %get-tuple-element.49.refs_0_), channel_id=1, source_target_pairs={{0,2},{1,3},{2,0},{3,1},{4,6},{5,7},{6,4},{7,5},{8,10},{9,11},{10,... | collective-permute-start | bytes 638984 | tf_op jit(solution)/shard_map/ppermute | solution.py:33
  11.7 0.0 collective-permute-done.6.refs_3_
  11.7 0.0 collective-permute-done.refs_1_
  11.7 1.5 %shard_map.79 = (bf16[160,512]{1,0:T(8,128)(2,1)S(1)}, bf16[160,512]{1,0:T(8,128)(2,1)S(1)}, bf16[160,512]{1,0:T(8,128)(2,1)S(1)}, f32[2,4,128,128]{3,2,1,0:T(8,128)S(1)}) custom-call(bf16[2048,1536]{1,0:T(8,128)(2,1)S(1)} %get-tuple-element.46.refs_0_.w_ref, bf16[1024,512]{1,0:T(8,128)(2,1)S(1)} %get-tuple-element.45.g_ref, ...), custom_call_target="tpu_custom_call" | custom-call | tf_op jit(solution)/shard_map/pallas_call | solution.py:41
  13.2 0.7 %collective-permute-done.4.value_ref = bf16[192,512]{1,0:T(8,128)(2,1)S(1)} collective-permute-done((bf16[192,512]{1,0:T(8,128)(2,1)S(1)}, bf16[192,512]{1,0:T(8,128)(2,1)S(1)}, u32[]{:S(2)}, u32[]{:S(2)}) %collective-permute-start.4) | collective-permute-done | bytes 196640 | tf_op jit(solution)/shard_map/ppermute | solution.py:33
  13.9 1.9 %collective-permute-start.2 = (bf16[224,512]{1,0:T(8,128)(2,1)S(1)}, bf16[224,512]{1,0:T(8,128)(2,1)S(1)}, u32[]{:S(2)}, u32[]{:S(2)}) collective-permute-start(bf16[224,512]{1,0:T(8,128)(2,1)S(1)} %get-tuple-element.48.refs_0_), channel_id=1, source_target_pairs={{0,2},{1,3},{2,0},{3,1},{4,6},{5,7},{6,4},{7,5},{8,10},{9,11},{10,... | collective-permute-start | bytes 688136 | tf_op jit(solution)/shard_map/ppermute | solution.py:33
  15.9 1.3 %shard_map.81.refs_4_.refs_24_.refs_19_ = f32[4,160,512]{2,1,0:T(8,128)S(1)} custom-call(f32[4,4]{1,0:T(4,128)S(1)} %copy-done, bf16[160,512]{1,0:T(8,128)(2,1)S(1)} %get-tuple-element.51.q_ref.refs_4_, bf16[160,512]{1,0:T(8,128)(2,1)S(1)} %get-tuple-element.52.k_ref.refs_9_, bf16[160,512]{1,0:T(8,128)(2,1)S(1)} %get-tuple-element.53.v_ref.refs_14_, ...), custom_call_target="tpu_custom_call" | custom-call | tf_op jit(solution)/shard_map/pallas_call | solution.py:41
  17.2 0.0 collective-permute-done.7.refs_3_
  17.2 1.7 %shard_map.82 = (bf16[192,512]{1,0:T(8,128)(2,1)S(1)}, bf16[192,512]{1,0:T(8,128)(2,1)S(1)}, bf16[192,512]{1,0:T(8,128)(2,1)S(1)}, f32[2,4,128,128]{3,2,1,0:T(8,128)S(1)}) custom-call(bf16[2048,1536]{1,0:T(8,128)(2,1)S(1)} %get-tuple-element.46.refs_0_.w_ref, bf16[1024,512]{1,0:T(8,128)(2,1)S(1)} %get-tuple-element.45.g_ref, ...), custom_call_target="tpu_custom_call" | custom-call | tf_op jit(solution)/shard_map/pallas_call | solution.py:41
  19.0 0.0 collective-permute-done.3.value_ref
  19.0 0.3 collective-permute-start.8
  19.3 1.1 %collective-permute-start.1 = (bf16[240,512]{1,0:T(8,128)(2,1)S(1)}, bf16[240,512]{1,0:T(8,128)(2,1)S(1)}, u32[]{:S(2)}, u32[]{:S(2)}) collective-permute-start(bf16[240,512]{1,0:T(8,128)(2,1)S(1)} %get-tuple-element.47.refs_0_), channel_id=1, source_target_pairs={{0,2},{1,3},{2,0},{3,1},{4,6},{5,7},{6,4},{7,5},{8,10},{9,11},{10,... | collective-permute-start | bytes 737288 | tf_op jit(solution)/shard_map/ppermute | solution.py:33
  20.5 1.5 %shard_map.84.refs_4_.refs_25_.refs_20_ = f32[4,192,512]{2,1,0:T(8,128)S(1)} custom-call(f32[4,4]{1,0:T(4,128)S(1)} %copy-done, bf16[192,512]{1,0:T(8,128)(2,1)S(1)} %get-tuple-element.55.q_ref.refs_5_, bf16[192,512]{1,0:T(8,128)(2,1)S(1)} %get-tuple-element.56.k_ref.refs_10_, bf16[192,512]{1,0:T(8,128)(2,1)S(1)} %get-tuple-element.57.v_ref.refs_15_, ...), custom_call_target="tpu_custom_call" | custom-call | tf_op jit(solution)/shard_map/pallas_call | solution.py:41
  21.9 1.8 %shard_map.85 = (bf16[208,512]{1,0:T(8,128)(2,1)S(1)}, bf16[208,512]{1,0:T(8,128)(2,1)S(1)}, bf16[208,512]{1,0:T(8,128)(2,1)S(1)}, f32[2,4,128,128]{3,2,1,0:T(8,128)S(1)}) custom-call(bf16[2048,1536]{1,0:T(8,128)(2,1)S(1)} %get-tuple-element.46.refs_0_.w_ref, bf16[1024,512]{1,0:T(8,128)(2,1)S(1)} %get-tuple-element.45.g_ref, ...), custom_call_target="tpu_custom_call" | custom-call | tf_op jit(solution)/shard_map/pallas_call | solution.py:41
  23.8 0.3 collective-permute-start.9
  24.1 1.5 %shard_map.87.refs_4_.refs_26_.refs_21_ = f32[4,208,512]{2,1,0:T(8,128)S(1)} custom-call(f32[4,4]{1,0:T(4,128)S(1)} %copy-done, bf16[208,512]{1,0:T(8,128)(2,1)S(1)} %get-tuple-element.59.q_ref.refs_6_, bf16[208,512]{1,0:T(8,128)(2,1)S(1)} %get-tuple-element.60.k_ref.refs_11_, bf16[208,512]{1,0:T(8,128)(2,1)S(1)} %get-tuple-element.61.v_ref.refs_16_, ...), custom_call_target="tpu_custom_call" | custom-call | tf_op jit(solution)/shard_map/pallas_call | solution.py:41
  25.6 1.9 %shard_map.88 = (bf16[224,512]{1,0:T(8,128)(2,1)S(1)}, bf16[224,512]{1,0:T(8,128)(2,1)S(1)}, bf16[224,512]{1,0:T(8,128)(2,1)S(1)}, f32[2,4,128,128]{3,2,1,0:T(8,128)S(1)}) custom-call(bf16[2048,1536]{1,0:T(8,128)(2,1)S(1)} %get-tuple-element.46.refs_0_.w_ref, bf16[1024,512]{1,0:T(8,128)(2,1)S(1)} %get-tuple-element.45.g_ref, ...), custom_call_target="tpu_custom_call" | custom-call | tf_op jit(solution)/shard_map/pallas_call | solution.py:41
  27.6 0.9 %collective-permute-done.1.value_ref = bf16[240,512]{1,0:T(8,128)(2,1)S(1)} collective-permute-done((bf16[240,512]{1,0:T(8,128)(2,1)S(1)}, bf16[240,512]{1,0:T(8,128)(2,1)S(1)}, u32[]{:S(2)}, u32[]{:S(2)}) %collective-permute-start.1) | collective-permute-done | bytes 245792 | tf_op jit(solution)/shard_map/ppermute | solution.py:33
  28.5 1.4 %shard_map.90 = (f32[240,1536]{1,0:T(8,128)S(1)}, f32[2,4,128,128]{3,2,1,0:T(8,128)S(1)}) custom-call(bf16[2048,1536]{1,0:T(8,128)(2,1)S(1)} %get-tuple-element.46.refs_0_.w_ref, bf16[240,512]{1,0:T(8,128)(2,1)S(1)} %get-tuple-element.47.refs_0_, bf16[1024,512]{1,0:T(8,128)(2,1)S(1)} %collective-permute-done.refs_1_, ...), custom_call_target="tpu_custom_call" | custom-call | tf_op jit(solution)/shard_map/pallas_call | solution.py:41
  30.0 0.1 collective-permute-done.10.late_ref
  30.0 0.9 %shard_map.91 = (bf16[240,512]{1,0:T(8,128)(2,1)S(1)}, bf16[240,512]{1,0:T(8,128)(2,1)S(1)}, bf16[240,512]{1,0:T(8,128)(2,1)S(1)}, f32[2,4,128,128]{3,2,1,0:T(8,...) custom-call(bf16[2048,1536]{1,0:T(8,128)(2,1)S(1)} %get-tuple-elemen, ...), custom_call_target="tpu_custom_call" | custom-call | tf_op jit(solution)/shard_map/pallas_call | solution.py:41
  30.9 2.8 %collective-permute-start.11 = (bf16[2,1,128,128]{3,2,1,0:T(8,128)(2,1)S(1)}, bf16[2,1,128,128]{3,2,1,0:T(8,128)(2,1)S(1)}, u32[]{:S(2)}, u32[]{:S(2)}) collective-permute-start(bf16[2,1,128,128]{3,2,1,0:T(8,128)(2,1)S(1)} %get-tuple-element.66), channel_id=1, source_target_pairs={{0,12},{4,8},{8,4},{12,0},{16,28},{20,24},{24,20},{28,16},{1,13},{... | collective-permute-start | bytes 196616 | tf_op jit(solution)/shard_map/ppermute | solution.py:33
  33.7 0.4 collective-permute-start.12
  34.2 0.3 collective-permute-start.13
  34.5 1.7 %shard_map.93.refs_4_.refs_28_.refs_23_ = f32[4,240,512]{2,1,0:T(8,128)S(1)} custom-call(f32[4,4]{1,0:T(4,128)S(1)} %copy-done, bf16[240,512]{1,0:T(8,128)(2,1)S(1)} %get-tuple-element.72.q_ref.refs_8_, bf16[240,512]{1,0:T(8,128)(2,1)S(1)} %get-tuple-element.73.k_ref.refs_13_, bf16[240,512]{1,0:T(8,128)(2,1)S(1)} %get-tuple-element.74.v_ref.refs_18_, ...), custom_call_target="tpu_custom_call" | custom-call | flops 2949120000 | tf_op jit(solution)/shard_map/pallas_call | solution.py:41
  36.1 1.8 %shard_map.92.refs_3_.refs_27_.refs_22_ = f32[4,224,512]{2,1,0:T(8,128)S(1)} custom-call(f32[4,4]{1,0:T(4,128)S(1)} %copy-done, bf16[224,512]{1,0:T(8,128)(2,1)S(1)} %get-tuple-element.69.q_ref.refs_7_, bf16[224,512]{1,0:T(8,128)(2,1)S(1)} %get-tuple-element.70.k_ref.refs_12_, bf16[224,512]{1,0:T(8,128)(2,1)S(1)} %get-tuple-element.71.v_ref.refs_17_, ...), custom_call_target="tpu_custom_call" | custom-call | flops 2569011200 | tf_op jit(solution)/shard_map/pallas_call | solution.py:41
  37.9 0.1 collective-permute-done.12.refs_1_
  38.0 0.4 collective-permute-done.13.refs_2_
  38.4 0.1 shard_map.94
  38.5 2.7 %collective-permute-start.17 = (bf16[1,128,128]{2,1,0:T(8,128)(2,1)S(1)}, bf16[1,128,128]{2,1,0:T(8,128)(2,1)S(1)}, u32[]{:S(2)}, u32[]{:S(2)}) collective-permute-start(bf16[1,128,128]{2,1,0:T(8,128)(2,1)S(1)} %get-tuple-element.79), channel_id=1, source_target_pairs={{0,16},{4,20},{8,24},{12,28},{16,0},{20,4},{24,8},{28,12},{1,17},{... | collective-permute-start | bytes 98312 | tf_op jit(solution)/shard_map/ppermute | solution.py:33
  41.1 1.3 %collective-permute-start.14 = (bf16[5,128,128]{2,1,0:T(8,128)(2,1)S(1)}, bf16[5,128,128]{2,1,0:T(8,128)(2,1)S(1)}, u32[]{:S(2)}, u32[]{:S(2)}) collective-permute-start(bf16[5,128,128]{2,1,0:T(8,128)(2,1)S(1)} %get-tuple-element.75.refs_0_), channel_id=1, source_target_pairs={{0,4},{4,0},{8,12},{12,8},{16,20},{20,16},{24,28},{28,24},{1,5},{5... | collective-permute-start | bytes 491528 | tf_op jit(solution)/shard_map/ppermute | solution.py:33
  42.4 1.8 %collective-permute-start.16 = (bf16[1,128,128]{2,1,0:T(8,128)(2,1)S(1)}, bf16[1,128,128]{2,1,0:T(8,128)(2,1)S(1)}, u32[]{:S(2)}, u32[]{:S(2)}) collective-permute-start(bf16[1,128,128]{2,1,0:T(8,128)(2,1)S(1)} %get-tuple-element.76), channel_id=1, source_target_pairs={{0,12},{4,8},{8,4},{12,0},{16,28},{20,24},{24,20},{28,16},{1,13},{... | collective-permute-start | bytes 98312 | tf_op jit(solution)/shard_map/ppermute | solution.py:33
  44.2 0.4 collective-permute-start.15
  44.6 2.3 %collective-permute-start.20 = (bf16[1,128,128]{2,1,0:T(8,128)(2,1)S(1)}, bf16[1,128,128]{2,1,0:T(8,128)(2,1)S(1)}, u32[]{:S(2)}, u32[]{:S(2)}) collective-permute-start(bf16[1,128,128]{2,1,0:T(8,128)(2,1)S(1)} %shard_map.96.refs_0_), channel_id=1, source_target_pairs={{0,12},{4,8},{8,4},{12,0},{16,28},{20,24},{24,20},{28,16},{1,13},{... | collective-permute-start | bytes 98312 | tf_op jit(solution)/shard_map/ppermute | solution.py:33
  46.9 0.4 collective-permute-start.19
  47.4 0.1 collective-permute-done.16.refs_3_
  47.4 0.7 %collective-permute-start.18 = (bf16[1,128,128]{2,1,0:T(8,128)(2,1)S(1)}, bf16[1,128,128]{2,1,0:T(8,128)(2,1)S(1)}, u32[]{:S(2)}, u32[]{:S(2)}) collective-permute-start(bf16[1,128,128]{2,1,0:T(8,128)(2,1)S(1)} %shard_map.96.refs_0_), channel_id=1, source_target_pairs={{0,4},{4,0},{8,12},{12,8},{16,20},{20,16},{24,28},{28,24},{1,5},{5... | collective-permute-start | bytes 98312 | tf_op jit(solution)/shard_map/ppermute | solution.py:33
  48.1 0.3 collective-permute-done.15.refs_2_
  48.4 2.5 %shard_map.95 = (bf16[1024,512]{1,0:T(8,128)(2,1)}, bf16[1024,512]{1,0:T(8,128)(2,1)}, bf16[1024,512]{1,0:T(8,128)(2,1)}, bf16[1024,512]{1,0:T(8,128)(2,1)}, f32[5,4,128,128]{3,2,1,0:T(8,128)S(1)}) custom-call(f32[4,4]{1,0:T(4,128)S(1)} %copy-done, bf16[1024,512]{1,0:T(8,128)(2,1)S(1)} %get-tuple-element.45.g_ref, ...), custom_call_target="tpu_custom_call" | custom-call | tf_op jit(solution)/shard_map/pallas_call | solution.py:41
  51.0 0.3 collective-permute-done.18.refs_1_
  51.3 2.3 %shard_map.97 = (bf16[1024,512]{1,0:T(8,128)(2,1)}, bf16[1024,512]{1,0:T(8,128)(2,1)}, bf16[1024,512]{1,0:T(8,128)(2,1)}, bf16[1024,512]{1,0:T(8,128)(2,1)}) custom-call(f32[4,4]{1,0:T(4,128)S(1)} %copy-done, bf16[1024,512]{1,0:T(8,128)(2,1)S(1)} %get-tuple-element.45.g_ref, ...), custom_call_target="tpu_custom_call", output_to_operand_aliasing={{0}: (27, {}), {1}: (28, {}), {2}: (29, {}), {3}: (30, {})} | custom-call | tf_op jit(solution)/shard_map/pallas_call | solution.py:41
  (19 shorter events, 0.0 us)
Async XLA Ops:
  0.6 11.1 %collective-permute-start = (bf16[1024,512]{1,0:T(8,128)(2,1)}, bf16[1024,512]{1,0:T(8,128)(2,1)S(1)}, u32[]{:S(2)}, u32[]{:S(2)}) collective-permute-start(bf16[1024,512]{1,0:T(8,128)(2,1)} %x_ref.3), channel_id=1, source_target_pairs={{0,1},{1,0},{2,3},{3,2},{4,5},{5,4},{6,7},{7,6},{8,9},{9,8},{10,11... | collective-permute-start | bytes 3145736 | tf_op jit(solution)/shard_map/ppermute | solution.py:33
  2.1 7.6 %collective-permute-start.5 = (bf16[160,512]{1,0:T(8,128)(2,1)S(1)}, bf16[160,512]{1,0:T(8,128)(2,1)S(1)}, u32[]{:S(2)}, u32[]{:S(2)}) collective-permute-start(bf16[160,512]{1,0:T(8,128)(2,1)S(1)} %shard_map.75.refs_0_), channel_id=1, source_target_pairs={{0,2},{1,3},{2,0},{3,1},{4,6},{5,7},{6,4},{7,5},{8,10},{9,11},{10,... | collective-permute-start | bytes 491528 | tf_op jit(solution)/shard_map/ppermute | solution.py:33
  6.0 8.0 %collective-permute-start.4 = (bf16[192,512]{1,0:T(8,128)(2,1)S(1)}, bf16[192,512]{1,0:T(8,128)(2,1)S(1)}, u32[]{:S(2)}, u32[]{:S(2)}) collective-permute-start(bf16[192,512]{1,0:T(8,128)(2,1)S(1)} %get-tuple-element.44.after_ref.refs_0_), channel_id=1, source_target_pairs={{0,2},{1,3},{2,0},{3,1},{4,6},{5,7},{6,4},{7,5},{8,10},{9,11},{10,... | collective-permute-start | bytes 589832 | tf_op jit(solution)/shard_map/ppermute | solution.py:33
  9.7 2.0 %collective-permute-start.6 = (bf16[160,512]{1,0:T(8,128)(2,1)S(1)}, bf16[160,512]{1,0:T(8,128)(2,1)S(1)}, u32[]{:S(2)}, u32[]{:S(2)}) collective-permute-start(bf16[160,512]{1,0:T(8,128)(2,1)S(1)} %shard_map.78.refs_2_), channel_id=1, source_target_pairs={{0,1},{1,0},{2,3},{3,2},{4,5},{5,4},{6,7},{7,6},{8,9},{9,8},{10,11... | collective-permute-start | bytes 491528 | tf_op jit(solution)/shard_map/ppermute | solution.py:33
  9.7 9.3 %collective-permute-start.3 = (bf16[208,512]{1,0:T(8,128)(2,1)S(1)}, bf16[208,512]{1,0:T(8,128)(2,1)S(1)}, u32[]{:S(2)}, u32[]{:S(2)}) collective-permute-start(bf16[208,512]{1,0:T(8,128)(2,1)S(1)} %get-tuple-element.49.refs_0_), channel_id=1, source_target_pairs={{0,2},{1,3},{2,0},{3,1},{4,6},{5,7},{6,4},{7,5},{8,10},{9,11},{10,... | collective-permute-start | bytes 638984 | tf_op jit(solution)/shard_map/ppermute | solution.py:33
  11.7 4.2 %copy-start = (f32[4,4]{1,0:T(4,128)S(1)}, f32[4,4]{1,0:T(4,128)}, u32[]{:S(2)}) copy-start(f32[4,4]{1,0:T(4,128)} %weight_ref.13) | copy-start | bytes 196
  13.9 3.3 %collective-permute-start.7 = (bf16[192,512]{1,0:T(8,128)(2,1)S(1)}, bf16[192,512]{1,0:T(8,128)(2,1)S(1)}, u32[]{:S(2)}, u32[]{:S(2)}) collective-permute-start(bf16[192,512]{1,0:T(8,128)(2,1)S(1)} %shard_map.80.after_ref.refs_2_), channel_id=1, source_target_pairs={{0,1},{1,0},{2,3},{3,2},{4,5},{5,4},{6,7},{7,6},{8,9},{9,8},{10,11... | collective-permute-start | bytes 589832 | tf_op jit(solution)/shard_map/ppermute | solution.py:33
  13.9 9.8 %collective-permute-start.2 = (bf16[224,512]{1,0:T(8,128)(2,1)S(1)}, bf16[224,512]{1,0:T(8,128)(2,1)S(1)}, u32[]{:S(2)}, u32[]{:S(2)}) collective-permute-start(bf16[224,512]{1,0:T(8,128)(2,1)S(1)} %get-tuple-element.48.refs_0_), channel_id=1, source_target_pairs={{0,2},{1,3},{2,0},{3,1},{4,6},{5,7},{6,4},{7,5},{8,10},{9,11},{10,... | collective-permute-start | bytes 688136 | tf_op jit(solution)/shard_map/ppermute | solution.py:33
  19.0 2.9 %collective-permute-start.8 = (bf16[208,512]{1,0:T(8,128)(2,1)S(1)}, bf16[208,512]{1,0:T(8,128)(2,1)S(1)}, u32[]{:S(2)}, u32[]{:S(2)}) collective-permute-start(bf16[208,512]{1,0:T(8,128)(2,1)S(1)} %shard_map.83.after_ref.refs_2_), channel_id=1, source_target_pairs={{0,1},{1,0},{2,3},{3,2},{4,5},{5,4},{6,7},{7,6},{8,9},{9,8},{10,11... | collective-permute-start | bytes 638984 | tf_op jit(solution)/shard_map/ppermute | solution.py:33
  19.3 9.2 %collective-permute-start.1 = (bf16[240,512]{1,0:T(8,128)(2,1)S(1)}, bf16[240,512]{1,0:T(8,128)(2,1)S(1)}, u32[]{:S(2)}, u32[]{:S(2)}) collective-permute-start(bf16[240,512]{1,0:T(8,128)(2,1)S(1)} %get-tuple-element.47.refs_0_), channel_id=1, source_target_pairs={{0,2},{1,3},{2,0},{3,1},{4,6},{5,7},{6,4},{7,5},{8,10},{9,11},{10,... | collective-permute-start | bytes 737288 | tf_op jit(solution)/shard_map/ppermute | solution.py:33
  23.8 1.8 %collective-permute-start.9 = (bf16[224,512]{1,0:T(8,128)(2,1)S(1)}, bf16[224,512]{1,0:T(8,128)(2,1)S(1)}, u32[]{:S(2)}, u32[]{:S(2)}) collective-permute-start(bf16[224,512]{1,0:T(8,128)(2,1)S(1)} %shard_map.86.after_ref.refs_2_), channel_id=1, source_target_pairs={{0,1},{1,0},{2,3},{3,2},{4,5},{5,4},{6,7},{7,6},{8,9},{9,8},{10,11... | collective-permute-start | bytes 688136 | tf_op jit(solution)/shard_map/ppermute | solution.py:33
  28.5 1.5 %collective-permute-start.10 = (bf16[240,512]{1,0:T(8,128)(2,1)S(1)}, bf16[240,512]{1,0:T(8,128)(2,1)S(1)}, u32[]{:S(2)}, u32[]{:S(2)}) collective-permute-start(bf16[240,512]{1,0:T(8,128)(2,1)S(1)} %shard_map.89.refs_2_), channel_id=1, source_target_pairs={{0,1},{1,0},{2,3},{3,2},{4,5},{5,4},{6,7},{7,6},{8,9},{9,8},{10,11... | collective-permute-start | bytes 737288 | tf_op jit(solution)/shard_map/ppermute | solution.py:33
  30.9 7.0 %collective-permute-start.11 = (bf16[2,1,128,128]{3,2,1,0:T(8,128)(2,1)S(1)}, bf16[2,1,128,128]{3,2,1,0:T(8,128)(2,1)S(1)}, u32[]{:S(2)}, u32[]{:S(2)}) collective-permute-start(bf16[2,1,128,128]{3,2,1,0:T(8,128)(2,1)S(1)} %get-tuple-element.66), channel_id=1, source_target_pairs={{0,12},{4,8},{8,4},{12,0},{16,28},{20,24},{24,20},{28,16},{1,13},{... | collective-permute-start | bytes 196616 | tf_op jit(solution)/shard_map/ppermute | solution.py:33
  33.7 4.3 %collective-permute-start.12 = (bf16[2,1,128,128]{3,2,1,0:T(8,128)(2,1)S(1)}, bf16[2,1,128,128]{3,2,1,0:T(8,128)(2,1)S(1)}, u32[]{:S(2)}, u32[]{:S(2)}) collective-permute-start(bf16[2,1,128,128]{3,2,1,0:T(8,128)(2,1)S(1)} %get-tuple-element.67), channel_id=1, source_target_pairs={{0,8},{4,12},{8,0},{12,4},{16,24},{20,28},{24,16},{28,20},{1,9},{5... | collective-permute-start | bytes 196616 | tf_op jit(solution)/shard_map/ppermute | solution.py:33
  34.2 4.3 %collective-permute-start.13 = (bf16[2,1,128,128]{3,2,1,0:T(8,128)(2,1)S(1)}, bf16[2,1,128,128]{3,2,1,0:T(8,128)(2,1)S(1)}, u32[]{:S(2)}, u32[]{:S(2)}) collective-permute-start(bf16[2,1,128,128]{3,2,1,0:T(8,128)(2,1)S(1)} %get-tuple-element.68.after_ref), channel_id=1, source_target_pairs={{0,4},{4,0},{8,12},{12,8},{16,20},{20,16},{24,28},{28,24},{1,5},{5... | collective-permute-start | bytes 196616 | tf_op jit(solution)/shard_map/ppermute | solution.py:33
  38.5 6.1 %collective-permute-start.17 = (bf16[1,128,128]{2,1,0:T(8,128)(2,1)S(1)}, bf16[1,128,128]{2,1,0:T(8,128)(2,1)S(1)}, u32[]{:S(2)}, u32[]{:S(2)}) collective-permute-start(bf16[1,128,128]{2,1,0:T(8,128)(2,1)S(1)} %get-tuple-element.79), channel_id=1, source_target_pairs={{0,16},{4,20},{8,24},{12,28},{16,0},{20,4},{24,8},{28,12},{1,17},{... | collective-permute-start | bytes 98312 | tf_op jit(solution)/shard_map/ppermute | solution.py:33
  41.1 7.3 %collective-permute-start.14 = (bf16[5,128,128]{2,1,0:T(8,128)(2,1)S(1)}, bf16[5,128,128]{2,1,0:T(8,128)(2,1)S(1)}, u32[]{:S(2)}, u32[]{:S(2)}) collective-permute-start(bf16[5,128,128]{2,1,0:T(8,128)(2,1)S(1)} %get-tuple-element.75.refs_0_), channel_id=1, source_target_pairs={{0,4},{4,0},{8,12},{12,8},{16,20},{20,16},{24,28},{28,24},{1,5},{5... | collective-permute-start | bytes 491528 | tf_op jit(solution)/shard_map/ppermute | solution.py:33
  42.4 5.0 %collective-permute-start.16 = (bf16[1,128,128]{2,1,0:T(8,128)(2,1)S(1)}, bf16[1,128,128]{2,1,0:T(8,128)(2,1)S(1)}, u32[]{:S(2)}, u32[]{:S(2)}) collective-permute-start(bf16[1,128,128]{2,1,0:T(8,128)(2,1)S(1)} %get-tuple-element.76), channel_id=1, source_target_pairs={{0,12},{4,8},{8,4},{12,0},{16,28},{20,24},{24,20},{28,16},{1,13},{... | collective-permute-start | bytes 98312 | tf_op jit(solution)/shard_map/ppermute | solution.py:33
  44.2 4.2 %collective-permute-start.15 = (bf16[1,128,128]{2,1,0:T(8,128)(2,1)S(1)}, bf16[1,128,128]{2,1,0:T(8,128)(2,1)S(1)}, u32[]{:S(2)}, u32[]{:S(2)}) collective-permute-start(bf16[1,128,128]{2,1,0:T(8,128)(2,1)S(1)} %get-tuple-element.76), channel_id=1, source_target_pairs={{0,8},{4,12},{8,0},{12,4},{16,24},{20,28},{24,16},{28,20},{1,9},{5... | collective-permute-start | bytes 98312 | tf_op jit(solution)/shard_map/ppermute | solution.py:33
  44.6 6.4 %collective-permute-start.20 = (bf16[1,128,128]{2,1,0:T(8,128)(2,1)S(1)}, bf16[1,128,128]{2,1,0:T(8,128)(2,1)S(1)}, u32[]{:S(2)}, u32[]{:S(2)}) collective-permute-start(bf16[1,128,128]{2,1,0:T(8,128)(2,1)S(1)} %shard_map.96.refs_0_), channel_id=1, source_target_pairs={{0,12},{4,8},{8,4},{12,0},{16,28},{20,24},{24,20},{28,16},{1,13},{... | collective-permute-start | bytes 98312 | tf_op jit(solution)/shard_map/ppermute | solution.py:33
  46.9 4.1 %collective-permute-start.19 = (bf16[1,128,128]{2,1,0:T(8,128)(2,1)S(1)}, bf16[1,128,128]{2,1,0:T(8,128)(2,1)S(1)}, u32[]{:S(2)}, u32[]{:S(2)}) collective-permute-start(bf16[1,128,128]{2,1,0:T(8,128)(2,1)S(1)} %shard_map.96.refs_0_), channel_id=1, source_target_pairs={{0,8},{4,12},{8,0},{12,4},{16,24},{20,28},{24,16},{28,20},{1,9},{5... | collective-permute-start | bytes 98312 | tf_op jit(solution)/shard_map/ppermute | solution.py:33
  47.4 3.9 %collective-permute-start.18 = (bf16[1,128,128]{2,1,0:T(8,128)(2,1)S(1)}, bf16[1,128,128]{2,1,0:T(8,128)(2,1)S(1)}, u32[]{:S(2)}, u32[]{:S(2)}) collective-permute-start(bf16[1,128,128]{2,1,0:T(8,128)(2,1)S(1)} %shard_map.96.refs_0_), channel_id=1, source_target_pairs={{0,4},{4,0},{8,12},{12,8},{16,20},{20,16},{24,28},{28,24},{1,5},{5... | collective-permute-start | bytes 98312 | tf_op jit(solution)/shard_map/ppermute | solution.py:33

commit v2 on v1

--- a/solution.py
+++ b/solution.py
@@ -104,8 +104,8 @@
     return pl.pallas_call(
         tie_kernel,
         out_shape=pltpu.VMEM(value.shape, value.dtype),
-        in_specs=[VMEM] + [ANY] * len(after),
-        out_specs=VMEM,
+        in_specs=[ANY] * (1 + len(after)),
+        out_specs=ANY,
         input_output_aliases={0: 0},
         compiler_params=pltpu.CompilerParams(vmem_limit_bytes=MIB),
         cost_estimate=pl.CostEstimate(flops=flops, bytes_accessed=0, transcendentals=0),
@@ -175,27 +175,20 @@
         q, k, v = q_ref[:, cols], k_ref[:, cols], v_ref[:, cols]
         g = g_ref[span[0] : span[1], cols]
         scale = weight_ref[h, 0] * norm
-        pairs = [(q, k, at >= of), (g, v, at >= of)]
-        if 2 * h >= heads:
-            pairs += [(v, g, of >= at), (k, q, of >= at)]
         masked.append(
             [
-                jnp.where(causal, dot(left, right, NT) * scale, 0.0).astype(BF16)
-                for left, right, causal in pairs
+                jnp.where(at >= of, dot(left, right, NT) * scale, 0.0).astype(BF16)
+                for left, right in ((q, k), (g, v))
             ]
         )
     for h, cols in enumerate(columns):
         q, k, v = q_ref[:, cols], k_ref[:, cols], v_ref[:, cols]
         g = g_ref[span[0] : span[1], cols]
-        attend, grad = masked[h][:2]
+        attend, grad = masked[h]
         out_ref[0, :, cols] = dot(attend, v)
         out_ref[1, :, cols] = dot(grad, k)
-        if 2 * h >= heads:
-            out_ref[2, :, cols] = dot(masked[h][2], q)
-            out_ref[3, :, cols] = dot(masked[h][3], g)
-        else:
-            out_ref[2, :, cols] = dot(grad, q, TN)
-            out_ref[3, :, cols] = dot(attend, g, TN)
+        out_ref[2, :, cols] = dot(grad, q, TN)
+        out_ref[3, :, cols] = dot(attend, g, TN)
 
 
 def owner_kernel(final, total_ref, *refs):

time: 54 us -> 53.9 us (level)
  waiting for transfers between devices: 3.38 us -> 4.13 us
  Pallas kernels: 27.5 us -> 26.8 us
    ppermute x21, waiting for transfers between devices: 3.38 us -> 4.13 us  [swap(): return lax.ppermute(value, axis, pairs)]
    pallas_call x17, Pallas kernels: 27.5 us -> 26.8 us  [call(): pl.pallas_call(kernel, out_shape=outs, in_specs=specs, out_specs=[VMEM] *...]
  transfers between devices with their start and end apart: 21 -> 21, of which waited for: 9 -> 9; matrix products, arithmetic and copies ran while one was open for 0% -> 0% of each run, Pallas kernels for 45% -> 44%
where the time goes in v2:
time: 53.9 us; the launch traced here: 53.7 us
  Pallas kernels  26.8 us (50%)
  starting transfers between devices  21.8 us (40%)
  waiting for transfers between devices  4.13 us (8%)
  between operations  0.99 us (2%)
    pallas_call x17, Pallas kernels, call(): pl.pallas_call(kernel, out_shape=outs, in_specs=specs, out_specs=[VMEM] *...  26.8 us
    ppermute x21, starting transfers between devices, swap(): return lax.ppermute(value, axis, pairs)  21.8 us
    ppermute x21, waiting for transfers between devices, swap(): return lax.ppermute(value, axis, pairs)  4.13 us
  transfers between devices with their start and end apart: 21, of which 9 were waited for; matrix products, arithmetic and copies ran while one was open for 0% of the time, Pallas kernels for 44%

profile of v2, /device:TPU:0, one launch (start us, length us, event | category | flops | bytes accessed | tf_op | source)
XLA Modules:
  0.0 53.7 jit_solution(9856755130368259514)
XLA Ops:
  0.6 0.5 collective-permute-start
  1.1 0.9 %shard_map.75.refs_0_ = bf16[160,512]{1,0:T(8,128)(2,1)S(1)} custom-call(bf16[1024,512]{1,0:T(8,128)(2,1)} %x_ref.3), custom_call_target="tpu_custom_call" | custom-call | bytes 2097152 | tf_op jit(solution)/shard_map/pallas_call | solution.py:41
  2.1 2.6 %collective-permute-start.5 = (bf16[160,512]{1,0:T(8,128)(2,1)S(1)}, bf16[160,512]{1,0:T(8,128)(2,1)S(1)}, u32[]{:S(2)}, u32[]{:S(2)}) collective-permute-start(bf16[160,512]{1,0:T(8,128)(2,1)S(1)} %shard_map.75.refs_0_), channel_id=1, source_target_pairs={{0,2},{1,3},{2,0},{3,1},{4,6},{5,7},{6,4},{7,5},{8,10},{9,11},{10,... | collective-permute-start | bytes 491528 | tf_op jit(solution)/shard_map/ppermute | solution.py:33
  4.7 1.3 %shard_map.76 = (bf16[192,512]{1,0:T(8,128)(2,1)S(1)}, bf16[208,512]{1,0:T(8,128)(2,1)S(1)}, bf16[224,512]{1,0:T(8,128)(2,1)S(1)}, bf16[240,512]{1,0:T(8,128)(2,1)S(1)}) custom-call(bf16[1024,512]{1,0:T(8,128)(2,1)} %x_ref.3, bf16[160,512]{1,0:T(8,128)(2,1)S(1)} %shard_map.75.refs_0_), custom_call_target="tpu_custom_call" | custom-call | bytes 2097152 | tf_op jit(solution)/shard_map/pallas_call | solution.py:41
  6.0 0.1 collective-permute-start.4
  6.1 3.2 %shard_map.77 = (bf16[1024,512]{1,0:T(8,128)(2,1)S(1)}, bf16[2048,1536]{1,0:T(8,128)(2,1)S(1)}) custom-call(bf16[1024,512]{1,0:T(8,128)(2,1)} %g_ref.1, bf16[3,2048,512]{2,1,0:T(8,128)(2,1)} %w_ref.1, bf16[192,512]{1,0:T(8,128)(2,1)S(1)} %get-tuple-element.44.after_ref.refs_0_), custom_call_target="tpu_custom_call" | custom-call | bytes 14680064 | tf_op jit(solution)/shard_map/pallas_call | solution.py:41
  9.3 0.5 collective-permute-done.5.value_ref
  9.7 1.9 %collective-permute-start.3 = (bf16[208,512]{1,0:T(8,128)(2,1)S(1)}, bf16[208,512]{1,0:T(8,128)(2,1)S(1)}, u32[]{:S(2)}, u32[]{:S(2)}) collective-permute-start(bf16[208,512]{1,0:T(8,128)(2,1)S(1)} %get-tuple-element.49.refs_0_), channel_id=1, source_target_pairs={{0,2},{1,3},{2,0},{3,1},{4,6},{5,7},{6,4},{7,5},{8,10},{9,11},{10,... | collective-permute-start | bytes 638984 | tf_op jit(solution)/shard_map/ppermute | solution.py:33
  11.7 0.0 collective-permute-done.6.refs_3_
  11.7 0.0 collective-permute-done.refs_1_
  11.7 1.5 %shard_map.79 = (bf16[160,512]{1,0:T(8,128)(2,1)S(1)}, bf16[160,512]{1,0:T(8,128)(2,1)S(1)}, bf16[160,512]{1,0:T(8,128)(2,1)S(1)}, f32[2,4,128,128]{3,2,1,0:T(8,128)S(1)}) custom-call(bf16[2048,1536]{1,0:T(8,128)(2,1)S(1)} %get-tuple-element.46.refs_0_.w_ref, bf16[1024,512]{1,0:T(8,128)(2,1)S(1)} %get-tuple-element.45.g_ref, ...), custom_call_target="tpu_custom_call" | custom-call | tf_op jit(solution)/shard_map/pallas_call | solution.py:41
  13.2 0.7 %collective-permute-done.4.value_ref = bf16[192,512]{1,0:T(8,128)(2,1)S(1)} collective-permute-done((bf16[192,512]{1,0:T(8,128)(2,1)S(1)}, bf16[192,512]{1,0:T(8,128)(2,1)S(1)}, u32[]{:S(2)}, u32[]{:S(2)}) %collective-permute-start.4) | collective-permute-done | bytes 196640 | tf_op jit(solution)/shard_map/ppermute | solution.py:33
  13.9 0.0 collective-permute-start.7
  13.9 1.9 %collective-permute-start.2 = (bf16[224,512]{1,0:T(8,128)(2,1)S(1)}, bf16[224,512]{1,0:T(8,128)(2,1)S(1)}, u32[]{:S(2)}, u32[]{:S(2)}) collective-permute-start(bf16[224,512]{1,0:T(8,128)(2,1)S(1)} %get-tuple-element.48.refs_0_), channel_id=1, source_target_pairs={{0,2},{1,3},{2,0},{3,1},{4,6},{5,7},{6,4},{7,5},{8,10},{9,11},{10,... | collective-permute-start | bytes 688136 | tf_op jit(solution)/shard_map/ppermute | solution.py:33
  15.9 1.3 %shard_map.81.refs_4_.refs_24_.refs_19_ = f32[4,160,512]{2,1,0:T(8,128)S(1)} custom-call(f32[4,4]{1,0:T(4,128)S(1)} %copy-done, bf16[160,512]{1,0:T(8,128)(2,1)S(1)} %get-tuple-element.51.q_ref.refs_4_, bf16[160,512]{1,0:T(8,128)(2,1)S(1)} %get-tuple-element.52.k_ref.refs_9_, bf16[160,512]{1,0:T(8,128)(2,1)S(1)} %get-tuple-element.53.v_ref.refs_14_, ...), custom_call_target="tpu_custom_call" | custom-call | tf_op jit(solution)/shard_map/pallas_call | solution.py:41
  17.2 1.7 %shard_map.82 = (bf16[192,512]{1,0:T(8,128)(2,1)S(1)}, bf16[192,512]{1,0:T(8,128)(2,1)S(1)}, bf16[192,512]{1,0:T(8,128)(2,1)S(1)}, f32[2,4,128,128]{3,2,1,0:T(8,128)S(1)}) custom-call(bf16[2048,1536]{1,0:T(8,128)(2,1)S(1)} %get-tuple-element.46.refs_0_.w_ref, bf16[1024,512]{1,0:T(8,128)(2,1)S(1)} %get-tuple-element.45.g_ref, ...), custom_call_target="tpu_custom_call" | custom-call | tf_op jit(solution)/shard_map/pallas_call | solution.py:41
  18.9 0.0 collective-permute-done.3.value_ref
  19.0 0.3 collective-permute-start.8
  19.3 1.2 %collective-permute-start.1 = (bf16[240,512]{1,0:T(8,128)(2,1)S(1)}, bf16[240,512]{1,0:T(8,128)(2,1)S(1)}, u32[]{:S(2)}, u32[]{:S(2)}) collective-permute-start(bf16[240,512]{1,0:T(8,128)(2,1)S(1)} %get-tuple-element.47.refs_0_), channel_id=1, source_target_pairs={{0,2},{1,3},{2,0},{3,1},{4,6},{5,7},{6,4},{7,5},{8,10},{9,11},{10,... | collective-permute-start | bytes 737288 | tf_op jit(solution)/shard_map/ppermute | solution.py:33
  20.5 1.4 %shard_map.84.refs_4_.refs_25_.refs_20_ = f32[4,192,512]{2,1,0:T(8,128)S(1)} custom-call(f32[4,4]{1,0:T(4,128)S(1)} %copy-done, bf16[192,512]{1,0:T(8,128)(2,1)S(1)} %get-tuple-element.55.q_ref.refs_5_, bf16[192,512]{1,0:T(8,128)(2,1)S(1)} %get-tuple-element.56.k_ref.refs_10_, bf16[192,512]{1,0:T(8,128)(2,1)S(1)} %get-tuple-element.57.v_ref.refs_15_, ...), custom_call_target="tpu_custom_call" | custom-call | tf_op jit(solution)/shard_map/pallas_call | solution.py:41
  21.8 1.8 %shard_map.85 = (bf16[208,512]{1,0:T(8,128)(2,1)S(1)}, bf16[208,512]{1,0:T(8,128)(2,1)S(1)}, bf16[208,512]{1,0:T(8,128)(2,1)S(1)}, f32[2,4,128,128]{3,2,1,0:T(8,128)S(1)}) custom-call(bf16[2048,1536]{1,0:T(8,128)(2,1)S(1)} %get-tuple-element.46.refs_0_.w_ref, bf16[1024,512]{1,0:T(8,128)(2,1)S(1)} %get-tuple-element.45.g_ref, ...), custom_call_target="tpu_custom_call" | custom-call | tf_op jit(solution)/shard_map/pallas_call | solution.py:41
  23.7 0.3 collective-permute-start.9
  24.0 1.4 %shard_map.87.refs_4_.refs_26_.refs_21_ = f32[4,208,512]{2,1,0:T(8,128)S(1)} custom-call(f32[4,4]{1,0:T(4,128)S(1)} %copy-done, bf16[208,512]{1,0:T(8,128)(2,1)S(1)} %get-tuple-element.59.q_ref.refs_6_, bf16[208,512]{1,0:T(8,128)(2,1)S(1)} %get-tuple-element.60.k_ref.refs_11_, bf16[208,512]{1,0:T(8,128)(2,1)S(1)} %get-tuple-element.61.v_ref.refs_16_, ...), custom_call_target="tpu_custom_call" | custom-call | tf_op jit(solution)/shard_map/pallas_call | solution.py:41
  25.4 1.9 %shard_map.88 = (bf16[224,512]{1,0:T(8,128)(2,1)S(1)}, bf16[224,512]{1,0:T(8,128)(2,1)S(1)}, bf16[224,512]{1,0:T(8,128)(2,1)S(1)}, f32[2,4,128,128]{3,2,1,0:T(8,128)S(1)}) custom-call(bf16[2048,1536]{1,0:T(8,128)(2,1)S(1)} %get-tuple-element.46.refs_0_.w_ref, bf16[1024,512]{1,0:T(8,128)(2,1)S(1)} %get-tuple-element.45.g_ref, ...), custom_call_target="tpu_custom_call" | custom-call | tf_op jit(solution)/shard_map/pallas_call | solution.py:41
  27.3 1.1 %collective-permute-done.1.value_ref = bf16[240,512]{1,0:T(8,128)(2,1)S(1)} collective-permute-done((bf16[240,512]{1,0:T(8,128)(2,1)S(1)}, bf16[240,512]{1,0:T(8,128)(2,1)S(1)}, u32[]{:S(2)}, u32[]{:S(2)}) %collective-permute-start.1) | collective-permute-done | bytes 245792 | tf_op jit(solution)/shard_map/ppermute | solution.py:33
  28.5 1.4 %shard_map.90 = (f32[240,1536]{1,0:T(8,128)S(1)}, f32[2,4,128,128]{3,2,1,0:T(8,128)S(1)}) custom-call(bf16[2048,1536]{1,0:T(8,128)(2,1)S(1)} %get-tuple-element.46.refs_0_.w_ref, bf16[240,512]{1,0:T(8,128)(2,1)S(1)} %get-tuple-element.47.refs_0_, bf16[1024,512]{1,0:T(8,128)(2,1)S(1)} %collective-permute-done.refs_1_, ...), custom_call_target="tpu_custom_call" | custom-call | tf_op jit(solution)/shard_map/pallas_call | solution.py:41
  30.0 0.1 collective-permute-done.10.late_ref
  30.0 0.9 %shard_map.91 = (bf16[240,512]{1,0:T(8,128)(2,1)S(1)}, bf16[240,512]{1,0:T(8,128)(2,1)S(1)}, bf16[240,512]{1,0:T(8,128)(2,1)S(1)}, f32[2,4,128,128]{3,2,1,0:T(8,...) custom-call(bf16[2048,1536]{1,0:T(8,128)(2,1)S(1)} %get-tuple-elemen, ...), custom_call_target="tpu_custom_call" | custom-call | tf_op jit(solution)/shard_map/pallas_call | solution.py:41
  30.9 2.8 %collective-permute-start.11 = (bf16[2,1,128,128]{3,2,1,0:T(8,128)(2,1)S(1)}, bf16[2,1,128,128]{3,2,1,0:T(8,128)(2,1)S(1)}, u32[]{:S(2)}, u32[]{:S(2)}) collective-permute-start(bf16[2,1,128,128]{3,2,1,0:T(8,128)(2,1)S(1)} %get-tuple-element.66), channel_id=1, source_target_pairs={{0,12},{4,8},{8,4},{12,0},{16,28},{20,24},{24,20},{28,16},{1,13},{... | collective-permute-start | bytes 196616 | tf_op jit(solution)/shard_map/ppermute | solution.py:33
  33.7 0.4 collective-permute-start.12
  34.2 0.3 collective-permute-start.13
  34.5 1.5 %shard_map.93.refs_4_.refs_28_.refs_23_ = f32[4,240,512]{2,1,0:T(8,128)S(1)} custom-call(f32[4,4]{1,0:T(4,128)S(1)} %copy-done, bf16[240,512]{1,0:T(8,128)(2,1)S(1)} %get-tuple-element.72.q_ref.refs_8_, bf16[240,512]{1,0:T(8,128)(2,1)S(1)} %get-tuple-element.73.k_ref.refs_13_, bf16[240,512]{1,0:T(8,128)(2,1)S(1)} %get-tuple-element.74.v_ref.refs_18_, ...), custom_call_target="tpu_custom_call" | custom-call | flops 2949120000 | tf_op jit(solution)/shard_map/pallas_call | solution.py:41
  36.0 1.5 %shard_map.92.refs_3_.refs_27_.refs_22_ = f32[4,224,512]{2,1,0:T(8,128)S(1)} custom-call(f32[4,4]{1,0:T(4,128)S(1)} %copy-done, bf16[224,512]{1,0:T(8,128)(2,1)S(1)} %get-tuple-element.69.q_ref.refs_7_, bf16[224,512]{1,0:T(8,128)(2,1)S(1)} %get-tuple-element.70.k_ref.refs_12_, bf16[224,512]{1,0:T(8,128)(2,1)S(1)} %get-tuple-element.71.v_ref.refs_17_, ...), custom_call_target="tpu_custom_call" | custom-call | flops 2569011200 | tf_op jit(solution)/shard_map/pallas_call | solution.py:41
  37.5 0.5 collective-permute-done.12.refs_1_
  38.0 0.4 collective-permute-done.13.refs_2_
  38.4 0.1 shard_map.94
  38.5 2.7 %collective-permute-start.17 = (bf16[1,128,128]{2,1,0:T(8,128)(2,1)S(1)}, bf16[1,128,128]{2,1,0:T(8,128)(2,1)S(1)}, u32[]{:S(2)}, u32[]{:S(2)}) collective-permute-start(bf16[1,128,128]{2,1,0:T(8,128)(2,1)S(1)} %get-tuple-element.79), channel_id=1, source_target_pairs={{0,16},{4,20},{8,24},{12,28},{16,0},{20,4},{24,8},{28,12},{1,17},{... | collective-permute-start | bytes 98312 | tf_op jit(solution)/shard_map/ppermute | solution.py:33
  41.1 1.0 %collective-permute-start.14 = (bf16[5,128,128]{2,1,0:T(8,128)(2,1)S(1)}, bf16[5,128,128]{2,1,0:T(8,128)(2,1)S(1)}, u32[]{:S(2)}, u32[]{:S(2)}) collective-permute-start(bf16[5,128,128]{2,1,0:T(8,128)(2,1)S(1)} %get-tuple-element.75.refs_0_), channel_id=1, source_target_pairs={{0,4},{4,0},{8,12},{12,8},{16,20},{20,16},{24,28},{28,24},{1,5},{5... | collective-permute-start | bytes 491528 | tf_op jit(solution)/shard_map/ppermute | solution.py:33
  42.2 2.0 %collective-permute-start.16 = (bf16[1,128,128]{2,1,0:T(8,128)(2,1)S(1)}, bf16[1,128,128]{2,1,0:T(8,128)(2,1)S(1)}, u32[]{:S(2)}, u32[]{:S(2)}) collective-permute-start(bf16[1,128,128]{2,1,0:T(8,128)(2,1)S(1)} %get-tuple-element.76), channel_id=1, source_target_pairs={{0,12},{4,8},{8,4},{12,0},{16,28},{20,24},{24,20},{28,16},{1,13},{... | collective-permute-start | bytes 98312 | tf_op jit(solution)/shard_map/ppermute | solution.py:33
  44.2 0.4 collective-permute-start.15
  44.6 2.1 %collective-permute-start.20 = (bf16[1,128,128]{2,1,0:T(8,128)(2,1)S(1)}, bf16[1,128,128]{2,1,0:T(8,128)(2,1)S(1)}, u32[]{:S(2)}, u32[]{:S(2)}) collective-permute-start(bf16[1,128,128]{2,1,0:T(8,128)(2,1)S(1)} %shard_map.96.refs_0_), channel_id=1, source_target_pairs={{0,12},{4,8},{8,4},{12,0},{16,28},{20,24},{24,20},{28,16},{1,13},{... | collective-permute-start | bytes 98312 | tf_op jit(solution)/shard_map/ppermute | solution.py:33
  46.7 0.4 collective-permute-start.19
  47.1 0.2 collective-permute-done.16.refs_3_
  47.4 0.8 %collective-permute-start.18 = (bf16[1,128,128]{2,1,0:T(8,128)(2,1)S(1)}, bf16[1,128,128]{2,1,0:T(8,128)(2,1)S(1)}, u32[]{:S(2)}, u32[]{:S(2)}) collective-permute-start(bf16[1,128,128]{2,1,0:T(8,128)(2,1)S(1)} %shard_map.96.refs_0_), channel_id=1, source_target_pairs={{0,4},{4,0},{8,12},{12,8},{16,20},{20,16},{24,28},{28,24},{1,5},{5... | collective-permute-start | bytes 98312 | tf_op jit(solution)/shard_map/ppermute | solution.py:33
  48.1 0.3 collective-permute-done.15.refs_2_
  48.4 2.6 %shard_map.95 = (bf16[1024,512]{1,0:T(8,128)(2,1)}, bf16[1024,512]{1,0:T(8,128)(2,1)}, bf16[1024,512]{1,0:T(8,128)(2,1)}, bf16[1024,512]{1,0:T(8,128)(2,1)}, f32[5,4,128,128]{3,2,1,0:T(8,128)S(1)}) custom-call(f32[4,4]{1,0:T(4,128)S(1)} %copy-done, bf16[1024,512]{1,0:T(8,128)(2,1)S(1)} %get-tuple-element.45.g_ref, ...), custom_call_target="tpu_custom_call" | custom-call | tf_op jit(solution)/shard_map/pallas_call | solution.py:41
  51.0 0.3 collective-permute-done.18.refs_1_
  51.3 2.3 %shard_map.97 = (bf16[1024,512]{1,0:T(8,128)(2,1)}, bf16[1024,512]{1,0:T(8,128)(2,1)}, bf16[1024,512]{1,0:T(8,128)(2,1)}, bf16[1024,512]{1,0:T(8,128)(2,1)}) custom-call(f32[4,4]{1,0:T(4,128)S(1)} %copy-done, bf16[1024,512]{1,0:T(8,128)(2,1)S(1)} %get-tuple-element.45.g_ref, ...), custom_call_target="tpu_custom_call", output_to_operand_aliasing={{0}: (27, {}), {1}: (28, {}), {2}: (29, {}), {3}: (30, {})} | custom-call | tf_op jit(solution)/shard_map/pallas_call | solution.py:41
  (19 shorter events, 0.0 us)
Async XLA Ops:
  0.6 11.1 %collective-permute-start = (bf16[1024,512]{1,0:T(8,128)(2,1)}, bf16[1024,512]{1,0:T(8,128)(2,1)S(1)}, u32[]{:S(2)}, u32[]{:S(2)}) collective-permute-start(bf16[1024,512]{1,0:T(8,128)(2,1)} %x_ref.3), channel_id=1, source_target_pairs={{0,1},{1,0},{2,3},{3,2},{4,5},{5,4},{6,7},{7,6},{8,9},{9,8},{10,11... | collective-permute-start | bytes 3145736 | tf_op jit(solution)/shard_map/ppermute | solution.py:33
  2.1 7.6 %collective-permute-start.5 = (bf16[160,512]{1,0:T(8,128)(2,1)S(1)}, bf16[160,512]{1,0:T(8,128)(2,1)S(1)}, u32[]{:S(2)}, u32[]{:S(2)}) collective-permute-start(bf16[160,512]{1,0:T(8,128)(2,1)S(1)} %shard_map.75.refs_0_), channel_id=1, source_target_pairs={{0,2},{1,3},{2,0},{3,1},{4,6},{5,7},{6,4},{7,5},{8,10},{9,11},{10,... | collective-permute-start | bytes 491528 | tf_op jit(solution)/shard_map/ppermute | solution.py:33
  6.0 8.0 %collective-permute-start.4 = (bf16[192,512]{1,0:T(8,128)(2,1)S(1)}, bf16[192,512]{1,0:T(8,128)(2,1)S(1)}, u32[]{:S(2)}, u32[]{:S(2)}) collective-permute-start(bf16[192,512]{1,0:T(8,128)(2,1)S(1)} %get-tuple-element.44.after_ref.refs_0_), channel_id=1, source_target_pairs={{0,2},{1,3},{2,0},{3,1},{4,6},{5,7},{6,4},{7,5},{8,10},{9,11},{10,... | collective-permute-start | bytes 589832 | tf_op jit(solution)/shard_map/ppermute | solution.py:33
  9.7 2.0 %collective-permute-start.6 = (bf16[160,512]{1,0:T(8,128)(2,1)S(1)}, bf16[160,512]{1,0:T(8,128)(2,1)S(1)}, u32[]{:S(2)}, u32[]{:S(2)}) collective-permute-start(bf16[160,512]{1,0:T(8,128)(2,1)S(1)} %shard_map.78.refs_2_), channel_id=1, source_target_pairs={{0,1},{1,0},{2,3},{3,2},{4,5},{5,4},{6,7},{7,6},{8,9},{9,8},{10,11... | collective-permute-start | bytes 491528 | tf_op jit(solution)/shard_map/ppermute | solution.py:33
  9.7 9.2 %collective-permute-start.3 = (bf16[208,512]{1,0:T(8,128)(2,1)S(1)}, bf16[208,512]{1,0:T(8,128)(2,1)S(1)}, u32[]{:S(2)}, u32[]{:S(2)}) collective-permute-start(bf16[208,512]{1,0:T(8,128)(2,1)S(1)} %get-tuple-element.49.refs_0_), channel_id=1, source_target_pairs={{0,2},{1,3},{2,0},{3,1},{4,6},{5,7},{6,4},{7,5},{8,10},{9,11},{10,... | collective-permute-start | bytes 638984 | tf_op jit(solution)/shard_map/ppermute | solution.py:33
  11.7 4.2 %copy-start = (f32[4,4]{1,0:T(4,128)S(1)}, f32[4,4]{1,0:T(4,128)}, u32[]{:S(2)}) copy-start(f32[4,4]{1,0:T(4,128)} %weight_ref.13) | copy-start | bytes 196
  13.9 3.2 %collective-permute-start.7 = (bf16[192,512]{1,0:T(8,128)(2,1)S(1)}, bf16[192,512]{1,0:T(8,128)(2,1)S(1)}, u32[]{:S(2)}, u32[]{:S(2)}) collective-permute-start(bf16[192,512]{1,0:T(8,128)(2,1)S(1)} %shard_map.80.after_ref.refs_2_), channel_id=1, source_target_pairs={{0,1},{1,0},{2,3},{3,2},{4,5},{5,4},{6,7},{7,6},{8,9},{9,8},{10,11... | collective-permute-start | bytes 589832 | tf_op jit(solution)/shard_map/ppermute | solution.py:33
  13.9 9.7 %collective-permute-start.2 = (bf16[224,512]{1,0:T(8,128)(2,1)S(1)}, bf16[224,512]{1,0:T(8,128)(2,1)S(1)}, u32[]{:S(2)}, u32[]{:S(2)}) collective-permute-start(bf16[224,512]{1,0:T(8,128)(2,1)S(1)} %get-tuple-element.48.refs_0_), channel_id=1, source_target_pairs={{0,2},{1,3},{2,0},{3,1},{4,6},{5,7},{6,4},{7,5},{8,10},{9,11},{10,... | collective-permute-start | bytes 688136 | tf_op jit(solution)/shard_map/ppermute | solution.py:33
  19.0 2.9 %collective-permute-start.8 = (bf16[208,512]{1,0:T(8,128)(2,1)S(1)}, bf16[208,512]{1,0:T(8,128)(2,1)S(1)}, u32[]{:S(2)}, u32[]{:S(2)}) collective-permute-start(bf16[208,512]{1,0:T(8,128)(2,1)S(1)} %shard_map.83.after_ref.refs_2_), channel_id=1, source_target_pairs={{0,1},{1,0},{2,3},{3,2},{4,5},{5,4},{6,7},{7,6},{8,9},{9,8},{10,11... | collective-permute-start | bytes 638984 | tf_op jit(solution)/shard_map/ppermute | solution.py:33
  19.3 9.2 %collective-permute-start.1 = (bf16[240,512]{1,0:T(8,128)(2,1)S(1)}, bf16[240,512]{1,0:T(8,128)(2,1)S(1)}, u32[]{:S(2)}, u32[]{:S(2)}) collective-permute-start(bf16[240,512]{1,0:T(8,128)(2,1)S(1)} %get-tuple-element.47.refs_0_), channel_id=1, source_target_pairs={{0,2},{1,3},{2,0},{3,1},{4,6},{5,7},{6,4},{7,5},{8,10},{9,11},{10,... | collective-permute-start | bytes 737288 | tf_op jit(solution)/shard_map/ppermute | solution.py:33
  23.7 1.7 %collective-permute-start.9 = (bf16[224,512]{1,0:T(8,128)(2,1)S(1)}, bf16[224,512]{1,0:T(8,128)(2,1)S(1)}, u32[]{:S(2)}, u32[]{:S(2)}) collective-permute-start(bf16[224,512]{1,0:T(8,128)(2,1)S(1)} %shard_map.86.after_ref.refs_2_), channel_id=1, source_target_pairs={{0,1},{1,0},{2,3},{3,2},{4,5},{5,4},{6,7},{7,6},{8,9},{9,8},{10,11... | collective-permute-start | bytes 688136 | tf_op jit(solution)/shard_map/ppermute | solution.py:33
  28.5 1.5 %collective-permute-start.10 = (bf16[240,512]{1,0:T(8,128)(2,1)S(1)}, bf16[240,512]{1,0:T(8,128)(2,1)S(1)}, u32[]{:S(2)}, u32[]{:S(2)}) collective-permute-start(bf16[240,512]{1,0:T(8,128)(2,1)S(1)} %shard_map.89.refs_2_), channel_id=1, source_target_pairs={{0,1},{1,0},{2,3},{3,2},{4,5},{5,4},{6,7},{7,6},{8,9},{9,8},{10,11... | collective-permute-start | bytes 737288 | tf_op jit(solution)/shard_map/ppermute | solution.py:33
  30.9 6.6 %collective-permute-start.11 = (bf16[2,1,128,128]{3,2,1,0:T(8,128)(2,1)S(1)}, bf16[2,1,128,128]{3,2,1,0:T(8,128)(2,1)S(1)}, u32[]{:S(2)}, u32[]{:S(2)}) collective-permute-start(bf16[2,1,128,128]{3,2,1,0:T(8,128)(2,1)S(1)} %get-tuple-element.66), channel_id=1, source_target_pairs={{0,12},{4,8},{8,4},{12,0},{16,28},{20,24},{24,20},{28,16},{1,13},{... | collective-permute-start | bytes 196616 | tf_op jit(solution)/shard_map/ppermute | solution.py:33
  33.7 4.3 %collective-permute-start.12 = (bf16[2,1,128,128]{3,2,1,0:T(8,128)(2,1)S(1)}, bf16[2,1,128,128]{3,2,1,0:T(8,128)(2,1)S(1)}, u32[]{:S(2)}, u32[]{:S(2)}) collective-permute-start(bf16[2,1,128,128]{3,2,1,0:T(8,128)(2,1)S(1)} %get-tuple-element.67), channel_id=1, source_target_pairs={{0,8},{4,12},{8,0},{12,4},{16,24},{20,28},{24,16},{28,20},{1,9},{5... | collective-permute-start | bytes 196616 | tf_op jit(solution)/shard_map/ppermute | solution.py:33
  34.2 4.3 %collective-permute-start.13 = (bf16[2,1,128,128]{3,2,1,0:T(8,128)(2,1)S(1)}, bf16[2,1,128,128]{3,2,1,0:T(8,128)(2,1)S(1)}, u32[]{:S(2)}, u32[]{:S(2)}) collective-permute-start(bf16[2,1,128,128]{3,2,1,0:T(8,128)(2,1)S(1)} %get-tuple-element.68.after_ref), channel_id=1, source_target_pairs={{0,4},{4,0},{8,12},{12,8},{16,20},{20,16},{24,28},{28,24},{1,5},{5... | collective-permute-start | bytes 196616 | tf_op jit(solution)/shard_map/ppermute | solution.py:33
  38.5 6.1 %collective-permute-start.17 = (bf16[1,128,128]{2,1,0:T(8,128)(2,1)S(1)}, bf16[1,128,128]{2,1,0:T(8,128)(2,1)S(1)}, u32[]{:S(2)}, u32[]{:S(2)}) collective-permute-start(bf16[1,128,128]{2,1,0:T(8,128)(2,1)S(1)} %get-tuple-element.79), channel_id=1, source_target_pairs={{0,16},{4,20},{8,24},{12,28},{16,0},{20,4},{24,8},{28,12},{1,17},{... | collective-permute-start | bytes 98312 | tf_op jit(solution)/shard_map/ppermute | solution.py:33
  41.1 7.2 %collective-permute-start.14 = (bf16[5,128,128]{2,1,0:T(8,128)(2,1)S(1)}, bf16[5,128,128]{2,1,0:T(8,128)(2,1)S(1)}, u32[]{:S(2)}, u32[]{:S(2)}) collective-permute-start(bf16[5,128,128]{2,1,0:T(8,128)(2,1)S(1)} %get-tuple-element.75.refs_0_), channel_id=1, source_target_pairs={{0,4},{4,0},{8,12},{12,8},{16,20},{20,16},{24,28},{28,24},{1,5},{5... | collective-permute-start | bytes 491528 | tf_op jit(solution)/shard_map/ppermute | solution.py:33
  42.2 5.2 %collective-permute-start.16 = (bf16[1,128,128]{2,1,0:T(8,128)(2,1)S(1)}, bf16[1,128,128]{2,1,0:T(8,128)(2,1)S(1)}, u32[]{:S(2)}, u32[]{:S(2)}) collective-permute-start(bf16[1,128,128]{2,1,0:T(8,128)(2,1)S(1)} %get-tuple-element.76), channel_id=1, source_target_pairs={{0,12},{4,8},{8,4},{12,0},{16,28},{20,24},{24,20},{28,16},{1,13},{... | collective-permute-start | bytes 98312 | tf_op jit(solution)/shard_map/ppermute | solution.py:33
  44.2 4.2 %collective-permute-start.15 = (bf16[1,128,128]{2,1,0:T(8,128)(2,1)S(1)}, bf16[1,128,128]{2,1,0:T(8,128)(2,1)S(1)}, u32[]{:S(2)}, u32[]{:S(2)}) collective-permute-start(bf16[1,128,128]{2,1,0:T(8,128)(2,1)S(1)} %get-tuple-element.76), channel_id=1, source_target_pairs={{0,8},{4,12},{8,0},{12,4},{16,24},{20,28},{24,16},{28,20},{1,9},{5... | collective-permute-start | bytes 98312 | tf_op jit(solution)/shard_map/ppermute | solution.py:33
  44.6 6.3 %collective-permute-start.20 = (bf16[1,128,128]{2,1,0:T(8,128)(2,1)S(1)}, bf16[1,128,128]{2,1,0:T(8,128)(2,1)S(1)}, u32[]{:S(2)}, u32[]{:S(2)}) collective-permute-start(bf16[1,128,128]{2,1,0:T(8,128)(2,1)S(1)} %shard_map.96.refs_0_), channel_id=1, source_target_pairs={{0,12},{4,8},{8,4},{12,0},{16,28},{20,24},{24,20},{28,16},{1,13},{... | collective-permute-start | bytes 98312 | tf_op jit(solution)/shard_map/ppermute | solution.py:33
  46.7 4.3 %collective-permute-start.19 = (bf16[1,128,128]{2,1,0:T(8,128)(2,1)S(1)}, bf16[1,128,128]{2,1,0:T(8,128)(2,1)S(1)}, u32[]{:S(2)}, u32[]{:S(2)}) collective-permute-start(bf16[1,128,128]{2,1,0:T(8,128)(2,1)S(1)} %shard_map.96.refs_0_), channel_id=1, source_target_pairs={{0,8},{4,12},{8,0},{12,4},{16,24},{20,28},{24,16},{28,20},{1,9},{5... | collective-permute-start | bytes 98312 | tf_op jit(solution)/shard_map/ppermute | solution.py:33
  47.4 3.9 %collective-permute-start.18 = (bf16[1,128,128]{2,1,0:T(8,128)(2,1)S(1)}, bf16[1,128,128]{2,1,0:T(8,128)(2,1)S(1)}, u32[]{:S(2)}, u32[]{:S(2)}) collective-permute-start(bf16[1,128,128]{2,1,0:T(8,128)(2,1)S(1)} %shard_map.96.refs_0_), channel_id=1, source_target_pairs={{0,4},{4,0},{8,12},{12,8},{16,20},{20,16},{24,28},{28,24},{1,5},{5... | collective-permute-start | bytes 98312 | tf_op jit(solution)/shard_map/ppermute | solution.py:33

commit v3 on v2

--- a/solution.py
+++ b/solution.py
@@ -120,10 +120,14 @@
 
 def write_states(span, heads, q_ref, k_ref, v_ref, g_ref, state_ref):
     size = q_ref.shape[1] // heads
-    for h in range(heads):
-        cols = slice(h * size, (h + 1) * size)
-        state_ref[0, h] = dot(k_ref[:, cols], v_ref[:, cols], TN)
-        state_ref[1, h] = dot(q_ref[:, cols], g_ref[span[0] : span[1], cols], TN)
+    for h in range(0, heads, 2):
+        cols = slice(h * size, (h + 2) * size)
+        for s, (left, right) in enumerate(
+            ((k_ref[:, cols], v_ref[:, cols]), (q_ref[:, cols], g_ref[span[0] : span[1], cols]))
+        ):
+            both = dot(left, right, TN)
+            state_ref[s, h] = both[:size, :size]
+            state_ref[s, h + 1] = both[size:, size:]
 
 
 def early_kernel(span, count, w_ref, *refs):
@@ -353,7 +357,7 @@
                 return [pair_block(*sums[h : h + 2]) for h in range(0, heads, 2)]
 
             rows_of = (q_refs, [g_ref] * chunks, v_refs, k_refs)
-            write_side(spans, side, False, weight_of, rows_of, part_refs, outs, held, sems)
+            write_side(spans, side, True, weight_of, rows_of, part_refs, outs, held, sems)
 
 
 def exchange(totals, sends, local, late):

time: 53.9 us -> 54 us (level)
  transfers between devices with their start and end apart: 21 -> 21, of which waited for: 9 -> 9; matrix products, arithmetic and copies ran while one was open for 0% -> 0% of each run, Pallas kernels for 44% -> 43%
where the time goes in v3:
time: 54 us; the launch traced here: 53.8 us
  Pallas kernels  26.6 us (49%)
  starting transfers between devices  21.9 us (41%)
  waiting for transfers between devices  4.32 us (8%)
  between operations  0.99 us (2%)
    pallas_call x17, Pallas kernels, call(): pl.pallas_call(kernel, out_shape=outs, in_specs=specs, out_specs=[VMEM] *...  26.6 us
    ppermute x21, starting transfers between devices, swap(): return lax.ppermute(value, axis, pairs)  21.9 us
    ppermute x21, waiting for transfers between devices, swap(): return lax.ppermute(value, axis, pairs)  4.32 us
  transfers between devices with their start and end apart: 21, of which 9 were waited for; matrix products, arithmetic and copies ran while one was open for 0% of the time, Pallas kernels for 43%

profile of v3, /device:TPU:0, one launch (start us, length us, event | category | flops | bytes accessed | tf_op | source)
XLA Modules:
  0.0 53.8 jit_solution(1954162089979719878)
XLA Ops:
  0.6 0.5 collective-permute-start
  1.1 0.9 %shard_map.75.refs_0_ = bf16[160,512]{1,0:T(8,128)(2,1)S(1)} custom-call(bf16[1024,512]{1,0:T(8,128)(2,1)} %x_ref.3), custom_call_target="tpu_custom_call" | custom-call | bytes 2097152 | tf_op jit(solution)/shard_map/pallas_call | solution.py:41
  2.1 2.6 %collective-permute-start.5 = (bf16[160,512]{1,0:T(8,128)(2,1)S(1)}, bf16[160,512]{1,0:T(8,128)(2,1)S(1)}, u32[]{:S(2)}, u32[]{:S(2)}) collective-permute-start(bf16[160,512]{1,0:T(8,128)(2,1)S(1)} %shard_map.75.refs_0_), channel_id=1, source_target_pairs={{0,2},{1,3},{2,0},{3,1},{4,6},{5,7},{6,4},{7,5},{8,10},{9,11},{10,... | collective-permute-start | bytes 491528 | tf_op jit(solution)/shard_map/ppermute | solution.py:33
  4.7 1.3 %shard_map.76 = (bf16[192,512]{1,0:T(8,128)(2,1)S(1)}, bf16[208,512]{1,0:T(8,128)(2,1)S(1)}, bf16[224,512]{1,0:T(8,128)(2,1)S(1)}, bf16[240,512]{1,0:T(8,128)(2,1)S(1)}) custom-call(bf16[1024,512]{1,0:T(8,128)(2,1)} %x_ref.3, bf16[160,512]{1,0:T(8,128)(2,1)S(1)} %shard_map.75.refs_0_), custom_call_target="tpu_custom_call" | custom-call | bytes 2097152 | tf_op jit(solution)/shard_map/pallas_call | solution.py:41
  6.0 0.1 collective-permute-start.4
  6.1 3.2 %shard_map.77 = (bf16[1024,512]{1,0:T(8,128)(2,1)S(1)}, bf16[2048,1536]{1,0:T(8,128)(2,1)S(1)}) custom-call(bf16[1024,512]{1,0:T(8,128)(2,1)} %g_ref.1, bf16[3,2048,512]{2,1,0:T(8,128)(2,1)} %w_ref.1, bf16[192,512]{1,0:T(8,128)(2,1)S(1)} %get-tuple-element.44.after_ref.refs_0_), custom_call_target="tpu_custom_call" | custom-call | bytes 14680064 | tf_op jit(solution)/shard_map/pallas_call | solution.py:41
  9.3 0.5 collective-permute-done.5.value_ref
  9.7 0.0 collective-permute-start.6
  9.7 1.9 %collective-permute-start.3 = (bf16[208,512]{1,0:T(8,128)(2,1)S(1)}, bf16[208,512]{1,0:T(8,128)(2,1)S(1)}, u32[]{:S(2)}, u32[]{:S(2)}) collective-permute-start(bf16[208,512]{1,0:T(8,128)(2,1)S(1)} %get-tuple-element.49.refs_0_), channel_id=1, source_target_pairs={{0,2},{1,3},{2,0},{3,1},{4,6},{5,7},{6,4},{7,5},{8,10},{9,11},{10,... | collective-permute-start | bytes 638984 | tf_op jit(solution)/shard_map/ppermute | solution.py:33
  11.7 0.0 collective-permute-done.refs_1_
  11.7 1.5 %shard_map.79 = (bf16[160,512]{1,0:T(8,128)(2,1)S(1)}, bf16[160,512]{1,0:T(8,128)(2,1)S(1)}, bf16[160,512]{1,0:T(8,128)(2,1)S(1)}, f32[2,4,128,128]{3,2,1,0:T(8,128)S(1)}) custom-call(bf16[2048,1536]{1,0:T(8,128)(2,1)S(1)} %get-tuple-element.46.refs_0_.w_ref, bf16[1024,512]{1,0:T(8,128)(2,1)S(1)} %get-tuple-element.45.g_ref, ...), custom_call_target="tpu_custom_call" | custom-call | tf_op jit(solution)/shard_map/pallas_call | solution.py:41
  13.2 0.8 %collective-permute-done.4.value_ref = bf16[192,512]{1,0:T(8,128)(2,1)S(1)} collective-permute-done((bf16[192,512]{1,0:T(8,128)(2,1)S(1)}, bf16[192,512]{1,0:T(8,128)(2,1)S(1)}, u32[]{:S(2)}, u32[]{:S(2)}) %collective-permute-start.4) | collective-permute-done | bytes 196640 | tf_op jit(solution)/shard_map/ppermute | solution.py:33
  13.9 0.0 collective-permute-start.7
  13.9 1.9 %collective-permute-start.2 = (bf16[224,512]{1,0:T(8,128)(2,1)S(1)}, bf16[224,512]{1,0:T(8,128)(2,1)S(1)}, u32[]{:S(2)}, u32[]{:S(2)}) collective-permute-start(bf16[224,512]{1,0:T(8,128)(2,1)S(1)} %get-tuple-element.48.refs_0_), channel_id=1, source_target_pairs={{0,2},{1,3},{2,0},{3,1},{4,6},{5,7},{6,4},{7,5},{8,10},{9,11},{10,... | collective-permute-start | bytes 688136 | tf_op jit(solution)/shard_map/ppermute | solution.py:33
  15.9 1.3 %shard_map.81.refs_4_.refs_24_.refs_19_ = f32[4,160,512]{2,1,0:T(8,128)S(1)} custom-call(f32[4,4]{1,0:T(4,128)S(1)} %copy-done, bf16[160,512]{1,0:T(8,128)(2,1)S(1)} %get-tuple-element.51.q_ref.refs_4_, bf16[160,512]{1,0:T(8,128)(2,1)S(1)} %get-tuple-element.52.k_ref.refs_9_, bf16[160,512]{1,0:T(8,128)(2,1)S(1)} %get-tuple-element.53.v_ref.refs_14_, ...), custom_call_target="tpu_custom_call" | custom-call | tf_op jit(solution)/shard_map/pallas_call | solution.py:41
  17.2 1.7 %shard_map.82 = (bf16[192,512]{1,0:T(8,128)(2,1)S(1)}, bf16[192,512]{1,0:T(8,128)(2,1)S(1)}, bf16[192,512]{1,0:T(8,128)(2,1)S(1)}, f32[2,4,128,128]{3,2,1,0:T(8,128)S(1)}) custom-call(bf16[2048,1536]{1,0:T(8,128)(2,1)S(1)} %get-tuple-element.46.refs_0_.w_ref, bf16[1024,512]{1,0:T(8,128)(2,1)S(1)} %get-tuple-element.45.g_ref, ...), custom_call_target="tpu_custom_call" | custom-call | tf_op jit(solution)/shard_map/pallas_call | solution.py:41
  18.9 0.0 collective-permute-done.3.value_ref
  18.9 0.3 collective-permute-start.8
  19.2 1.3 %collective-permute-start.1 = (bf16[240,512]{1,0:T(8,128)(2,1)S(1)}, bf16[240,512]{1,0:T(8,128)(2,1)S(1)}, u32[]{:S(2)}, u32[]{:S(2)}) collective-permute-start(bf16[240,512]{1,0:T(8,128)(2,1)S(1)} %get-tuple-element.47.refs_0_), channel_id=1, source_target_pairs={{0,2},{1,3},{2,0},{3,1},{4,6},{5,7},{6,4},{7,5},{8,10},{9,11},{10,... | collective-permute-start | bytes 737288 | tf_op jit(solution)/shard_map/ppermute | solution.py:33
  20.5 1.4 %shard_map.84.refs_4_.refs_25_.refs_20_ = f32[4,192,512]{2,1,0:T(8,128)S(1)} custom-call(f32[4,4]{1,0:T(4,128)S(1)} %copy-done, bf16[192,512]{1,0:T(8,128)(2,1)S(1)} %get-tuple-element.55.q_ref.refs_5_, bf16[192,512]{1,0:T(8,128)(2,1)S(1)} %get-tuple-element.56.k_ref.refs_10_, bf16[192,512]{1,0:T(8,128)(2,1)S(1)} %get-tuple-element.57.v_ref.refs_15_, ...), custom_call_target="tpu_custom_call" | custom-call | tf_op jit(solution)/shard_map/pallas_call | solution.py:41
  21.8 1.8 %shard_map.85 = (bf16[208,512]{1,0:T(8,128)(2,1)S(1)}, bf16[208,512]{1,0:T(8,128)(2,1)S(1)}, bf16[208,512]{1,0:T(8,128)(2,1)S(1)}, f32[2,4,128,128]{3,2,1,0:T(8,128)S(1)}) custom-call(bf16[2048,1536]{1,0:T(8,128)(2,1)S(1)} %get-tuple-element.46.refs_0_.w_ref, bf16[1024,512]{1,0:T(8,128)(2,1)S(1)} %get-tuple-element.45.g_ref, ...), custom_call_target="tpu_custom_call" | custom-call | tf_op jit(solution)/shard_map/pallas_call | solution.py:41
  23.6 0.3 collective-permute-start.9
  23.9 1.4 %shard_map.87.refs_4_.refs_26_.refs_21_ = f32[4,208,512]{2,1,0:T(8,128)S(1)} custom-call(f32[4,4]{1,0:T(4,128)S(1)} %copy-done, bf16[208,512]{1,0:T(8,128)(2,1)S(1)} %get-tuple-element.59.q_ref.refs_6_, bf16[208,512]{1,0:T(8,128)(2,1)S(1)} %get-tuple-element.60.k_ref.refs_11_, bf16[208,512]{1,0:T(8,128)(2,1)S(1)} %get-tuple-element.61.v_ref.refs_16_, ...), custom_call_target="tpu_custom_call" | custom-call | tf_op jit(solution)/shard_map/pallas_call | solution.py:41
  25.4 1.9 %shard_map.88 = (bf16[224,512]{1,0:T(8,128)(2,1)S(1)}, bf16[224,512]{1,0:T(8,128)(2,1)S(1)}, bf16[224,512]{1,0:T(8,128)(2,1)S(1)}, f32[2,4,128,128]{3,2,1,0:T(8,128)S(1)}) custom-call(bf16[2048,1536]{1,0:T(8,128)(2,1)S(1)} %get-tuple-element.46.refs_0_.w_ref, bf16[1024,512]{1,0:T(8,128)(2,1)S(1)} %get-tuple-element.45.g_ref, ...), custom_call_target="tpu_custom_call" | custom-call | tf_op jit(solution)/shard_map/pallas_call | solution.py:41
  27.2 1.3 %collective-permute-done.1.value_ref = bf16[240,512]{1,0:T(8,128)(2,1)S(1)} collective-permute-done((bf16[240,512]{1,0:T(8,128)(2,1)S(1)}, bf16[240,512]{1,0:T(8,128)(2,1)S(1)}, u32[]{:S(2)}, u32[]{:S(2)}) %collective-permute-start.1) | collective-permute-done | bytes 245792 | tf_op jit(solution)/shard_map/ppermute | solution.py:33
  28.5 1.4 %shard_map.90 = (f32[240,1536]{1,0:T(8,128)S(1)}, f32[2,4,128,128]{3,2,1,0:T(8,128)S(1)}) custom-call(bf16[2048,1536]{1,0:T(8,128)(2,1)S(1)} %get-tuple-element.46.refs_0_.w_ref, bf16[240,512]{1,0:T(8,128)(2,1)S(1)} %get-tuple-element.47.refs_0_, bf16[1024,512]{1,0:T(8,128)(2,1)S(1)} %collective-permute-done.refs_1_, ...), custom_call_target="tpu_custom_call" | custom-call | tf_op jit(solution)/shard_map/pallas_call | solution.py:41
  30.0 0.1 collective-permute-done.10.late_ref
  30.0 0.9 %shard_map.91 = (bf16[240,512]{1,0:T(8,128)(2,1)S(1)}, bf16[240,512]{1,0:T(8,128)(2,1)S(1)}, bf16[240,512]{1,0:T(8,128)(2,1)S(1)}, f32[2,4,128,128]{3,2,1,0:T(8,...) custom-call(bf16[2048,1536]{1,0:T(8,128)(2,1)S(1)} %get-tuple-elemen, ...), custom_call_target="tpu_custom_call" | custom-call | tf_op jit(solution)/shard_map/pallas_call | solution.py:41
  30.9 2.8 %collective-permute-start.11 = (bf16[2,1,128,128]{3,2,1,0:T(8,128)(2,1)S(1)}, bf16[2,1,128,128]{3,2,1,0:T(8,128)(2,1)S(1)}, u32[]{:S(2)}, u32[]{:S(2)}) collective-permute-start(bf16[2,1,128,128]{3,2,1,0:T(8,128)(2,1)S(1)} %get-tuple-element.66), channel_id=1, source_target_pairs={{0,12},{4,8},{8,4},{12,0},{16,28},{20,24},{24,20},{28,16},{1,13},{... | collective-permute-start | bytes 196616 | tf_op jit(solution)/shard_map/ppermute | solution.py:33
  33.7 0.5 collective-permute-start.12
  34.1 0.3 collective-permute-start.13
  34.5 1.5 %shard_map.93.refs_4_.refs_28_.refs_23_ = f32[4,240,512]{2,1,0:T(8,128)S(1)} custom-call(f32[4,4]{1,0:T(4,128)S(1)} %copy-done, bf16[240,512]{1,0:T(8,128)(2,1)S(1)} %get-tuple-element.72.q_ref.refs_8_, bf16[240,512]{1,0:T(8,128)(2,1)S(1)} %get-tuple-element.73.k_ref.refs_13_, bf16[240,512]{1,0:T(8,128)(2,1)S(1)} %get-tuple-element.74.v_ref.refs_18_, ...), custom_call_target="tpu_custom_call" | custom-call | flops 2949120000 | tf_op jit(solution)/shard_map/pallas_call | solution.py:41
  36.0 1.5 %shard_map.92.refs_3_.refs_27_.refs_22_ = f32[4,224,512]{2,1,0:T(8,128)S(1)} custom-call(f32[4,4]{1,0:T(4,128)S(1)} %copy-done, bf16[224,512]{1,0:T(8,128)(2,1)S(1)} %get-tuple-element.69.q_ref.refs_7_, bf16[224,512]{1,0:T(8,128)(2,1)S(1)} %get-tuple-element.70.k_ref.refs_12_, bf16[224,512]{1,0:T(8,128)(2,1)S(1)} %get-tuple-element.71.v_ref.refs_17_, ...), custom_call_target="tpu_custom_call" | custom-call | flops 2569011200 | tf_op jit(solution)/shard_map/pallas_call | solution.py:41
  37.5 0.5 collective-permute-done.12.refs_1_
  38.0 0.4 collective-permute-done.13.refs_2_
  38.4 0.1 shard_map.94
  38.5 2.7 %collective-permute-start.17 = (bf16[1,128,128]{2,1,0:T(8,128)(2,1)S(1)}, bf16[1,128,128]{2,1,0:T(8,128)(2,1)S(1)}, u32[]{:S(2)}, u32[]{:S(2)}) collective-permute-start(bf16[1,128,128]{2,1,0:T(8,128)(2,1)S(1)} %get-tuple-element.79), channel_id=1, source_target_pairs={{0,16},{4,20},{8,24},{12,28},{16,0},{20,4},{24,8},{28,12},{1,17},{... | collective-permute-start | bytes 98312 | tf_op jit(solution)/shard_map/ppermute | solution.py:33
  41.1 1.0 %collective-permute-start.14 = (bf16[5,128,128]{2,1,0:T(8,128)(2,1)S(1)}, bf16[5,128,128]{2,1,0:T(8,128)(2,1)S(1)}, u32[]{:S(2)}, u32[]{:S(2)}) collective-permute-start(bf16[5,128,128]{2,1,0:T(8,128)(2,1)S(1)} %get-tuple-element.75.refs_0_), channel_id=1, source_target_pairs={{0,4},{4,0},{8,12},{12,8},{16,20},{20,16},{24,28},{28,24},{1,5},{5... | collective-permute-start | bytes 491528 | tf_op jit(solution)/shard_map/ppermute | solution.py:33
  42.2 2.0 %collective-permute-start.16 = (bf16[1,128,128]{2,1,0:T(8,128)(2,1)S(1)}, bf16[1,128,128]{2,1,0:T(8,128)(2,1)S(1)}, u32[]{:S(2)}, u32[]{:S(2)}) collective-permute-start(bf16[1,128,128]{2,1,0:T(8,128)(2,1)S(1)} %get-tuple-element.76), channel_id=1, source_target_pairs={{0,12},{4,8},{8,4},{12,0},{16,28},{20,24},{24,20},{28,16},{1,13},{... | collective-permute-start | bytes 98312 | tf_op jit(solution)/shard_map/ppermute | solution.py:33
  44.2 0.4 collective-permute-start.15
  44.6 2.1 %collective-permute-start.20 = (bf16[1,128,128]{2,1,0:T(8,128)(2,1)S(1)}, bf16[1,128,128]{2,1,0:T(8,128)(2,1)S(1)}, u32[]{:S(2)}, u32[]{:S(2)}) collective-permute-start(bf16[1,128,128]{2,1,0:T(8,128)(2,1)S(1)} %shard_map.96.refs_0_), channel_id=1, source_target_pairs={{0,12},{4,8},{8,4},{12,0},{16,28},{20,24},{24,20},{28,16},{1,13},{... | collective-permute-start | bytes 98312 | tf_op jit(solution)/shard_map/ppermute | solution.py:33
  46.7 0.4 collective-permute-start.19
  47.1 0.2 collective-permute-done.16.refs_3_
  47.4 0.8 %collective-permute-start.18 = (bf16[1,128,128]{2,1,0:T(8,128)(2,1)S(1)}, bf16[1,128,128]{2,1,0:T(8,128)(2,1)S(1)}, u32[]{:S(2)}, u32[]{:S(2)}) collective-permute-start(bf16[1,128,128]{2,1,0:T(8,128)(2,1)S(1)} %shard_map.96.refs_0_), channel_id=1, source_target_pairs={{0,4},{4,0},{8,12},{12,8},{16,20},{20,16},{24,28},{28,24},{1,5},{5... | collective-permute-start | bytes 98312 | tf_op jit(solution)/shard_map/ppermute | solution.py:33
  48.1 0.3 collective-permute-done.15.refs_2_
  48.4 2.5 %shard_map.95 = (bf16[1024,512]{1,0:T(8,128)(2,1)}, bf16[1024,512]{1,0:T(8,128)(2,1)}, bf16[1024,512]{1,0:T(8,128)(2,1)}, bf16[1024,512]{1,0:T(8,128)(2,1)}, f32[5,4,128,128]{3,2,1,0:T(8,128)S(1)}) custom-call(f32[4,4]{1,0:T(4,128)S(1)} %copy-done, bf16[1024,512]{1,0:T(8,128)(2,1)S(1)} %get-tuple-element.45.g_ref, ...), custom_call_target="tpu_custom_call" | custom-call | tf_op jit(solution)/shard_map/pallas_call | solution.py:41
  50.9 0.3 collective-permute-done.18.refs_1_
  51.3 2.4 %shard_map.97 = (bf16[1024,512]{1,0:T(8,128)(2,1)}, bf16[1024,512]{1,0:T(8,128)(2,1)}, bf16[1024,512]{1,0:T(8,128)(2,1)}, bf16[1024,512]{1,0:T(8,128)(2,1)}) custom-call(f32[4,4]{1,0:T(4,128)S(1)} %copy-done, bf16[1024,512]{1,0:T(8,128)(2,1)S(1)} %get-tuple-element.45.g_ref, ...), custom_call_target="tpu_custom_call", output_to_operand_aliasing={{0}: (27, {}), {1}: (28, {}), {2}: (29, {}), {3}: (30, {})} | custom-call | tf_op jit(solution)/shard_map/pallas_call | solution.py:41
  (19 shorter events, 0.0 us)
Async XLA Ops:
  0.6 11.1 %collective-permute-start = (bf16[1024,512]{1,0:T(8,128)(2,1)}, bf16[1024,512]{1,0:T(8,128)(2,1)S(1)}, u32[]{:S(2)}, u32[]{:S(2)}) collective-permute-start(bf16[1024,512]{1,0:T(8,128)(2,1)} %x_ref.3), channel_id=1, source_target_pairs={{0,1},{1,0},{2,3},{3,2},{4,5},{5,4},{6,7},{7,6},{8,9},{9,8},{10,11... | collective-permute-start | bytes 3145736 | tf_op jit(solution)/shard_map/ppermute | solution.py:33
  2.1 7.6 %collective-permute-start.5 = (bf16[160,512]{1,0:T(8,128)(2,1)S(1)}, bf16[160,512]{1,0:T(8,128)(2,1)S(1)}, u32[]{:S(2)}, u32[]{:S(2)}) collective-permute-start(bf16[160,512]{1,0:T(8,128)(2,1)S(1)} %shard_map.75.refs_0_), channel_id=1, source_target_pairs={{0,2},{1,3},{2,0},{3,1},{4,6},{5,7},{6,4},{7,5},{8,10},{9,11},{10,... | collective-permute-start | bytes 491528 | tf_op jit(solution)/shard_map/ppermute | solution.py:33
  6.0 8.0 %collective-permute-start.4 = (bf16[192,512]{1,0:T(8,128)(2,1)S(1)}, bf16[192,512]{1,0:T(8,128)(2,1)S(1)}, u32[]{:S(2)}, u32[]{:S(2)}) collective-permute-start(bf16[192,512]{1,0:T(8,128)(2,1)S(1)} %get-tuple-element.44.after_ref.refs_0_), channel_id=1, source_target_pairs={{0,2},{1,3},{2,0},{3,1},{4,6},{5,7},{6,4},{7,5},{8,10},{9,11},{10,... | collective-permute-start | bytes 589832 | tf_op jit(solution)/shard_map/ppermute | solution.py:33
  9.7 2.0 %collective-permute-start.6 = (bf16[160,512]{1,0:T(8,128)(2,1)S(1)}, bf16[160,512]{1,0:T(8,128)(2,1)S(1)}, u32[]{:S(2)}, u32[]{:S(2)}) collective-permute-start(bf16[160,512]{1,0:T(8,128)(2,1)S(1)} %shard_map.78.refs_2_), channel_id=1, source_target_pairs={{0,1},{1,0},{2,3},{3,2},{4,5},{5,4},{6,7},{7,6},{8,9},{9,8},{10,11... | collective-permute-start | bytes 491528 | tf_op jit(solution)/shard_map/ppermute | solution.py:33
  9.7 9.2 %collective-permute-start.3 = (bf16[208,512]{1,0:T(8,128)(2,1)S(1)}, bf16[208,512]{1,0:T(8,128)(2,1)S(1)}, u32[]{:S(2)}, u32[]{:S(2)}) collective-permute-start(bf16[208,512]{1,0:T(8,128)(2,1)S(1)} %get-tuple-element.49.refs_0_), channel_id=1, source_target_pairs={{0,2},{1,3},{2,0},{3,1},{4,6},{5,7},{6,4},{7,5},{8,10},{9,11},{10,... | collective-permute-start | bytes 638984 | tf_op jit(solution)/shard_map/ppermute | solution.py:33
  11.7 4.2 %copy-start = (f32[4,4]{1,0:T(4,128)S(1)}, f32[4,4]{1,0:T(4,128)}, u32[]{:S(2)}) copy-start(f32[4,4]{1,0:T(4,128)} %weight_ref.13) | copy-start | bytes 196
  13.9 3.2 %collective-permute-start.7 = (bf16[192,512]{1,0:T(8,128)(2,1)S(1)}, bf16[192,512]{1,0:T(8,128)(2,1)S(1)}, u32[]{:S(2)}, u32[]{:S(2)}) collective-permute-start(bf16[192,512]{1,0:T(8,128)(2,1)S(1)} %shard_map.80.after_ref.refs_2_), channel_id=1, source_target_pairs={{0,1},{1,0},{2,3},{3,2},{4,5},{5,4},{6,7},{7,6},{8,9},{9,8},{10,11... | collective-permute-start | bytes 589832 | tf_op jit(solution)/shard_map/ppermute | solution.py:33
  13.9 9.7 %collective-permute-start.2 = (bf16[224,512]{1,0:T(8,128)(2,1)S(1)}, bf16[224,512]{1,0:T(8,128)(2,1)S(1)}, u32[]{:S(2)}, u32[]{:S(2)}) collective-permute-start(bf16[224,512]{1,0:T(8,128)(2,1)S(1)} %get-tuple-element.48.refs_0_), channel_id=1, source_target_pairs={{0,2},{1,3},{2,0},{3,1},{4,6},{5,7},{6,4},{7,5},{8,10},{9,11},{10,... | collective-permute-start | bytes 688136 | tf_op jit(solution)/shard_map/ppermute | solution.py:33
  18.9 2.9 %collective-permute-start.8 = (bf16[208,512]{1,0:T(8,128)(2,1)S(1)}, bf16[208,512]{1,0:T(8,128)(2,1)S(1)}, u32[]{:S(2)}, u32[]{:S(2)}) collective-permute-start(bf16[208,512]{1,0:T(8,128)(2,1)S(1)} %shard_map.83.after_ref.refs_2_), channel_id=1, source_target_pairs={{0,1},{1,0},{2,3},{3,2},{4,5},{5,4},{6,7},{7,6},{8,9},{9,8},{10,11... | collective-permute-start | bytes 638984 | tf_op jit(solution)/shard_map/ppermute | solution.py:33
  19.2 9.3 %collective-permute-start.1 = (bf16[240,512]{1,0:T(8,128)(2,1)S(1)}, bf16[240,512]{1,0:T(8,128)(2,1)S(1)}, u32[]{:S(2)}, u32[]{:S(2)}) collective-permute-start(bf16[240,512]{1,0:T(8,128)(2,1)S(1)} %get-tuple-element.47.refs_0_), channel_id=1, source_target_pairs={{0,2},{1,3},{2,0},{3,1},{4,6},{5,7},{6,4},{7,5},{8,10},{9,11},{10,... | collective-permute-start | bytes 737288 | tf_op jit(solution)/shard_map/ppermute | solution.py:33
  23.6 1.7 %collective-permute-start.9 = (bf16[224,512]{1,0:T(8,128)(2,1)S(1)}, bf16[224,512]{1,0:T(8,128)(2,1)S(1)}, u32[]{:S(2)}, u32[]{:S(2)}) collective-permute-start(bf16[224,512]{1,0:T(8,128)(2,1)S(1)} %shard_map.86.after_ref.refs_2_), channel_id=1, source_target_pairs={{0,1},{1,0},{2,3},{3,2},{4,5},{5,4},{6,7},{7,6},{8,9},{9,8},{10,11... | collective-permute-start | bytes 688136 | tf_op jit(solution)/shard_map/ppermute | solution.py:33
  28.5 1.5 %collective-permute-start.10 = (bf16[240,512]{1,0:T(8,128)(2,1)S(1)}, bf16[240,512]{1,0:T(8,128)(2,1)S(1)}, u32[]{:S(2)}, u32[]{:S(2)}) collective-permute-start(bf16[240,512]{1,0:T(8,128)(2,1)S(1)} %shard_map.89.refs_2_), channel_id=1, source_target_pairs={{0,1},{1,0},{2,3},{3,2},{4,5},{5,4},{6,7},{7,6},{8,9},{9,8},{10,11... | collective-permute-start | bytes 737288 | tf_op jit(solution)/shard_map/ppermute | solution.py:33
  30.9 6.6 %collective-permute-start.11 = (bf16[2,1,128,128]{3,2,1,0:T(8,128)(2,1)S(1)}, bf16[2,1,128,128]{3,2,1,0:T(8,128)(2,1)S(1)}, u32[]{:S(2)}, u32[]{:S(2)}) collective-permute-start(bf16[2,1,128,128]{3,2,1,0:T(8,128)(2,1)S(1)} %get-tuple-element.66), channel_id=1, source_target_pairs={{0,12},{4,8},{8,4},{12,0},{16,28},{20,24},{24,20},{28,16},{1,13},{... | collective-permute-start | bytes 196616 | tf_op jit(solution)/shard_map/ppermute | solution.py:33
  33.7 4.3 %collective-permute-start.12 = (bf16[2,1,128,128]{3,2,1,0:T(8,128)(2,1)S(1)}, bf16[2,1,128,128]{3,2,1,0:T(8,128)(2,1)S(1)}, u32[]{:S(2)}, u32[]{:S(2)}) collective-permute-start(bf16[2,1,128,128]{3,2,1,0:T(8,128)(2,1)S(1)} %get-tuple-element.67), channel_id=1, source_target_pairs={{0,8},{4,12},{8,0},{12,4},{16,24},{20,28},{24,16},{28,20},{1,9},{5... | collective-permute-start | bytes 196616 | tf_op jit(solution)/shard_map/ppermute | solution.py:33
  34.1 4.3 %collective-permute-start.13 = (bf16[2,1,128,128]{3,2,1,0:T(8,128)(2,1)S(1)}, bf16[2,1,128,128]{3,2,1,0:T(8,128)(2,1)S(1)}, u32[]{:S(2)}, u32[]{:S(2)}) collective-permute-start(bf16[2,1,128,128]{3,2,1,0:T(8,128)(2,1)S(1)} %get-tuple-element.68.after_ref), channel_id=1, source_target_pairs={{0,4},{4,0},{8,12},{12,8},{16,20},{20,16},{24,28},{28,24},{1,5},{5... | collective-permute-start | bytes 196616 | tf_op jit(solution)/shard_map/ppermute | solution.py:33
  38.5 6.1 %collective-permute-start.17 = (bf16[1,128,128]{2,1,0:T(8,128)(2,1)S(1)}, bf16[1,128,128]{2,1,0:T(8,128)(2,1)S(1)}, u32[]{:S(2)}, u32[]{:S(2)}) collective-permute-start(bf16[1,128,128]{2,1,0:T(8,128)(2,1)S(1)} %get-tuple-element.79), channel_id=1, source_target_pairs={{0,16},{4,20},{8,24},{12,28},{16,0},{20,4},{24,8},{28,12},{1,17},{... | collective-permute-start | bytes 98312 | tf_op jit(solution)/shard_map/ppermute | solution.py:33
  41.1 7.2 %collective-permute-start.14 = (bf16[5,128,128]{2,1,0:T(8,128)(2,1)S(1)}, bf16[5,128,128]{2,1,0:T(8,128)(2,1)S(1)}, u32[]{:S(2)}, u32[]{:S(2)}) collective-permute-start(bf16[5,128,128]{2,1,0:T(8,128)(2,1)S(1)} %get-tuple-element.75.refs_0_), channel_id=1, source_target_pairs={{0,4},{4,0},{8,12},{12,8},{16,20},{20,16},{24,28},{28,24},{1,5},{5... | collective-permute-start | bytes 491528 | tf_op jit(solution)/shard_map/ppermute | solution.py:33
  42.2 5.2 %collective-permute-start.16 = (bf16[1,128,128]{2,1,0:T(8,128)(2,1)S(1)}, bf16[1,128,128]{2,1,0:T(8,128)(2,1)S(1)}, u32[]{:S(2)}, u32[]{:S(2)}) collective-permute-start(bf16[1,128,128]{2,1,0:T(8,128)(2,1)S(1)} %get-tuple-element.76), channel_id=1, source_target_pairs={{0,12},{4,8},{8,4},{12,0},{16,28},{20,24},{24,20},{28,16},{1,13},{... | collective-permute-start | bytes 98312 | tf_op jit(solution)/shard_map/ppermute | solution.py:33
  44.2 4.2 %collective-permute-start.15 = (bf16[1,128,128]{2,1,0:T(8,128)(2,1)S(1)}, bf16[1,128,128]{2,1,0:T(8,128)(2,1)S(1)}, u32[]{:S(2)}, u32[]{:S(2)}) collective-permute-start(bf16[1,128,128]{2,1,0:T(8,128)(2,1)S(1)} %get-tuple-element.76), channel_id=1, source_target_pairs={{0,8},{4,12},{8,0},{12,4},{16,24},{20,28},{24,16},{28,20},{1,9},{5... | collective-permute-start | bytes 98312 | tf_op jit(solution)/shard_map/ppermute | solution.py:33
  44.6 6.3 %collective-permute-start.20 = (bf16[1,128,128]{2,1,0:T(8,128)(2,1)S(1)}, bf16[1,128,128]{2,1,0:T(8,128)(2,1)S(1)}, u32[]{:S(2)}, u32[]{:S(2)}) collective-permute-start(bf16[1,128,128]{2,1,0:T(8,128)(2,1)S(1)} %shard_map.96.refs_0_), channel_id=1, source_target_pairs={{0,12},{4,8},{8,4},{12,0},{16,28},{20,24},{24,20},{28,16},{1,13},{... | collective-permute-start | bytes 98312 | tf_op jit(solution)/shard_map/ppermute | solution.py:33
  46.7 4.3 %collective-permute-start.19 = (bf16[1,128,128]{2,1,0:T(8,128)(2,1)S(1)}, bf16[1,128,128]{2,1,0:T(8,128)(2,1)S(1)}, u32[]{:S(2)}, u32[]{:S(2)}) collective-permute-start(bf16[1,128,128]{2,1,0:T(8,128)(2,1)S(1)} %shard_map.96.refs_0_), channel_id=1, source_target_pairs={{0,8},{4,12},{8,0},{12,4},{16,24},{20,28},{24,16},{28,20},{1,9},{5... | collective-permute-start | bytes 98312 | tf_op jit(solution)/shard_map/ppermute | solution.py:33
  47.4 3.9 %collective-permute-start.18 = (bf16[1,128,128]{2,1,0:T(8,128)(2,1)S(1)}, bf16[1,128,128]{2,1,0:T(8,128)(2,1)S(1)}, u32[]{:S(2)}, u32[]{:S(2)}) collective-permute-start(bf16[1,128,128]{2,1,0:T(8,128)(2,1)S(1)} %shard_map.96.refs_0_), channel_id=1, source_target_pairs={{0,4},{4,0},{8,12},{12,8},{16,20},{20,16},{24,28},{28,24},{1,5},{5... | collective-permute-start | bytes 98312 | tf_op jit(solution)/shard_map/ppermute | solution.py:33

commit v4 on v3

--- a/solution.py
+++ b/solution.py
@@ -357,7 +357,7 @@
                 return [pair_block(*sums[h : h + 2]) for h in range(0, heads, 2)]
 
             rows_of = (q_refs, [g_ref] * chunks, v_refs, k_refs)
-            write_side(spans, side, True, weight_of, rows_of, part_refs, outs, held, sems)
+            write_side(spans, side, False, weight_of, rows_of, part_refs, outs, held, sems)
 
 
 def exchange(totals, sends, local, late):

time: 54 us -> 53.9 us (level)
  no operation moved by 1% of the time
where the time goes in v4:
time: 53.9 us; the launch traced here: 53.7 us
  Pallas kernels  26.5 us (49%)
  starting transfers between devices  21.9 us (41%)
  waiting for transfers between devices  4.32 us (8%)
  between operations  0.99 us (2%)
    pallas_call x17, Pallas kernels, call(): pl.pallas_call(kernel, out_shape=outs, in_specs=specs, out_specs=[VMEM] *...  26.5 us
    ppermute x21, starting transfers between devices, swap(): return lax.ppermute(value, axis, pairs)  21.9 us
    ppermute x21, waiting for transfers between devices, swap(): return lax.ppermute(value, axis, pairs)  4.32 us
  transfers between devices with their start and end apart: 21, of which 9 were waited for; matrix products, arithmetic and copies ran while one was open for 0% of the time, Pallas kernels for 43%

profile of v4, /device:TPU:0, one launch (start us, length us, event | category | flops | bytes accessed | tf_op | source)
XLA Modules:
  0.0 53.7 jit_solution(12658001524461499273)
XLA Ops:
  0.6 0.5 collective-permute-start
  1.1 0.9 %shard_map.75.refs_0_ = bf16[160,512]{1,0:T(8,128)(2,1)S(1)} custom-call(bf16[1024,512]{1,0:T(8,128)(2,1)} %x_ref.3), custom_call_target="tpu_custom_call" | custom-call | bytes 2097152 | tf_op jit(solution)/shard_map/pallas_call | solution.py:41
  2.1 2.6 %collective-permute-start.5 = (bf16[160,512]{1,0:T(8,128)(2,1)S(1)}, bf16[160,512]{1,0:T(8,128)(2,1)S(1)}, u32[]{:S(2)}, u32[]{:S(2)}) collective-permute-start(bf16[160,512]{1,0:T(8,128)(2,1)S(1)} %shard_map.75.refs_0_), channel_id=1, source_target_pairs={{0,2},{1,3},{2,0},{3,1},{4,6},{5,7},{6,4},{7,5},{8,10},{9,11},{10,... | collective-permute-start | bytes 491528 | tf_op jit(solution)/shard_map/ppermute | solution.py:33
  4.7 1.3 %shard_map.76 = (bf16[192,512]{1,0:T(8,128)(2,1)S(1)}, bf16[208,512]{1,0:T(8,128)(2,1)S(1)}, bf16[224,512]{1,0:T(8,128)(2,1)S(1)}, bf16[240,512]{1,0:T(8,128)(2,1)S(1)}) custom-call(bf16[1024,512]{1,0:T(8,128)(2,1)} %x_ref.3, bf16[160,512]{1,0:T(8,128)(2,1)S(1)} %shard_map.75.refs_0_), custom_call_target="tpu_custom_call" | custom-call | bytes 2097152 | tf_op jit(solution)/shard_map/pallas_call | solution.py:41
  6.0 0.1 collective-permute-start.4
  6.1 3.2 %shard_map.77 = (bf16[1024,512]{1,0:T(8,128)(2,1)S(1)}, bf16[2048,1536]{1,0:T(8,128)(2,1)S(1)}) custom-call(bf16[1024,512]{1,0:T(8,128)(2,1)} %g_ref.1, bf16[3,2048,512]{2,1,0:T(8,128)(2,1)} %w_ref.1, bf16[192,512]{1,0:T(8,128)(2,1)S(1)} %get-tuple-element.44.after_ref.refs_0_), custom_call_target="tpu_custom_call" | custom-call | bytes 14680064 | tf_op jit(solution)/shard_map/pallas_call | solution.py:41
  9.3 0.5 collective-permute-done.5.value_ref
  9.7 0.0 collective-permute-start.6
  9.7 1.9 %collective-permute-start.3 = (bf16[208,512]{1,0:T(8,128)(2,1)S(1)}, bf16[208,512]{1,0:T(8,128)(2,1)S(1)}, u32[]{:S(2)}, u32[]{:S(2)}) collective-permute-start(bf16[208,512]{1,0:T(8,128)(2,1)S(1)} %get-tuple-element.49.refs_0_), channel_id=1, source_target_pairs={{0,2},{1,3},{2,0},{3,1},{4,6},{5,7},{6,4},{7,5},{8,10},{9,11},{10,... | collective-permute-start | bytes 638984 | tf_op jit(solution)/shard_map/ppermute | solution.py:33
  11.7 1.5 %shard_map.79 = (bf16[160,512]{1,0:T(8,128)(2,1)S(1)}, bf16[160,512]{1,0:T(8,128)(2,1)S(1)}, bf16[160,512]{1,0:T(8,128)(2,1)S(1)}, f32[2,4,128,128]{3,2,1,0:T(8,128)S(1)}) custom-call(bf16[2048,1536]{1,0:T(8,128)(2,1)S(1)} %get-tuple-element.46.refs_0_.w_ref, bf16[1024,512]{1,0:T(8,128)(2,1)S(1)} %get-tuple-element.45.g_ref, ...), custom_call_target="tpu_custom_call" | custom-call | tf_op jit(solution)/shard_map/pallas_call | solution.py:41
  13.2 0.8 %collective-permute-done.4.value_ref = bf16[192,512]{1,0:T(8,128)(2,1)S(1)} collective-permute-done((bf16[192,512]{1,0:T(8,128)(2,1)S(1)}, bf16[192,512]{1,0:T(8,128)(2,1)S(1)}, u32[]{:S(2)}, u32[]{:S(2)}) %collective-permute-start.4) | collective-permute-done | bytes 196640 | tf_op jit(solution)/shard_map/ppermute | solution.py:33
  13.9 0.0 collective-permute-start.7
  13.9 1.9 %collective-permute-start.2 = (bf16[224,512]{1,0:T(8,128)(2,1)S(1)}, bf16[224,512]{1,0:T(8,128)(2,1)S(1)}, u32[]{:S(2)}, u32[]{:S(2)}) collective-permute-start(bf16[224,512]{1,0:T(8,128)(2,1)S(1)} %get-tuple-element.48.refs_0_), channel_id=1, source_target_pairs={{0,2},{1,3},{2,0},{3,1},{4,6},{5,7},{6,4},{7,5},{8,10},{9,11},{10,... | collective-permute-start | bytes 688136 | tf_op jit(solution)/shard_map/ppermute | solution.py:33
  15.9 1.3 %shard_map.81.refs_4_.refs_24_.refs_19_ = f32[4,160,512]{2,1,0:T(8,128)S(1)} custom-call(f32[4,4]{1,0:T(4,128)S(1)} %copy-done, bf16[160,512]{1,0:T(8,128)(2,1)S(1)} %get-tuple-element.51.q_ref.refs_4_, bf16[160,512]{1,0:T(8,128)(2,1)S(1)} %get-tuple-element.52.k_ref.refs_9_, bf16[160,512]{1,0:T(8,128)(2,1)S(1)} %get-tuple-element.53.v_ref.refs_14_, ...), custom_call_target="tpu_custom_call" | custom-call | tf_op jit(solution)/shard_map/pallas_call | solution.py:41
  17.2 0.0 collective-permute-done.7.refs_3_
  17.2 1.7 %shard_map.82 = (bf16[192,512]{1,0:T(8,128)(2,1)S(1)}, bf16[192,512]{1,0:T(8,128)(2,1)S(1)}, bf16[192,512]{1,0:T(8,128)(2,1)S(1)}, f32[2,4,128,128]{3,2,1,0:T(8,128)S(1)}) custom-call(bf16[2048,1536]{1,0:T(8,128)(2,1)S(1)} %get-tuple-element.46.refs_0_.w_ref, bf16[1024,512]{1,0:T(8,128)(2,1)S(1)} %get-tuple-element.45.g_ref, ...), custom_call_target="tpu_custom_call" | custom-call | tf_op jit(solution)/shard_map/pallas_call | solution.py:41
  18.9 0.0 collective-permute-done.3.value_ref
  18.9 0.3 collective-permute-start.8
  19.2 1.3 %collective-permute-start.1 = (bf16[240,512]{1,0:T(8,128)(2,1)S(1)}, bf16[240,512]{1,0:T(8,128)(2,1)S(1)}, u32[]{:S(2)}, u32[]{:S(2)}) collective-permute-start(bf16[240,512]{1,0:T(8,128)(2,1)S(1)} %get-tuple-element.47.refs_0_), channel_id=1, source_target_pairs={{0,2},{1,3},{2,0},{3,1},{4,6},{5,7},{6,4},{7,5},{8,10},{9,11},{10,... | collective-permute-start | bytes 737288 | tf_op jit(solution)/shard_map/ppermute | solution.py:33
  20.5 1.4 %shard_map.84.refs_4_.refs_25_.refs_20_ = f32[4,192,512]{2,1,0:T(8,128)S(1)} custom-call(f32[4,4]{1,0:T(4,128)S(1)} %copy-done, bf16[192,512]{1,0:T(8,128)(2,1)S(1)} %get-tuple-element.55.q_ref.refs_5_, bf16[192,512]{1,0:T(8,128)(2,1)S(1)} %get-tuple-element.56.k_ref.refs_10_, bf16[192,512]{1,0:T(8,128)(2,1)S(1)} %get-tuple-element.57.v_ref.refs_15_, ...), custom_call_target="tpu_custom_call" | custom-call | tf_op jit(solution)/shard_map/pallas_call | solution.py:41
  21.8 1.8 %shard_map.85 = (bf16[208,512]{1,0:T(8,128)(2,1)S(1)}, bf16[208,512]{1,0:T(8,128)(2,1)S(1)}, bf16[208,512]{1,0:T(8,128)(2,1)S(1)}, f32[2,4,128,128]{3,2,1,0:T(8,128)S(1)}) custom-call(bf16[2048,1536]{1,0:T(8,128)(2,1)S(1)} %get-tuple-element.46.refs_0_.w_ref, bf16[1024,512]{1,0:T(8,128)(2,1)S(1)} %get-tuple-element.45.g_ref, ...), custom_call_target="tpu_custom_call" | custom-call | tf_op jit(solution)/shard_map/pallas_call | solution.py:41
  23.6 0.3 collective-permute-start.9
  23.9 1.4 %shard_map.87.refs_4_.refs_26_.refs_21_ = f32[4,208,512]{2,1,0:T(8,128)S(1)} custom-call(f32[4,4]{1,0:T(4,128)S(1)} %copy-done, bf16[208,512]{1,0:T(8,128)(2,1)S(1)} %get-tuple-element.59.q_ref.refs_6_, bf16[208,512]{1,0:T(8,128)(2,1)S(1)} %get-tuple-element.60.k_ref.refs_11_, bf16[208,512]{1,0:T(8,128)(2,1)S(1)} %get-tuple-element.61.v_ref.refs_16_, ...), custom_call_target="tpu_custom_call" | custom-call | tf_op jit(solution)/shard_map/pallas_call | solution.py:41
  25.4 1.9 %shard_map.88 = (bf16[224,512]{1,0:T(8,128)(2,1)S(1)}, bf16[224,512]{1,0:T(8,128)(2,1)S(1)}, bf16[224,512]{1,0:T(8,128)(2,1)S(1)}, f32[2,4,128,128]{3,2,1,0:T(8,128)S(1)}) custom-call(bf16[2048,1536]{1,0:T(8,128)(2,1)S(1)} %get-tuple-element.46.refs_0_.w_ref, bf16[1024,512]{1,0:T(8,128)(2,1)S(1)} %get-tuple-element.45.g_ref, ...), custom_call_target="tpu_custom_call" | custom-call | tf_op jit(solution)/shard_map/pallas_call | solution.py:41
  27.2 1.3 %collective-permute-done.1.value_ref = bf16[240,512]{1,0:T(8,128)(2,1)S(1)} collective-permute-done((bf16[240,512]{1,0:T(8,128)(2,1)S(1)}, bf16[240,512]{1,0:T(8,128)(2,1)S(1)}, u32[]{:S(2)}, u32[]{:S(2)}) %collective-permute-start.1) | collective-permute-done | bytes 245792 | tf_op jit(solution)/shard_map/ppermute | solution.py:33
  28.5 1.4 %shard_map.90 = (f32[240,1536]{1,0:T(8,128)S(1)}, f32[2,4,128,128]{3,2,1,0:T(8,128)S(1)}) custom-call(bf16[2048,1536]{1,0:T(8,128)(2,1)S(1)} %get-tuple-element.46.refs_0_.w_ref, bf16[240,512]{1,0:T(8,128)(2,1)S(1)} %get-tuple-element.47.refs_0_, bf16[1024,512]{1,0:T(8,128)(2,1)S(1)} %collective-permute-done.refs_1_, ...), custom_call_target="tpu_custom_call" | custom-call | tf_op jit(solution)/shard_map/pallas_call | solution.py:41
  30.0 0.1 collective-permute-done.10.late_ref
  30.0 0.9 %shard_map.91 = (bf16[240,512]{1,0:T(8,128)(2,1)S(1)}, bf16[240,512]{1,0:T(8,128)(2,1)S(1)}, bf16[240,512]{1,0:T(8,128)(2,1)S(1)}, f32[2,4,128,128]{3,2,1,0:T(8,...) custom-call(bf16[2048,1536]{1,0:T(8,128)(2,1)S(1)} %get-tuple-elemen, ...), custom_call_target="tpu_custom_call" | custom-call | tf_op jit(solution)/shard_map/pallas_call | solution.py:41
  30.9 2.8 %collective-permute-start.11 = (bf16[2,1,128,128]{3,2,1,0:T(8,128)(2,1)S(1)}, bf16[2,1,128,128]{3,2,1,0:T(8,128)(2,1)S(1)}, u32[]{:S(2)}, u32[]{:S(2)}) collective-permute-start(bf16[2,1,128,128]{3,2,1,0:T(8,128)(2,1)S(1)} %get-tuple-element.66), channel_id=1, source_target_pairs={{0,12},{4,8},{8,4},{12,0},{16,28},{20,24},{24,20},{28,16},{1,13},{... | collective-permute-start | bytes 196616 | tf_op jit(solution)/shard_map/ppermute | solution.py:33
  33.7 0.5 collective-permute-start.12
  34.1 0.3 collective-permute-start.13
  34.5 1.5 %shard_map.93.refs_4_.refs_28_.refs_23_ = f32[4,240,512]{2,1,0:T(8,128)S(1)} custom-call(f32[4,4]{1,0:T(4,128)S(1)} %copy-done, bf16[240,512]{1,0:T(8,128)(2,1)S(1)} %get-tuple-element.72.q_ref.refs_8_, bf16[240,512]{1,0:T(8,128)(2,1)S(1)} %get-tuple-element.73.k_ref.refs_13_, bf16[240,512]{1,0:T(8,128)(2,1)S(1)} %get-tuple-element.74.v_ref.refs_18_, ...), custom_call_target="tpu_custom_call" | custom-call | flops 2949120000 | tf_op jit(solution)/shard_map/pallas_call | solution.py:41
  36.0 1.5 %shard_map.92.refs_3_.refs_27_.refs_22_ = f32[4,224,512]{2,1,0:T(8,128)S(1)} custom-call(f32[4,4]{1,0:T(4,128)S(1)} %copy-done, bf16[224,512]{1,0:T(8,128)(2,1)S(1)} %get-tuple-element.69.q_ref.refs_7_, bf16[224,512]{1,0:T(8,128)(2,1)S(1)} %get-tuple-element.70.k_ref.refs_12_, bf16[224,512]{1,0:T(8,128)(2,1)S(1)} %get-tuple-element.71.v_ref.refs_17_, ...), custom_call_target="tpu_custom_call" | custom-call | flops 2569011200 | tf_op jit(solution)/shard_map/pallas_call | solution.py:41
  37.5 0.5 collective-permute-done.12.refs_1_
  38.0 0.4 collective-permute-done.13.refs_2_
  38.4 0.1 shard_map.94
  38.5 2.7 %collective-permute-start.17 = (bf16[1,128,128]{2,1,0:T(8,128)(2,1)S(1)}, bf16[1,128,128]{2,1,0:T(8,128)(2,1)S(1)}, u32[]{:S(2)}, u32[]{:S(2)}) collective-permute-start(bf16[1,128,128]{2,1,0:T(8,128)(2,1)S(1)} %get-tuple-element.79), channel_id=1, source_target_pairs={{0,16},{4,20},{8,24},{12,28},{16,0},{20,4},{24,8},{28,12},{1,17},{... | collective-permute-start | bytes 98312 | tf_op jit(solution)/shard_map/ppermute | solution.py:33
  41.1 1.0 %collective-permute-start.14 = (bf16[5,128,128]{2,1,0:T(8,128)(2,1)S(1)}, bf16[5,128,128]{2,1,0:T(8,128)(2,1)S(1)}, u32[]{:S(2)}, u32[]{:S(2)}) collective-permute-start(bf16[5,128,128]{2,1,0:T(8,128)(2,1)S(1)} %get-tuple-element.75.refs_0_), channel_id=1, source_target_pairs={{0,4},{4,0},{8,12},{12,8},{16,20},{20,16},{24,28},{28,24},{1,5},{5... | collective-permute-start | bytes 491528 | tf_op jit(solution)/shard_map/ppermute | solution.py:33
  42.2 2.0 %collective-permute-start.16 = (bf16[1,128,128]{2,1,0:T(8,128)(2,1)S(1)}, bf16[1,128,128]{2,1,0:T(8,128)(2,1)S(1)}, u32[]{:S(2)}, u32[]{:S(2)}) collective-permute-start(bf16[1,128,128]{2,1,0:T(8,128)(2,1)S(1)} %get-tuple-element.76), channel_id=1, source_target_pairs={{0,12},{4,8},{8,4},{12,0},{16,28},{20,24},{24,20},{28,16},{1,13},{... | collective-permute-start | bytes 98312 | tf_op jit(solution)/shard_map/ppermute | solution.py:33
  44.2 0.4 collective-permute-start.15
  44.6 2.1 %collective-permute-start.20 = (bf16[1,128,128]{2,1,0:T(8,128)(2,1)S(1)}, bf16[1,128,128]{2,1,0:T(8,128)(2,1)S(1)}, u32[]{:S(2)}, u32[]{:S(2)}) collective-permute-start(bf16[1,128,128]{2,1,0:T(8,128)(2,1)S(1)} %shard_map.96.refs_0_), channel_id=1, source_target_pairs={{0,12},{4,8},{8,4},{12,0},{16,28},{20,24},{24,20},{28,16},{1,13},{... | collective-permute-start | bytes 98312 | tf_op jit(solution)/shard_map/ppermute | solution.py:33
  46.7 0.4 collective-permute-start.19
  47.1 0.2 collective-permute-done.16.refs_3_
  47.4 0.8 %collective-permute-start.18 = (bf16[1,128,128]{2,1,0:T(8,128)(2,1)S(1)}, bf16[1,128,128]{2,1,0:T(8,128)(2,1)S(1)}, u32[]{:S(2)}, u32[]{:S(2)}) collective-permute-start(bf16[1,128,128]{2,1,0:T(8,128)(2,1)S(1)} %shard_map.96.refs_0_), channel_id=1, source_target_pairs={{0,4},{4,0},{8,12},{12,8},{16,20},{20,16},{24,28},{28,24},{1,5},{5... | collective-permute-start | bytes 98312 | tf_op jit(solution)/shard_map/ppermute | solution.py:33
  48.1 0.3 collective-permute-done.15.refs_2_
  48.4 2.5 %shard_map.95 = (bf16[1024,512]{1,0:T(8,128)(2,1)}, bf16[1024,512]{1,0:T(8,128)(2,1)}, bf16[1024,512]{1,0:T(8,128)(2,1)}, bf16[1024,512]{1,0:T(8,128)(2,1)}, f32[5,4,128,128]{3,2,1,0:T(8,128)S(1)}) custom-call(f32[4,4]{1,0:T(4,128)S(1)} %copy-done, bf16[1024,512]{1,0:T(8,128)(2,1)S(1)} %get-tuple-element.45.g_ref, ...), custom_call_target="tpu_custom_call" | custom-call | tf_op jit(solution)/shard_map/pallas_call | solution.py:41
  50.9 0.3 collective-permute-done.18.refs_1_
  51.3 2.3 %shard_map.97 = (bf16[1024,512]{1,0:T(8,128)(2,1)}, bf16[1024,512]{1,0:T(8,128)(2,1)}, bf16[1024,512]{1,0:T(8,128)(2,1)}, bf16[1024,512]{1,0:T(8,128)(2,1)}) custom-call(f32[4,4]{1,0:T(4,128)S(1)} %copy-done, bf16[1024,512]{1,0:T(8,128)(2,1)S(1)} %get-tuple-element.45.g_ref, ...), custom_call_target="tpu_custom_call", output_to_operand_aliasing={{0}: (27, {}), {1}: (28, {}), {2}: (29, {}), {3}: (30, {})} | custom-call | tf_op jit(solution)/shard_map/pallas_call | solution.py:41
  (19 shorter events, 0.0 us)
Async XLA Ops:
  0.6 11.1 %collective-permute-start = (bf16[1024,512]{1,0:T(8,128)(2,1)}, bf16[1024,512]{1,0:T(8,128)(2,1)S(1)}, u32[]{:S(2)}, u32[]{:S(2)}) collective-permute-start(bf16[1024,512]{1,0:T(8,128)(2,1)} %x_ref.3), channel_id=1, source_target_pairs={{0,1},{1,0},{2,3},{3,2},{4,5},{5,4},{6,7},{7,6},{8,9},{9,8},{10,11... | collective-permute-start | bytes 3145736 | tf_op jit(solution)/shard_map/ppermute | solution.py:33
  2.1 7.6 %collective-permute-start.5 = (bf16[160,512]{1,0:T(8,128)(2,1)S(1)}, bf16[160,512]{1,0:T(8,128)(2,1)S(1)}, u32[]{:S(2)}, u32[]{:S(2)}) collective-permute-start(bf16[160,512]{1,0:T(8,128)(2,1)S(1)} %shard_map.75.refs_0_), channel_id=1, source_target_pairs={{0,2},{1,3},{2,0},{3,1},{4,6},{5,7},{6,4},{7,5},{8,10},{9,11},{10,... | collective-permute-start | bytes 491528 | tf_op jit(solution)/shard_map/ppermute | solution.py:33
  6.0 8.0 %collective-permute-start.4 = (bf16[192,512]{1,0:T(8,128)(2,1)S(1)}, bf16[192,512]{1,0:T(8,128)(2,1)S(1)}, u32[]{:S(2)}, u32[]{:S(2)}) collective-permute-start(bf16[192,512]{1,0:T(8,128)(2,1)S(1)} %get-tuple-element.44.after_ref.refs_0_), channel_id=1, source_target_pairs={{0,2},{1,3},{2,0},{3,1},{4,6},{5,7},{6,4},{7,5},{8,10},{9,11},{10,... | collective-permute-start | bytes 589832 | tf_op jit(solution)/shard_map/ppermute | solution.py:33
  9.7 2.0 %collective-permute-start.6 = (bf16[160,512]{1,0:T(8,128)(2,1)S(1)}, bf16[160,512]{1,0:T(8,128)(2,1)S(1)}, u32[]{:S(2)}, u32[]{:S(2)}) collective-permute-start(bf16[160,512]{1,0:T(8,128)(2,1)S(1)} %shard_map.78.refs_2_), channel_id=1, source_target_pairs={{0,1},{1,0},{2,3},{3,2},{4,5},{5,4},{6,7},{7,6},{8,9},{9,8},{10,11... | collective-permute-start | bytes 491528 | tf_op jit(solution)/shard_map/ppermute | solution.py:33
  9.7 9.2 %collective-permute-start.3 = (bf16[208,512]{1,0:T(8,128)(2,1)S(1)}, bf16[208,512]{1,0:T(8,128)(2,1)S(1)}, u32[]{:S(2)}, u32[]{:S(2)}) collective-permute-start(bf16[208,512]{1,0:T(8,128)(2,1)S(1)} %get-tuple-element.49.refs_0_), channel_id=1, source_target_pairs={{0,2},{1,3},{2,0},{3,1},{4,6},{5,7},{6,4},{7,5},{8,10},{9,11},{10,... | collective-permute-start | bytes 638984 | tf_op jit(solution)/shard_map/ppermute | solution.py:33
  11.7 4.2 %copy-start = (f32[4,4]{1,0:T(4,128)S(1)}, f32[4,4]{1,0:T(4,128)}, u32[]{:S(2)}) copy-start(f32[4,4]{1,0:T(4,128)} %weight_ref.13) | copy-start | bytes 196
  13.9 3.2 %collective-permute-start.7 = (bf16[192,512]{1,0:T(8,128)(2,1)S(1)}, bf16[192,512]{1,0:T(8,128)(2,1)S(1)}, u32[]{:S(2)}, u32[]{:S(2)}) collective-permute-start(bf16[192,512]{1,0:T(8,128)(2,1)S(1)} %shard_map.80.after_ref.refs_2_), channel_id=1, source_target_pairs={{0,1},{1,0},{2,3},{3,2},{4,5},{5,4},{6,7},{7,6},{8,9},{9,8},{10,11... | collective-permute-start | bytes 589832 | tf_op jit(solution)/shard_map/ppermute | solution.py:33
  13.9 9.7 %collective-permute-start.2 = (bf16[224,512]{1,0:T(8,128)(2,1)S(1)}, bf16[224,512]{1,0:T(8,128)(2,1)S(1)}, u32[]{:S(2)}, u32[]{:S(2)}) collective-permute-start(bf16[224,512]{1,0:T(8,128)(2,1)S(1)} %get-tuple-element.48.refs_0_), channel_id=1, source_target_pairs={{0,2},{1,3},{2,0},{3,1},{4,6},{5,7},{6,4},{7,5},{8,10},{9,11},{10,... | collective-permute-start | bytes 688136 | tf_op jit(solution)/shard_map/ppermute | solution.py:33
  18.9 2.9 %collective-permute-start.8 = (bf16[208,512]{1,0:T(8,128)(2,1)S(1)}, bf16[208,512]{1,0:T(8,128)(2,1)S(1)}, u32[]{:S(2)}, u32[]{:S(2)}) collective-permute-start(bf16[208,512]{1,0:T(8,128)(2,1)S(1)} %shard_map.83.after_ref.refs_2_), channel_id=1, source_target_pairs={{0,1},{1,0},{2,3},{3,2},{4,5},{5,4},{6,7},{7,6},{8,9},{9,8},{10,11... | collective-permute-start | bytes 638984 | tf_op jit(solution)/shard_map/ppermute | solution.py:33
  19.2 9.3 %collective-permute-start.1 = (bf16[240,512]{1,0:T(8,128)(2,1)S(1)}, bf16[240,512]{1,0:T(8,128)(2,1)S(1)}, u32[]{:S(2)}, u32[]{:S(2)}) collective-permute-start(bf16[240,512]{1,0:T(8,128)(2,1)S(1)} %get-tuple-element.47.refs_0_), channel_id=1, source_target_pairs={{0,2},{1,3},{2,0},{3,1},{4,6},{5,7},{6,4},{7,5},{8,10},{9,11},{10,... | collective-permute-start | bytes 737288 | tf_op jit(solution)/shard_map/ppermute | solution.py:33
  23.6 1.7 %collective-permute-start.9 = (bf16[224,512]{1,0:T(8,128)(2,1)S(1)}, bf16[224,512]{1,0:T(8,128)(2,1)S(1)}, u32[]{:S(2)}, u32[]{:S(2)}) collective-permute-start(bf16[224,512]{1,0:T(8,128)(2,1)S(1)} %shard_map.86.after_ref.refs_2_), channel_id=1, source_target_pairs={{0,1},{1,0},{2,3},{3,2},{4,5},{5,4},{6,7},{7,6},{8,9},{9,8},{10,11... | collective-permute-start | bytes 688136 | tf_op jit(solution)/shard_map/ppermute | solution.py:33
  28.5 1.5 %collective-permute-start.10 = (bf16[240,512]{1,0:T(8,128)(2,1)S(1)}, bf16[240,512]{1,0:T(8,128)(2,1)S(1)}, u32[]{:S(2)}, u32[]{:S(2)}) collective-permute-start(bf16[240,512]{1,0:T(8,128)(2,1)S(1)} %shard_map.89.refs_2_), channel_id=1, source_target_pairs={{0,1},{1,0},{2,3},{3,2},{4,5},{5,4},{6,7},{7,6},{8,9},{9,8},{10,11... | collective-permute-start | bytes 737288 | tf_op jit(solution)/shard_map/ppermute | solution.py:33
  30.9 6.6 %collective-permute-start.11 = (bf16[2,1,128,128]{3,2,1,0:T(8,128)(2,1)S(1)}, bf16[2,1,128,128]{3,2,1,0:T(8,128)(2,1)S(1)}, u32[]{:S(2)}, u32[]{:S(2)}) collective-permute-start(bf16[2,1,128,128]{3,2,1,0:T(8,128)(2,1)S(1)} %get-tuple-element.66), channel_id=1, source_target_pairs={{0,12},{4,8},{8,4},{12,0},{16,28},{20,24},{24,20},{28,16},{1,13},{... | collective-permute-start | bytes 196616 | tf_op jit(solution)/shard_map/ppermute | solution.py:33
  33.7 4.3 %collective-permute-start.12 = (bf16[2,1,128,128]{3,2,1,0:T(8,128)(2,1)S(1)}, bf16[2,1,128,128]{3,2,1,0:T(8,128)(2,1)S(1)}, u32[]{:S(2)}, u32[]{:S(2)}) collective-permute-start(bf16[2,1,128,128]{3,2,1,0:T(8,128)(2,1)S(1)} %get-tuple-element.67), channel_id=1, source_target_pairs={{0,8},{4,12},{8,0},{12,4},{16,24},{20,28},{24,16},{28,20},{1,9},{5... | collective-permute-start | bytes 196616 | tf_op jit(solution)/shard_map/ppermute | solution.py:33
  34.1 4.3 %collective-permute-start.13 = (bf16[2,1,128,128]{3,2,1,0:T(8,128)(2,1)S(1)}, bf16[2,1,128,128]{3,2,1,0:T(8,128)(2,1)S(1)}, u32[]{:S(2)}, u32[]{:S(2)}) collective-permute-start(bf16[2,1,128,128]{3,2,1,0:T(8,128)(2,1)S(1)} %get-tuple-element.68.after_ref), channel_id=1, source_target_pairs={{0,4},{4,0},{8,12},{12,8},{16,20},{20,16},{24,28},{28,24},{1,5},{5... | collective-permute-start | bytes 196616 | tf_op jit(solution)/shard_map/ppermute | solution.py:33
  38.5 6.1 %collective-permute-start.17 = (bf16[1,128,128]{2,1,0:T(8,128)(2,1)S(1)}, bf16[1,128,128]{2,1,0:T(8,128)(2,1)S(1)}, u32[]{:S(2)}, u32[]{:S(2)}) collective-permute-start(bf16[1,128,128]{2,1,0:T(8,128)(2,1)S(1)} %get-tuple-element.79), channel_id=1, source_target_pairs={{0,16},{4,20},{8,24},{12,28},{16,0},{20,4},{24,8},{28,12},{1,17},{... | collective-permute-start | bytes 98312 | tf_op jit(solution)/shard_map/ppermute | solution.py:33
  41.1 7.2 %collective-permute-start.14 = (bf16[5,128,128]{2,1,0:T(8,128)(2,1)S(1)}, bf16[5,128,128]{2,1,0:T(8,128)(2,1)S(1)}, u32[]{:S(2)}, u32[]{:S(2)}) collective-permute-start(bf16[5,128,128]{2,1,0:T(8,128)(2,1)S(1)} %get-tuple-element.75.refs_0_), channel_id=1, source_target_pairs={{0,4},{4,0},{8,12},{12,8},{16,20},{20,16},{24,28},{28,24},{1,5},{5... | collective-permute-start | bytes 491528 | tf_op jit(solution)/shard_map/ppermute | solution.py:33
  42.2 5.2 %collective-permute-start.16 = (bf16[1,128,128]{2,1,0:T(8,128)(2,1)S(1)}, bf16[1,128,128]{2,1,0:T(8,128)(2,1)S(1)}, u32[]{:S(2)}, u32[]{:S(2)}) collective-permute-start(bf16[1,128,128]{2,1,0:T(8,128)(2,1)S(1)} %get-tuple-element.76), channel_id=1, source_target_pairs={{0,12},{4,8},{8,4},{12,0},{16,28},{20,24},{24,20},{28,16},{1,13},{... | collective-permute-start | bytes 98312 | tf_op jit(solution)/shard_map/ppermute | solution.py:33
  44.2 4.2 %collective-permute-start.15 = (bf16[1,128,128]{2,1,0:T(8,128)(2,1)S(1)}, bf16[1,128,128]{2,1,0:T(8,128)(2,1)S(1)}, u32[]{:S(2)}, u32[]{:S(2)}) collective-permute-start(bf16[1,128,128]{2,1,0:T(8,128)(2,1)S(1)} %get-tuple-element.76), channel_id=1, source_target_pairs={{0,8},{4,12},{8,0},{12,4},{16,24},{20,28},{24,16},{28,20},{1,9},{5... | collective-permute-start | bytes 98312 | tf_op jit(solution)/shard_map/ppermute | solution.py:33
  44.6 6.3 %collective-permute-start.20 = (bf16[1,128,128]{2,1,0:T(8,128)(2,1)S(1)}, bf16[1,128,128]{2,1,0:T(8,128)(2,1)S(1)}, u32[]{:S(2)}, u32[]{:S(2)}) collective-permute-start(bf16[1,128,128]{2,1,0:T(8,128)(2,1)S(1)} %shard_map.96.refs_0_), channel_id=1, source_target_pairs={{0,12},{4,8},{8,4},{12,0},{16,28},{20,24},{24,20},{28,16},{1,13},{... | collective-permute-start | bytes 98312 | tf_op jit(solution)/shard_map/ppermute | solution.py:33
  46.7 4.3 %collective-permute-start.19 = (bf16[1,128,128]{2,1,0:T(8,128)(2,1)S(1)}, bf16[1,128,128]{2,1,0:T(8,128)(2,1)S(1)}, u32[]{:S(2)}, u32[]{:S(2)}) collective-permute-start(bf16[1,128,128]{2,1,0:T(8,128)(2,1)S(1)} %shard_map.96.refs_0_), channel_id=1, source_target_pairs={{0,8},{4,12},{8,0},{12,4},{16,24},{20,28},{24,16},{28,20},{1,9},{5... | collective-permute-start | bytes 98312 | tf_op jit(solution)/shard_map/ppermute | solution.py:33
  47.4 3.9 %collective-permute-start.18 = (bf16[1,128,128]{2,1,0:T(8,128)(2,1)S(1)}, bf16[1,128,128]{2,1,0:T(8,128)(2,1)S(1)}, u32[]{:S(2)}, u32[]{:S(2)}) collective-permute-start(bf16[1,128,128]{2,1,0:T(8,128)(2,1)S(1)} %shard_map.96.refs_0_), channel_id=1, source_target_pairs={{0,4},{4,0},{8,12},{12,8},{16,20},{20,16},{24,28},{28,24},{1,5},{5... | collective-permute-start | bytes 98312 | tf_op jit(solution)/shard_map/ppermute | solution.py:33

commit v5 on v4

--- a/solution.py
+++ b/solution.py
@@ -139,6 +139,11 @@
     for state in states[1:]:
         sums = sums + state[...]
     sum_ref[...] = sums
+
+
+def more_kernel(span, start, w_ref, part_ref, *refs):
+    rows = beside(refs[:-1], span)
+    refs[-1][...] = part_ref[...] + dot(rows, w_ref[start : start + rows.shape[1], :])
 
 
 def project_kernel(span, count, heads, w_ref, g_ref, *refs):
@@ -446,13 +451,24 @@
     after = None
     for c in range(CHUNKS):
         pieces = {**whole, 0: mine[c]}
-        pieces[top] = arrived[c] if after is None else tie(arrived[c], after)
+        span = spans[c]
+        chunk = span[1] - span[0]
+        ready = [after] if c else []
+        if c == CHUNKS - 1:
+            near = [pieces[k] for k in sorted(pieces)]
+            begun, before = call(
+                functools.partial(early_kernel, span, len(near)),
+                [pltpu.VMEM((chunk, 3 * width), F32), state],
+                [weights, *near, *states],
+                [VMEM] * (1 + len(near) + len(states)),
+                0,
+            )
+            ready.append(begun)
+        pieces[top] = tie(arrived[c], *ready) if ready else arrived[c]
         for low in lows:
             for k in [k for k in sorted(pieces) if k & top]:
                 pieces[k | low] = swap(pieces[k], "head", low)
         segments = [pieces[k] for k in sorted(pieces)]
-        span = spans[c]
-        chunk = span[1] - span[0]
         flat = pltpu.VMEM((chunk, width), BF16)
         if c < CHUNKS - 1:
             if c > 0:
@@ -466,14 +482,15 @@
                 0,
             )
         else:
-            operands = [weights, *segments[:-1], *states]
-            begun, before = call(
-                functools.partial(early_kernel, span, len(segments) - 1),
-                [pltpu.VMEM((chunk, 3 * width), F32), state],
-                operands,
-                [VMEM] * len(operands),
-                0,
-            )
+            middle = segments[len(near) : -1]
+            if middle:
+                (begun,) = call(
+                    functools.partial(more_kernel, span, len(near) * inputs.shape[1]),
+                    [pltpu.VMEM((chunk, 3 * width), F32)],
+                    [weights, begun, *middle],
+                    [VMEM] * (2 + len(middle)),
+                    0,
+                )
             got = call(
                 functools.partial(last_kernel, span, heads),
                 [

time: 53.9 us -> 53.5 us (level)
  waiting for transfers between devices: 4.32 us -> 3.29 us
    ppermute x21, waiting for transfers between devices: 4.32 us -> 3.29 us  [swap(): return lax.ppermute(value, axis, pairs)]
    pallas_call x17 -> x18, Pallas kernels: 26.5 us -> 26.7 us  [call(): pl.pallas_call(kernel, out_shape=outs, in_specs=specs, out_specs=[VMEM] *...]
  transfers between devices with their start and end apart: 21 -> 21, of which waited for: 9 -> 7; matrix products, arithmetic and copies ran while one was open for 0% -> 0% of each run, Pallas kernels for 43% -> 44%
where the time goes in v5:
time: 53.5 us; the launch traced here: 53.3 us
  Pallas kernels  26.7 us (50%)
  starting transfers between devices  22.3 us (42%)
  waiting for transfers between devices  3.29 us (6%)
  between operations  1 us (2%)
    pallas_call x18, Pallas kernels, call(): pl.pallas_call(kernel, out_shape=outs, in_specs=specs, out_specs=[VMEM] *...  26.7 us
    ppermute x21, starting transfers between devices, swap(): return lax.ppermute(value, axis, pairs)  22.3 us
    ppermute x21, waiting for transfers between devices, swap(): return lax.ppermute(value, axis, pairs)  3.29 us
  transfers between devices with their start and end apart: 21, of which 7 were waited for; matrix products, arithmetic and copies ran while one was open for 0% of the time, Pallas kernels for 44%

profile of v5, /device:TPU:0, one launch (start us, length us, event | category | flops | bytes accessed | tf_op | source)
XLA Modules:
  0.0 53.3 jit_solution(3451155150992756995)
XLA Ops:
  0.6 0.5 collective-permute-start
  1.1 0.9 %shard_map.75.refs_0_ = bf16[160,512]{1,0:T(8,128)(2,1)S(1)} custom-call(bf16[1024,512]{1,0:T(8,128)(2,1)} %x_ref.3), custom_call_target="tpu_custom_call" | custom-call | bytes 2097152 | tf_op jit(solution)/shard_map/pallas_call | solution.py:41
  2.1 2.6 %collective-permute-start.1 = (bf16[160,512]{1,0:T(8,128)(2,1)S(1)}, bf16[160,512]{1,0:T(8,128)(2,1)S(1)}, u32[]{:S(2)}, u32[]{:S(2)}) collective-permute-start(bf16[160,512]{1,0:T(8,128)(2,1)S(1)} %shard_map.75.refs_0_), channel_id=1, source_target_pairs={{0,2},{1,3},{2,0},{3,1},{4,6},{5,7},{6,4},{7,5},{8,10},{9,11},{10,... | collective-permute-start | bytes 491528 | tf_op jit(solution)/shard_map/ppermute | solution.py:33
  4.7 1.3 %shard_map.76 = (bf16[192,512]{1,0:T(8,128)(2,1)S(1)}, bf16[208,512]{1,0:T(8,128)(2,1)S(1)}, bf16[224,512]{1,0:T(8,128)(2,1)S(1)}, bf16[240,512]{1,0:T(8,128)(2,1)S(1)}) custom-call(bf16[1024,512]{1,0:T(8,128)(2,1)} %x_ref.3, bf16[160,512]{1,0:T(8,128)(2,1)S(1)} %shard_map.75.refs_0_), custom_call_target="tpu_custom_call" | custom-call | bytes 2097152 | tf_op jit(solution)/shard_map/pallas_call | solution.py:41
  6.0 0.1 collective-permute-start.3
  6.1 3.2 %shard_map.77 = (bf16[1024,512]{1,0:T(8,128)(2,1)S(1)}, bf16[2048,1536]{1,0:T(8,128)(2,1)S(1)}) custom-call(bf16[1024,512]{1,0:T(8,128)(2,1)} %g_ref.1, bf16[3,2048,512]{2,1,0:T(8,128)(2,1)} %w_ref.1, bf16[192,512]{1,0:T(8,128)(2,1)S(1)} %get-tuple-element.44.after_ref.refs_0_), custom_call_target="tpu_custom_call" | custom-call | bytes 14680064 | tf_op jit(solution)/shard_map/pallas_call | solution.py:41
  9.3 0.5 collective-permute-done.1.value_ref
  9.7 1.9 %collective-permute-start.5 = (bf16[208,512]{1,0:T(8,128)(2,1)S(1)}, bf16[208,512]{1,0:T(8,128)(2,1)S(1)}, u32[]{:S(2)}, u32[]{:S(2)}) collective-permute-start(bf16[208,512]{1,0:T(8,128)(2,1)S(1)} %get-tuple-element.53.refs_0_), channel_id=1, source_target_pairs={{0,2},{1,3},{2,0},{3,1},{4,6},{5,7},{6,4},{7,5},{8,10},{9,11},{10,... | collective-permute-start | bytes 638984 | tf_op jit(solution)/shard_map/ppermute | solution.py:33
  11.7 0.0 collective-permute-done.2.refs_3_
  11.7 0.0 collective-permute-done.refs_1_
  11.7 1.5 %shard_map.79 = (bf16[160,512]{1,0:T(8,128)(2,1)S(1)}, bf16[160,512]{1,0:T(8,128)(2,1)S(1)}, bf16[160,512]{1,0:T(8,128)(2,1)S(1)}, f32[2,4,128,128]{3,2,1,0:T(8,128)S(1)}) custom-call(bf16[2048,1536]{1,0:T(8,128)(2,1)S(1)} %get-tuple-element.46.refs_0_.w_ref, bf16[1024,512]{1,0:T(8,128)(2,1)S(1)} %get-tuple-element.45.g_ref, ...), custom_call_target="tpu_custom_call" | custom-call | tf_op jit(solution)/shard_map/pallas_call | solution.py:41
  13.2 0.8 %collective-permute-done.3.value_ref = bf16[192,512]{1,0:T(8,128)(2,1)S(1)} collective-permute-done((bf16[192,512]{1,0:T(8,128)(2,1)S(1)}, bf16[192,512]{1,0:T(8,128)(2,1)S(1)}, u32[]{:S(2)}, u32[]{:S(2)}) %collective-permute-start.3) | collective-permute-done | bytes 196640 | tf_op jit(solution)/shard_map/ppermute | solution.py:33
  13.9 0.0 collective-permute-start.4
  13.9 1.9 %collective-permute-start.7 = (bf16[224,512]{1,0:T(8,128)(2,1)S(1)}, bf16[224,512]{1,0:T(8,128)(2,1)S(1)}, u32[]{:S(2)}, u32[]{:S(2)}) collective-permute-start(bf16[224,512]{1,0:T(8,128)(2,1)S(1)} %get-tuple-element.58.refs_0_), channel_id=1, source_target_pairs={{0,2},{1,3},{2,0},{3,1},{4,6},{5,7},{6,4},{7,5},{8,10},{9,11},{10,... | collective-permute-start | bytes 688136 | tf_op jit(solution)/shard_map/ppermute | solution.py:33
  15.9 1.3 %shard_map.81.refs_4_.refs_24_.refs_19_ = f32[4,160,512]{2,1,0:T(8,128)S(1)} custom-call(f32[4,4]{1,0:T(4,128)S(1)} %copy-done, bf16[160,512]{1,0:T(8,128)(2,1)S(1)} %get-tuple-element.49.q_ref.refs_4_, bf16[160,512]{1,0:T(8,128)(2,1)S(1)} %get-tuple-element.50.k_ref.refs_9_, bf16[160,512]{1,0:T(8,128)(2,1)S(1)} %get-tuple-element.51.v_ref.refs_14_, ...), custom_call_target="tpu_custom_call" | custom-call | tf_op jit(solution)/shard_map/pallas_call | solution.py:41
  17.2 1.7 %shard_map.82 = (bf16[192,512]{1,0:T(8,128)(2,1)S(1)}, bf16[192,512]{1,0:T(8,128)(2,1)S(1)}, bf16[192,512]{1,0:T(8,128)(2,1)S(1)}, f32[2,4,128,128]{3,2,1,0:T(8,128)S(1)}) custom-call(bf16[2048,1536]{1,0:T(8,128)(2,1)S(1)} %get-tuple-element.46.refs_0_.w_ref, bf16[1024,512]{1,0:T(8,128)(2,1)S(1)} %get-tuple-element.45.g_ref, ...), custom_call_target="tpu_custom_call" | custom-call | tf_op jit(solution)/shard_map/pallas_call | solution.py:41
  18.9 0.0 collective-permute-done.5.value_ref
  18.9 0.3 collective-permute-start.6
  19.2 1.3 %collective-permute-start.9 = (bf16[240,512]{1,0:T(8,128)(2,1)S(1)}, bf16[240,512]{1,0:T(8,128)(2,1)S(1)}, u32[]{:S(2)}, u32[]{:S(2)}) collective-permute-start(bf16[240,512]{1,0:T(8,128)(2,1)S(1)} %get-tuple-element.47.refs_0_), channel_id=1, source_target_pairs={{0,2},{1,3},{2,0},{3,1},{4,6},{5,7},{6,4},{7,5},{8,10},{9,11},{10,... | collective-permute-start | bytes 737288 | tf_op jit(solution)/shard_map/ppermute | solution.py:33
  20.5 1.4 %shard_map.84.refs_4_.refs_25_.refs_20_ = f32[4,192,512]{2,1,0:T(8,128)S(1)} custom-call(f32[4,4]{1,0:T(4,128)S(1)} %copy-done, bf16[192,512]{1,0:T(8,128)(2,1)S(1)} %get-tuple-element.54.q_ref.refs_5_, bf16[192,512]{1,0:T(8,128)(2,1)S(1)} %get-tuple-element.55.k_ref.refs_10_, bf16[192,512]{1,0:T(8,128)(2,1)S(1)} %get-tuple-element.56.v_ref.refs_15_, ...), custom_call_target="tpu_custom_call" | custom-call | tf_op jit(solution)/shard_map/pallas_call | solution.py:41
  21.8 1.8 %shard_map.85 = (bf16[208,512]{1,0:T(8,128)(2,1)S(1)}, bf16[208,512]{1,0:T(8,128)(2,1)S(1)}, bf16[208,512]{1,0:T(8,128)(2,1)S(1)}, f32[2,4,128,128]{3,2,1,0:T(8,128)S(1)}) custom-call(bf16[2048,1536]{1,0:T(8,128)(2,1)S(1)} %get-tuple-element.46.refs_0_.w_ref, bf16[1024,512]{1,0:T(8,128)(2,1)S(1)} %get-tuple-element.45.g_ref, ...), custom_call_target="tpu_custom_call" | custom-call | tf_op jit(solution)/shard_map/pallas_call | solution.py:41
  23.6 0.3 collective-permute-start.8
  23.9 1.4 %shard_map.87.refs_4_.refs_26_.refs_21_ = f32[4,208,512]{2,1,0:T(8,128)S(1)} custom-call(f32[4,4]{1,0:T(4,128)S(1)} %copy-done, bf16[208,512]{1,0:T(8,128)(2,1)S(1)} %get-tuple-element.59.q_ref.refs_6_, bf16[208,512]{1,0:T(8,128)(2,1)S(1)} %get-tuple-element.60.k_ref.refs_11_, bf16[208,512]{1,0:T(8,128)(2,1)S(1)} %get-tuple-element.61.v_ref.refs_16_, ...), custom_call_target="tpu_custom_call" | custom-call | tf_op jit(solution)/shard_map/pallas_call | solution.py:41
  25.4 1.9 %shard_map.88 = (bf16[224,512]{1,0:T(8,128)(2,1)S(1)}, bf16[224,512]{1,0:T(8,128)(2,1)S(1)}, bf16[224,512]{1,0:T(8,128)(2,1)S(1)}, f32[2,4,128,128]{3,2,1,0:T(8,128)S(1)}) custom-call(bf16[2048,1536]{1,0:T(8,128)(2,1)S(1)} %get-tuple-element.46.refs_0_.w_ref, bf16[1024,512]{1,0:T(8,128)(2,1)S(1)} %get-tuple-element.45.g_ref, ...), custom_call_target="tpu_custom_call" | custom-call | tf_op jit(solution)/shard_map/pallas_call | solution.py:41
  27.2 1.0 %shard_map.89 = (f32[240,1536]{1,0:T(8,128)S(1)}, f32[2,4,128,128]{3,2,1,0:T(8,128)S(1)}) custom-call(bf16[2048,1536]{1,0:T(8,128)(2,1)S(1)} %get-tuple-element.46.refs_0_.w_ref, bf16[240,512]{1,0:T(8,128)(2,1)S(1)} %get-tuple-element.47.refs_0_, bf16[1024,512]{1,0:T(8,128)(2,1)S(1)} %collective-permute-done.refs_1_, ...), custom_call_target="tpu_custom_call" | custom-call | tf_op jit(solution)/shard_map/pallas_call | solution.py:41
  28.3 0.2 collective-permute-done.9.value_ref
  28.5 0.2 collective-permute-start.10
  28.7 0.5 %shard_map.91.part_ref = f32[240,1536]{1,0:T(8,128)S(1)} custom-call(bf16[2048,1536]{1,0:T(8,128)(2,1)S(1)} %get-tuple-element.46.refs_0_.w_ref, f32[240,1536]{1,0:T(8,128)S(1)} %get-tuple-element.63.refs_1_.part_ref, bf16[240,512]{1,0:T(8,128)(2,1)S(1)} %shard_map.90.refs_0_), custom_call_target="tpu_custom_call" | custom-call | tf_op jit(solution)/shard_map/pallas_call | solution.py:41
  29.2 0.8 %collective-permute-done.10.late_ref = bf16[240,512]{1,0:T(8,128)(2,1)S(1)} collective-permute-done((bf16[240,512]{1,0:T(8,128)(2,1)S(1)}, bf16[240,512]{1,0:T(8,128)(2,1)S(1)}, u32[]{:S(2)}, u32[]{:S(2)}) %collective-permute-start.10) | collective-permute-done | bytes 245792 | tf_op jit(solution)/shard_map/ppermute | solution.py:33
  30.0 0.9 %shard_map.92 = (bf16[240,512]{1,0:T(8,128)(2,1)S(1)}, bf16[240,512]{1,0:T(8,128)(2,1)S(1)}, bf16[240,512]{1,0:T(8,128)(2,1)S(1)}, f32[2,4,128,128]{3,2,1,0:T(8,...) custom-call(bf16[2048,1536]{1,0:T(8,128)(2,1)S(1)} %get-tuple-elemen, ...), custom_call_target="tpu_custom_call" | custom-call | tf_op jit(solution)/shard_map/pallas_call | solution.py:41
  30.9 2.8 %collective-permute-start.11 = (bf16[2,1,128,128]{3,2,1,0:T(8,128)(2,1)S(1)}, bf16[2,1,128,128]{3,2,1,0:T(8,128)(2,1)S(1)}, u32[]{:S(2)}, u32[]{:S(2)}) collective-permute-start(bf16[2,1,128,128]{3,2,1,0:T(8,128)(2,1)S(1)} %get-tuple-element.66), channel_id=1, source_target_pairs={{0,12},{4,8},{8,4},{12,0},{16,28},{20,24},{24,20},{28,16},{1,13},{... | collective-permute-start | bytes 196616 | tf_op jit(solution)/shard_map/ppermute | solution.py:33
  33.7 0.5 collective-permute-start.12
  34.1 0.3 collective-permute-start.13
  34.4 1.5 %shard_map.94.refs_4_.refs_28_.refs_23_ = f32[4,240,512]{2,1,0:T(8,128)S(1)} custom-call(f32[4,4]{1,0:T(4,128)S(1)} %copy-done, bf16[240,512]{1,0:T(8,128)(2,1)S(1)} %get-tuple-element.72.q_ref.refs_8_, bf16[240,512]{1,0:T(8,128)(2,1)S(1)} %get-tuple-element.73.k_ref.refs_13_, bf16[240,512]{1,0:T(8,128)(2,1)S(1)} %get-tuple-element.74.v_ref.refs_18_, ...), custom_call_target="tpu_custom_call" | custom-call | flops 2949120000 | tf_op jit(solution)/shard_map/pallas_call | solution.py:41
  36.0 1.5 %shard_map.93.refs_3_.refs_27_.refs_22_ = f32[4,224,512]{2,1,0:T(8,128)S(1)} custom-call(f32[4,4]{1,0:T(4,128)S(1)} %copy-done, bf16[224,512]{1,0:T(8,128)(2,1)S(1)} %get-tuple-element.69.q_ref.refs_7_, bf16[224,512]{1,0:T(8,128)(2,1)S(1)} %get-tuple-element.70.k_ref.refs_12_, bf16[224,512]{1,0:T(8,128)(2,1)S(1)} %get-tuple-element.71.v_ref.refs_17_, ...), custom_call_target="tpu_custom_call" | custom-call | flops 2569011200 | tf_op jit(solution)/shard_map/pallas_call | solution.py:41
  37.5 0.5 collective-permute-done.12.refs_1_
  37.9 0.5 collective-permute-done.13.refs_2_
  38.4 0.1 shard_map.95
  38.4 2.7 %collective-permute-start.17 = (bf16[1,128,128]{2,1,0:T(8,128)(2,1)S(1)}, bf16[1,128,128]{2,1,0:T(8,128)(2,1)S(1)}, u32[]{:S(2)}, u32[]{:S(2)}) collective-permute-start(bf16[1,128,128]{2,1,0:T(8,128)(2,1)S(1)} %get-tuple-element.79), channel_id=1, source_target_pairs={{0,16},{4,20},{8,24},{12,28},{16,0},{20,4},{24,8},{28,12},{1,17},{... | collective-permute-start | bytes 98312 | tf_op jit(solution)/shard_map/ppermute | solution.py:33
  41.1 0.8 %collective-permute-start.14 = (bf16[5,128,128]{2,1,0:T(8,128)(2,1)S(1)}, bf16[5,128,128]{2,1,0:T(8,128)(2,1)S(1)}, u32[]{:S(2)}, u32[]{:S(2)}) collective-permute-start(bf16[5,128,128]{2,1,0:T(8,128)(2,1)S(1)} %get-tuple-element.75.refs_0_), channel_id=1, source_target_pairs={{0,4},{4,0},{8,12},{12,8},{16,20},{20,16},{24,28},{28,24},{1,5},{5... | collective-permute-start | bytes 491528 | tf_op jit(solution)/shard_map/ppermute | solution.py:33
  41.9 2.2 %collective-permute-start.16 = (bf16[1,128,128]{2,1,0:T(8,128)(2,1)S(1)}, bf16[1,128,128]{2,1,0:T(8,128)(2,1)S(1)}, u32[]{:S(2)}, u32[]{:S(2)}) collective-permute-start(bf16[1,128,128]{2,1,0:T(8,128)(2,1)S(1)} %get-tuple-element.76), channel_id=1, source_target_pairs={{0,12},{4,8},{8,4},{12,0},{16,28},{20,24},{24,20},{28,16},{1,13},{... | collective-permute-start | bytes 98312 | tf_op jit(solution)/shard_map/ppermute | solution.py:33
  44.1 0.4 collective-permute-start.15
  44.6 1.8 %collective-permute-start.20 = (bf16[1,128,128]{2,1,0:T(8,128)(2,1)S(1)}, bf16[1,128,128]{2,1,0:T(8,128)(2,1)S(1)}, u32[]{:S(2)}, u32[]{:S(2)}) collective-permute-start(bf16[1,128,128]{2,1,0:T(8,128)(2,1)S(1)} %shard_map.97.refs_0_), channel_id=1, source_target_pairs={{0,12},{4,8},{8,4},{12,0},{16,28},{20,24},{24,20},{28,16},{1,13},{... | collective-permute-start | bytes 98312 | tf_op jit(solution)/shard_map/ppermute | solution.py:33
  46.4 0.4 collective-permute-start.19
  46.9 1.2 %collective-permute-start.18 = (bf16[1,128,128]{2,1,0:T(8,128)(2,1)S(1)}, bf16[1,128,128]{2,1,0:T(8,128)(2,1)S(1)}, u32[]{:S(2)}, u32[]{:S(2)}) collective-permute-start(bf16[1,128,128]{2,1,0:T(8,128)(2,1)S(1)} %shard_map.97.refs_0_), channel_id=1, source_target_pairs={{0,4},{4,0},{8,12},{12,8},{16,20},{20,16},{24,28},{28,24},{1,5},{5... | collective-permute-start | bytes 98312 | tf_op jit(solution)/shard_map/ppermute | solution.py:33
  48.1 2.6 %shard_map.96 = (bf16[1024,512]{1,0:T(8,128)(2,1)}, bf16[1024,512]{1,0:T(8,128)(2,1)}, bf16[1024,512]{1,0:T(8,128)(2,1)}, bf16[1024,512]{1,0:T(8,128)(2,1)}, f32[5,4,128,128]{3,2,1,0:T(8,128)S(1)}) custom-call(f32[4,4]{1,0:T(4,128)S(1)} %copy-done, bf16[1024,512]{1,0:T(8,128)(2,1)S(1)} %get-tuple-element.45.g_ref, ...), custom_call_target="tpu_custom_call" | custom-call | tf_op jit(solution)/shard_map/pallas_call | solution.py:41
  50.7 0.1 collective-permute-done.18.refs_1_
  50.8 2.3 %shard_map.98 = (bf16[1024,512]{1,0:T(8,128)(2,1)}, bf16[1024,512]{1,0:T(8,128)(2,1)}, bf16[1024,512]{1,0:T(8,128)(2,1)}, bf16[1024,512]{1,0:T(8,128)(2,1)}) custom-call(f32[4,4]{1,0:T(4,128)S(1)} %copy-done, bf16[1024,512]{1,0:T(8,128)(2,1)S(1)} %get-tuple-element.45.g_ref, ...), custom_call_target="tpu_custom_call", output_to_operand_aliasing={{0}: (27, {}), {1}: (28, {}), {2}: (29, {}), {3}: (30, {})} | custom-call | tf_op jit(solution)/shard_map/pallas_call | solution.py:41
  (20 shorter events, 0.0 us)
Async XLA Ops:
  0.6 11.1 %collective-permute-start = (bf16[1024,512]{1,0:T(8,128)(2,1)}, bf16[1024,512]{1,0:T(8,128)(2,1)S(1)}, u32[]{:S(2)}, u32[]{:S(2)}) collective-permute-start(bf16[1024,512]{1,0:T(8,128)(2,1)} %x_ref.3), channel_id=1, source_target_pairs={{0,1},{1,0},{2,3},{3,2},{4,5},{5,4},{6,7},{7,6},{8,9},{9,8},{10,11... | collective-permute-start | bytes 3145736 | tf_op jit(solution)/shard_map/ppermute | solution.py:33
  2.1 7.6 %collective-permute-start.1 = (bf16[160,512]{1,0:T(8,128)(2,1)S(1)}, bf16[160,512]{1,0:T(8,128)(2,1)S(1)}, u32[]{:S(2)}, u32[]{:S(2)}) collective-permute-start(bf16[160,512]{1,0:T(8,128)(2,1)S(1)} %shard_map.75.refs_0_), channel_id=1, source_target_pairs={{0,2},{1,3},{2,0},{3,1},{4,6},{5,7},{6,4},{7,5},{8,10},{9,11},{10,... | collective-permute-start | bytes 491528 | tf_op jit(solution)/shard_map/ppermute | solution.py:33
  6.0 8.0 %collective-permute-start.3 = (bf16[192,512]{1,0:T(8,128)(2,1)S(1)}, bf16[192,512]{1,0:T(8,128)(2,1)S(1)}, u32[]{:S(2)}, u32[]{:S(2)}) collective-permute-start(bf16[192,512]{1,0:T(8,128)(2,1)S(1)} %get-tuple-element.44.after_ref.refs_0_), channel_id=1, source_target_pairs={{0,2},{1,3},{2,0},{3,1},{4,6},{5,7},{6,4},{7,5},{8,10},{9,11},{10,... | collective-permute-start | bytes 589832 | tf_op jit(solution)/shard_map/ppermute | solution.py:33
  9.7 2.0 %collective-permute-start.2 = (bf16[160,512]{1,0:T(8,128)(2,1)S(1)}, bf16[160,512]{1,0:T(8,128)(2,1)S(1)}, u32[]{:S(2)}, u32[]{:S(2)}) collective-permute-start(bf16[160,512]{1,0:T(8,128)(2,1)S(1)} %shard_map.78.refs_2_), channel_id=1, source_target_pairs={{0,1},{1,0},{2,3},{3,2},{4,5},{5,4},{6,7},{7,6},{8,9},{9,8},{10,11... | collective-permute-start | bytes 491528 | tf_op jit(solution)/shard_map/ppermute | solution.py:33
  9.7 9.1 %collective-permute-start.5 = (bf16[208,512]{1,0:T(8,128)(2,1)S(1)}, bf16[208,512]{1,0:T(8,128)(2,1)S(1)}, u32[]{:S(2)}, u32[]{:S(2)}) collective-permute-start(bf16[208,512]{1,0:T(8,128)(2,1)S(1)} %get-tuple-element.53.refs_0_), channel_id=1, source_target_pairs={{0,2},{1,3},{2,0},{3,1},{4,6},{5,7},{6,4},{7,5},{8,10},{9,11},{10,... | collective-permute-start | bytes 638984 | tf_op jit(solution)/shard_map/ppermute | solution.py:33
  11.7 4.2 %copy-start = (f32[4,4]{1,0:T(4,128)S(1)}, f32[4,4]{1,0:T(4,128)}, u32[]{:S(2)}) copy-start(f32[4,4]{1,0:T(4,128)} %weight_ref.13) | copy-start | bytes 196
  13.9 3.2 %collective-permute-start.4 = (bf16[192,512]{1,0:T(8,128)(2,1)S(1)}, bf16[192,512]{1,0:T(8,128)(2,1)S(1)}, u32[]{:S(2)}, u32[]{:S(2)}) collective-permute-start(bf16[192,512]{1,0:T(8,128)(2,1)S(1)} %shard_map.80.after_ref.refs_2_), channel_id=1, source_target_pairs={{0,1},{1,0},{2,3},{3,2},{4,5},{5,4},{6,7},{7,6},{8,9},{9,8},{10,11... | collective-permute-start | bytes 589832 | tf_op jit(solution)/shard_map/ppermute | solution.py:33
  13.9 9.7 %collective-permute-start.7 = (bf16[224,512]{1,0:T(8,128)(2,1)S(1)}, bf16[224,512]{1,0:T(8,128)(2,1)S(1)}, u32[]{:S(2)}, u32[]{:S(2)}) collective-permute-start(bf16[224,512]{1,0:T(8,128)(2,1)S(1)} %get-tuple-element.58.refs_0_), channel_id=1, source_target_pairs={{0,2},{1,3},{2,0},{3,1},{4,6},{5,7},{6,4},{7,5},{8,10},{9,11},{10,... | collective-permute-start | bytes 688136 | tf_op jit(solution)/shard_map/ppermute | solution.py:33
  18.9 2.9 %collective-permute-start.6 = (bf16[208,512]{1,0:T(8,128)(2,1)S(1)}, bf16[208,512]{1,0:T(8,128)(2,1)S(1)}, u32[]{:S(2)}, u32[]{:S(2)}) collective-permute-start(bf16[208,512]{1,0:T(8,128)(2,1)S(1)} %shard_map.83.after_ref.refs_2_), channel_id=1, source_target_pairs={{0,1},{1,0},{2,3},{3,2},{4,5},{5,4},{6,7},{7,6},{8,9},{9,8},{10,11... | collective-permute-start | bytes 638984 | tf_op jit(solution)/shard_map/ppermute | solution.py:33
  19.2 9.3 %collective-permute-start.9 = (bf16[240,512]{1,0:T(8,128)(2,1)S(1)}, bf16[240,512]{1,0:T(8,128)(2,1)S(1)}, u32[]{:S(2)}, u32[]{:S(2)}) collective-permute-start(bf16[240,512]{1,0:T(8,128)(2,1)S(1)} %get-tuple-element.47.refs_0_), channel_id=1, source_target_pairs={{0,2},{1,3},{2,0},{3,1},{4,6},{5,7},{6,4},{7,5},{8,10},{9,11},{10,... | collective-permute-start | bytes 737288 | tf_op jit(solution)/shard_map/ppermute | solution.py:33
  23.6 1.7 %collective-permute-start.8 = (bf16[224,512]{1,0:T(8,128)(2,1)S(1)}, bf16[224,512]{1,0:T(8,128)(2,1)S(1)}, u32[]{:S(2)}, u32[]{:S(2)}) collective-permute-start(bf16[224,512]{1,0:T(8,128)(2,1)S(1)} %shard_map.86.after_ref.refs_2_), channel_id=1, source_target_pairs={{0,1},{1,0},{2,3},{3,2},{4,5},{5,4},{6,7},{7,6},{8,9},{9,8},{10,11... | collective-permute-start | bytes 688136 | tf_op jit(solution)/shard_map/ppermute | solution.py:33
  28.5 1.5 %collective-permute-start.10 = (bf16[240,512]{1,0:T(8,128)(2,1)S(1)}, bf16[240,512]{1,0:T(8,128)(2,1)S(1)}, u32[]{:S(2)}, u32[]{:S(2)}) collective-permute-start(bf16[240,512]{1,0:T(8,128)(2,1)S(1)} %shard_map.90.refs_0_), channel_id=1, source_target_pairs={{0,1},{1,0},{2,3},{3,2},{4,5},{5,4},{6,7},{7,6},{8,9},{9,8},{10,11... | collective-permute-start | bytes 737288 | tf_op jit(solution)/shard_map/ppermute | solution.py:33
  30.9 6.6 %collective-permute-start.11 = (bf16[2,1,128,128]{3,2,1,0:T(8,128)(2,1)S(1)}, bf16[2,1,128,128]{3,2,1,0:T(8,128)(2,1)S(1)}, u32[]{:S(2)}, u32[]{:S(2)}) collective-permute-start(bf16[2,1,128,128]{3,2,1,0:T(8,128)(2,1)S(1)} %get-tuple-element.66), channel_id=1, source_target_pairs={{0,12},{4,8},{8,4},{12,0},{16,28},{20,24},{24,20},{28,16},{1,13},{... | collective-permute-start | bytes 196616 | tf_op jit(solution)/shard_map/ppermute | solution.py:33
  33.7 4.3 %collective-permute-start.12 = (bf16[2,1,128,128]{3,2,1,0:T(8,128)(2,1)S(1)}, bf16[2,1,128,128]{3,2,1,0:T(8,128)(2,1)S(1)}, u32[]{:S(2)}, u32[]{:S(2)}) collective-permute-start(bf16[2,1,128,128]{3,2,1,0:T(8,128)(2,1)S(1)} %get-tuple-element.67), channel_id=1, source_target_pairs={{0,8},{4,12},{8,0},{12,4},{16,24},{20,28},{24,16},{28,20},{1,9},{5... | collective-permute-start | bytes 196616 | tf_op jit(solution)/shard_map/ppermute | solution.py:33
  34.1 4.3 %collective-permute-start.13 = (bf16[2,1,128,128]{3,2,1,0:T(8,128)(2,1)S(1)}, bf16[2,1,128,128]{3,2,1,0:T(8,128)(2,1)S(1)}, u32[]{:S(2)}, u32[]{:S(2)}) collective-permute-start(bf16[2,1,128,128]{3,2,1,0:T(8,128)(2,1)S(1)} %get-tuple-element.68.after_ref), channel_id=1, source_target_pairs={{0,4},{4,0},{8,12},{12,8},{16,20},{20,16},{24,28},{28,24},{1,5},{5... | collective-permute-start | bytes 196616 | tf_op jit(solution)/shard_map/ppermute | solution.py:33
  38.4 6.1 %collective-permute-start.17 = (bf16[1,128,128]{2,1,0:T(8,128)(2,1)S(1)}, bf16[1,128,128]{2,1,0:T(8,128)(2,1)S(1)}, u32[]{:S(2)}, u32[]{:S(2)}) collective-permute-start(bf16[1,128,128]{2,1,0:T(8,128)(2,1)S(1)} %get-tuple-element.79), channel_id=1, source_target_pairs={{0,16},{4,20},{8,24},{12,28},{16,0},{20,4},{24,8},{28,12},{1,17},{... | collective-permute-start | bytes 98312 | tf_op jit(solution)/shard_map/ppermute | solution.py:33
  41.1 7.0 %collective-permute-start.14 = (bf16[5,128,128]{2,1,0:T(8,128)(2,1)S(1)}, bf16[5,128,128]{2,1,0:T(8,128)(2,1)S(1)}, u32[]{:S(2)}, u32[]{:S(2)}) collective-permute-start(bf16[5,128,128]{2,1,0:T(8,128)(2,1)S(1)} %get-tuple-element.75.refs_0_), channel_id=1, source_target_pairs={{0,4},{4,0},{8,12},{12,8},{16,20},{20,16},{24,28},{28,24},{1,5},{5... | collective-permute-start | bytes 491528 | tf_op jit(solution)/shard_map/ppermute | solution.py:33
  41.9 5.0 %collective-permute-start.16 = (bf16[1,128,128]{2,1,0:T(8,128)(2,1)S(1)}, bf16[1,128,128]{2,1,0:T(8,128)(2,1)S(1)}, u32[]{:S(2)}, u32[]{:S(2)}) collective-permute-start(bf16[1,128,128]{2,1,0:T(8,128)(2,1)S(1)} %get-tuple-element.76), channel_id=1, source_target_pairs={{0,12},{4,8},{8,4},{12,0},{16,28},{20,24},{24,20},{28,16},{1,13},{... | collective-permute-start | bytes 98312 | tf_op jit(solution)/shard_map/ppermute | solution.py:33
  44.1 4.0 %collective-permute-start.15 = (bf16[1,128,128]{2,1,0:T(8,128)(2,1)S(1)}, bf16[1,128,128]{2,1,0:T(8,128)(2,1)S(1)}, u32[]{:S(2)}, u32[]{:S(2)}) collective-permute-start(bf16[1,128,128]{2,1,0:T(8,128)(2,1)S(1)} %get-tuple-element.76), channel_id=1, source_target_pairs={{0,8},{4,12},{8,0},{12,4},{16,24},{20,28},{24,16},{28,20},{1,9},{5... | collective-permute-start | bytes 98312 | tf_op jit(solution)/shard_map/ppermute | solution.py:33
  44.6 6.1 %collective-permute-start.20 = (bf16[1,128,128]{2,1,0:T(8,128)(2,1)S(1)}, bf16[1,128,128]{2,1,0:T(8,128)(2,1)S(1)}, u32[]{:S(2)}, u32[]{:S(2)}) collective-permute-start(bf16[1,128,128]{2,1,0:T(8,128)(2,1)S(1)} %shard_map.97.refs_0_), channel_id=1, source_target_pairs={{0,12},{4,8},{8,4},{12,0},{16,28},{20,24},{24,20},{28,16},{1,13},{... | collective-permute-start | bytes 98312 | tf_op jit(solution)/shard_map/ppermute | solution.py:33
  46.4 4.2 %collective-permute-start.19 = (bf16[1,128,128]{2,1,0:T(8,128)(2,1)S(1)}, bf16[1,128,128]{2,1,0:T(8,128)(2,1)S(1)}, u32[]{:S(2)}, u32[]{:S(2)}) collective-permute-start(bf16[1,128,128]{2,1,0:T(8,128)(2,1)S(1)} %shard_map.97.refs_0_), channel_id=1, source_target_pairs={{0,8},{4,12},{8,0},{12,4},{16,24},{20,28},{24,16},{28,20},{1,9},{5... | collective-permute-start | bytes 98312 | tf_op jit(solution)/shard_map/ppermute | solution.py:33
  46.9 3.9 %collective-permute-start.18 = (bf16[1,128,128]{2,1,0:T(8,128)(2,1)S(1)}, bf16[1,128,128]{2,1,0:T(8,128)(2,1)S(1)}, u32[]{:S(2)}, u32[]{:S(2)}) collective-permute-start(bf16[1,128,128]{2,1,0:T(8,128)(2,1)S(1)} %shard_map.97.refs_0_), channel_id=1, source_target_pairs={{0,4},{4,0},{8,12},{12,8},{16,20},{20,16},{24,28},{28,24},{1,5},{5... | collective-permute-start | bytes 98312 | tf_op jit(solution)/shard_map/ppermute | solution.py:33
